TPU v7x, 32 devices: a whole 2x2x4 slice. The times are simulated.
32 devices in a mesh: group: 2 (over x), cand: 16 (over z, y, core).
Axes of the slice: x: 2, y: 2, z: 4, core: 2. Of those that a mesh axis runs over, the one named last changes fastest.
Arguments:
- embeddings: bfloat16 [64, 1024, 768], P(('group', 'cand')), parts along dimension 0
- lengths: int32 [64], P(('group', 'cand')), parts along dimension 0, may hold values from 256 to 1024, as said below
Outputs:
- consensus: float32 [64, 1024], P(('group', 'cand')), parts along dimension 0
There are 2 independent parts, one for each index of `group`. A program takes and returns all parts, laid end to end along the dimension named above; each array names one. Nothing has to cross between parts.
Inputs may be any that keep to these rules, and one draw needn't show every extreme that they name: `lengths`: at least one answer of every prompt has exactly 1024 tokens; every answer has 256 tokens or more.
All inputs are finite; a program needn't handle non-finite values.
Results may differ from a plain program's by a relative error of at most 0.0005.
Values may be sent and summed in bfloat16 or wider, within the bound.
No kernel may reach another device: no remote copies, remote signals or barrier semaphores. Data moves between devices by JAX's collectives and lax.ppermute only.
A program may use at most 64 MiB of HBM per device.

v0:
```python
import jax
import jax.numpy as jnp
from jax import lax
from jax.sharding import PartitionSpec as P

INV_TEMP = 256.0


def from_behind(shard, axis, by):
    count = lax.axis_size(axis)
    return lax.ppermute(shard, axis, [(i, (i + by) % count) for i in range(count)])


def unit_rows(embeddings):
    values = embeddings.astype(jnp.float32)
    scale = lax.rsqrt(jnp.sum(values * values, axis=-1, keepdims=True) + 1e-06)
    return (values * scale).astype(jnp.bfloat16)


def soft_terms(left, left_valid, right, right_valid):
    scores = jnp.einsum("te,bse->bts", left, right, preferred_element_type=jnp.float32) * INV_TEMP
    row_scores = jnp.where(right_valid[:, None, :] > 0.5, scores, -1e30)
    row_peak = jnp.max(row_scores, axis=2, keepdims=True)
    row_terms = (
        row_peak[..., 0] + jnp.log(jnp.sum(jnp.exp(row_scores - row_peak), axis=2))
    ) / INV_TEMP
    col_scores = jnp.where(left_valid[None, :, None] > 0.5, scores, -1e30)
    col_peak = jnp.max(col_scores, axis=1, keepdims=True)
    col_terms = (
        col_peak[:, 0, :] + jnp.log(jnp.sum(jnp.exp(col_scores - col_peak), axis=1))
    ) / INV_TEMP
    return (row_terms, col_terms)


def cross_block(unit, valid, partner):
    their_unit, their_mask = partner
    their_valid = their_mask.astype(jnp.float32)
    row_list = []
    col_total = jnp.zeros(their_valid.shape, jnp.float32)
    for slot in range(unit.shape[0]):
        row_terms, col_terms = soft_terms(unit[slot], valid[slot], their_unit, their_valid)
        row_list.append(jnp.sum(row_terms, axis=0))
        col_total = col_total + col_terms
    return (jnp.stack(row_list), col_total)


def shards(embeddings, lengths):
    answers = embeddings.shape[0]
    length = embeddings.shape[1]
    unit = unit_rows(embeddings)
    valid = (lax.broadcasted_iota(jnp.int32, (answers, length), 1) < lengths[:, None]).astype(
        jnp.float32
    )
    own_block = (unit, valid.astype(jnp.bfloat16))
    totals = jnp.zeros((answers, length), jnp.float32)
    first = from_behind((own_block[0], own_block[1]), "cand", 1)
    second = from_behind((own_block[0], own_block[1]), "cand", 2)
    row_terms, col_terms = soft_terms(unit[0], valid[0], unit[1:], valid[1:])
    totals = totals.at[0].add(jnp.sum(row_terms, axis=0))
    totals = totals.at[1:].add(col_terms)
    rows_first, cols_first = cross_block(unit, valid, first)
    returned_first = from_behind(cols_first, "cand", -1)
    rows_second, cols_second = cross_block(unit, valid, second)
    returned_second = from_behind(cols_second, "cand", -2)
    totals = totals + rows_first + rows_second + returned_first + returned_second
    return totals * valid / (answers - 1 + 4 * answers)


def solution(mesh):
    return jax.shard_map(
        shards,
        mesh=mesh,
        in_specs=(P(("group", "cand"), None, None), P(("group", "cand"))),
        out_specs=P(("group", "cand"), None),
        check_vma=False,
    )
```

profile of v0, /device:TPU:0, one launch (start us, length us, event | category | flops | bytes accessed | tf_op | source)
XLA Modules:
  0.0 145.0 jit_solution(10423566783832293790)
XLA Ops:
  0.0 0.0 copy-start
  0.0 2.6 %fusion.16 = f32[2,1024]{1,0:T(2,128)S(1)} fusion(bf16[2,1024,768]{2,1,0:T(8,128)(2,1)} %param.6), kind=kLoop, calls=%fused_computation.34 | loop fusion | flops 4716544 | bytes 3153920 | tf_op jit(solution)/shard_map/reduce_sum | solution.py:16
  2.6 2.5 %fusion.17 = bf16[2,1024,768]{2,1,0:T(8,128)(2,1)S(1)} fusion(bf16[2,1024,768]{2,1,0:T(8,128)(2,1)} %param.6, f32[2,1024]{1,0:T(2,128)S(1)} %add_rsqrt_fusion), kind=kLoop, calls=%fused_computation.35 | loop fusion | flops 4718592 | bytes 6299648 | tf_op jit(solution)/shard_map/convert_element_type | solution.py:17
  5.1 0.5 collective-permute-start.1
  5.6 0.0 copy-done
  5.6 0.1 fusion.41
  5.7 2.5 %collective-permute-start.2 = (bf16[2,1024]{1,0:T(2,128)(2,1)S(1)}, bf16[2,1024]{1,0:T(2,128)(2,1)S(1)}, u32[]{:S(2)}, u32[]{:S(2)}) collective-permute-start(bf16[2,1024]{1,0:T(2,128)(2,1)S(1)} %get-tuple-element.46), channel_id=1, source_target_pairs={{0,2},{1,3},{2,4},{3,5},{4,6},{5,7},{6,8},{7,9},{8,10},{9,11},{10,... | collective-permute-start | bytes 12296 | tf_op jit(solution)/shard_map/ppermute | solution.py:11
  8.2 1.3 collective-permute-start
  9.5 1.5 %collective-permute-start.3 = (bf16[2,1024,768]{2,1,0:T(8,128)(2,1)S(1)}, bf16[2,1024,768]{2,1,0:T(8,128)(2,1)S(1)}, u32[]{:S(2)}, u32[]{:S(2)}) collective-permute-start(bf16[2,1024,768]{2,1,0:T(8,128)(2,1)S(1)} %fusion.17), channel_id=1, source_target_pairs={{0,2},{1,3},{2,4},{3,5},{4,6},{5,7},{6,8},{7,9},{8,10},{9,11},{10,... | collective-permute-start | bytes 9437192 | tf_op jit(solution)/shard_map/ppermute | solution.py:11
  11.1 1.8 %fusion.18 = (f32[1024]{0:T(1024)S(1)}, f32[1024,1024]{1,0:T(8,128)S(1)}) fusion(pred[1024]{0:T(1024)(128)(4,1)S(1)} %get-tuple-element.40, bf16[2,1024,768]{2,1,0:T(8,128)(2,1)S(1)} %fusion.17), kind=kOutput, calls=%fused_computation.40 | convolution fusion | flops 1613757440 | bytes 7345152 | tf_op jit(solution)/shard_map/te,bse->bts/dot_general | solution.py:21
  12.9 1.9 %exponential_reduce_fusion.1 = (f32[1024]{0:T(1024)S(1)}, f32[1024]{0:T(1024)S(1)}) fusion(f32[1024,1024]{1,0:T(8,128)S(1)} %get-tuple-element.54, f32[1024]{0:T(1024)S(1)} %get-tuple-element.53, pred[1024]{0:T(1024)(128)(4,1)S(1)} %get-tuple-element.40, pred[1024]{0:T(1024)(128)(4,1)S(1)} %get-tuple-element.39), kind=kLoop, calls=%fused_computation.39 | loop fusion | flops 6289408 | bytes 4208640 | tf_op jit(solution)/shard_map/reduce_sum | solution.py:25
  14.9 1.0 exponential_reduce_fusion
  16.0 0.0 collective-permute-done.2
  16.0 59.5 %collective-permute-done = bf16[2,1024]{1,0:T(2,128)(2,1)S(1)} collective-permute-done((bf16[2,1024]{1,0:T(2,128)(2,1)S(1)}, bf16[2,1024]{1,0:T(2,128)(2,1)S(1)}, u32[]{:S(2)}, u32[]{:S(2)}) %collective-permute-start) | collective-permute-done | bytes 4128 | tf_op jit(solution)/shard_map/ppermute | solution.py:11
  75.5 0.0 collective-permute-done.1
  75.5 3.7 %bitcast_reduce_fusion.7 = (f32[2,1024]{1,0:T(2,128)S(1)}, f32[2,1024,1024]{2,1,0:T(8,128)S(1)}) fusion(pred[2,1024]{1,0:T(4,128)(4,1)S(1)} %convert_compare_fusion.1, bf16[2,1024,768]{2,1,0:T(8,128)(2,1)S(1)} %collective-permute-done.1, bf16[2,1024,768]{2,1,0:T(8,128)(2,1)S(1)} %fusion.17), kind=kOutput, calls=%fused_computation.29 | convolution fusion | flops 3227514880 | bytes 13119488 | tf_op jit(solution)/shard_map/te,bse->bts/dot_general | solution.py:21
  79.2 0.0 copy-start.2
  79.2 6.1 %fusion.15 = (f32[2,1024]{1,0:T(2,128)S(1)}, f32[2,1024]{1,0:T(2,128)S(1)}, f32[2,1024]{1,0:T(2,128)S(1)}, f32[2,1024,1024]{2,1,0:T(8,128)S(1)}) fusion(f32[2,1024,1024]{2,1,0:T(8,128)S(1)} %get-tuple-element.50, f32[2,1024]{1,0:T(2,128)S(1)} %get-tuple-element.49, pred[2,1024]{1,0:T(4,128)(4,1)S(1)} %convert_compare_fusion.1, ...), kind=kOutput, calls=%fused_computation.31 | convolution fusion | flops 3240093696 | bytes 21533696 | tf_op jit(solution)/shard_map/te,bse->bts/dot_general | solution.py:21
  85.3 0.0 copy-done.2
  85.3 3.2 %fusion.13 = (f32[2,1024]{1,0:T(2,128)S(1)}, f32[2,1024]{1,0:T(2,128)S(1)}) fusion(f32[2,1024,1024]{2,1,0:T(8,128)S(1)} %get-tuple-element.51, f32[2,1024]{1,0:T(2,128)S(1)} %get-tuple-element.41, pred[2,1024]{1,0:T(4,128)(4,1)S(1)} %convert_compare_fusion.1, pred[1024]{0:T(1024)(128)(4,1)S(1)} %get-tuple-element.40), kind=kLoop, calls=%fused_computation.27 | loop fusion | flops 12578816 | bytes 8416256 | tf_op jit(solution)/shard_map/reduce_sum | solution.py:25
  88.5 0.0 collective-permute-done.3
  88.5 0.0 copy-start.1
  88.5 5.7 %bitcast_reduce_fusion.5 = (f32[2,1024]{1,0:T(2,128)S(1)}, f32[2,1024,1024]{2,1,0:T(8,128)}) fusion(pred[2,1024]{1,0:T(4,128)(4,1)S(1)} %convert_compare_fusion, bf16[2,1024,768]{2,1,0:T(8,128)(2,1)S(1)} %collective-permute-done.3, bf16[2,1024,768]{2,1,0:T(8,128)(2,1)S(1)} %fusion.17), kind=kOutput, calls=%fused_computation.21 | convolution fusion | flops 3227514880 | bytes 13119488 | tf_op jit(solution)/shard_map/te,bse->bts/dot_general | solution.py:21
  94.2 0.0 copy-done.1
  94.2 10.8 %fusion.11 = (f32[2,1024]{1,0:T(2,128)S(1)}, f32[2,1024]{1,0:T(2,128)S(1)}, f32[2,1024]{1,0:T(2,128)S(1)}, f32[2,1024]{1,0:T(2,128)S(1)}, f32[2,1024,1024]{2,1,0:T(8,128)S(1)}) fusion(f32[2,1024,1024]{2,1,0:T(8,128)} %get-tuple-element.48, f32[2,1024]{1,0:T(2,128)S(1)} %get-tuple-element.47, pred[2,1024]{1,0:T(4,128)(4,1)S(1)} %convert_compare_fusion, ...), kind=kOutput, calls=%fused_computation.23 | convolution fusion | flops 3248480256 | bytes 29938688 | tf_op jit(solution)/shard_map/te,bse->bts/dot_general | solution.py:21
  104.9 8.4 %fusion.9 = (f32[2,1024]{1,0:T(2,128)S(1)}, f32[2,1024]{1,0:T(2,128)S(1)}, f32[2,1024]{1,0:T(2,128)S(1)}, f32[2,1024]{1,0:T(2,128)S(1)}) fusion(f32[2,1024,1024]{2,1,0:T(8,128)S(1)} %get-tuple-element.52, f32[2,1024]{1,0:T(2,128)S(1)} %get-tuple-element.42, pred[2,1024]{1,0:T(4,128)(4,1)S(1)} %convert_compare_fusion, ...), kind=kLoop, calls=%fused_computation.19 | loop fusion | flops 29351936 | bytes 25227264 | tf_op jit(solution)/shard_map/reduce_sum | solution.py:25
  113.4 2.0 %fusion.1 = f32[2,1024]{1,0:T(2,128)S(1)} fusion(f32[2,1024,1024]{2,1,0:T(8,128)S(1)} %get-tuple-element.52, f32[2,1024]{1,0:T(2,128)S(1)} %get-tuple-element.36, pred[1024]{0:T(1024)(128)(4,1)S(1)} %get-tuple-element.40), kind=kLoop, calls=%fused_computation.3 | loop fusion | flops 8386560 | bytes 8406016 | tf_op jit(solution)/shard_map/reduce_sum | solution.py:30
  115.4 4.2 %collective-permute-start.5 = (f32[2,1024]{1,0:T(2,128)S(1)}, f32[2,1024]{1,0:T(2,128)S(1)}, u32[]{:S(2)}, u32[]{:S(2)}) collective-permute-start(f32[2,1024]{1,0:T(2,128)S(1)} %add_multiply_fusion), channel_id=1, source_target_pairs={{0,14},{1,15},{2,0},{3,1},{4,2},{5,3},{6,4},{7,5},{8,6},{9,7},{10,... | collective-permute-start | bytes 24584 | tf_op jit(solution)/shard_map/ppermute | solution.py:11
  119.6 23.4 %collective-permute-start.4 = (f32[2,1024]{1,0:T(2,128)S(1)}, f32[2,1024]{1,0:T(2,128)S(1)}, u32[]{:S(2)}, u32[]{:S(2)}) collective-permute-start(f32[2,1024]{1,0:T(2,128)S(1)} %add_multiply_fusion.1), channel_id=1, source_target_pairs={{0,15},{1,0},{2,1},{3,2},{4,3},{5,4},{6,5},{7,6},{8,7},{9,8},{10,9... | collective-permute-start | bytes 24584 | tf_op jit(solution)/shard_map/ppermute | solution.py:11
  143.0 0.0 collective-permute-done.5
  143.0 1.3 collective-permute-done.4
  144.3 0.7 fusion.42
  (10 shorter events, 0.2 us)
Async XLA Ops:
  0.0 5.6 %copy-start = (s32[2]{0:T(128)S(1)}, s32[2]{0:T(128)}, u32[]{:S(2)}) copy-start(s32[2]{0:T(128)} %param.7) | copy-start | bytes 28
  5.1 70.4 %collective-permute-start.1 = (bf16[2,1024,768]{2,1,0:T(8,128)(2,1)S(1)}, bf16[2,1024,768]{2,1,0:T(8,128)(2,1)S(1)}, u32[]{:S(2)}, u32[]{:S(2)}) collective-permute-start(bf16[2,1024,768]{2,1,0:T(8,128)(2,1)S(1)} %fusion.17), channel_id=1, source_target_pairs={{0,1},{1,2},{2,3},{3,4},{4,5},{5,6},{6,7},{7,8},{8,9},{9,10},{10,1... | collective-permute-start | bytes 9437192 | tf_op jit(solution)/shard_map/ppermute | solution.py:11
  5.7 10.3 %collective-permute-start.2 = (bf16[2,1024]{1,0:T(2,128)(2,1)S(1)}, bf16[2,1024]{1,0:T(2,128)(2,1)S(1)}, u32[]{:S(2)}, u32[]{:S(2)}) collective-permute-start(bf16[2,1024]{1,0:T(2,128)(2,1)S(1)} %get-tuple-element.46), channel_id=1, source_target_pairs={{0,2},{1,3},{2,4},{3,5},{4,6},{5,7},{6,8},{7,9},{8,10},{9,11},{10,... | collective-permute-start | bytes 12296 | tf_op jit(solution)/shard_map/ppermute | solution.py:11
  8.2 67.3 %collective-permute-start = (bf16[2,1024]{1,0:T(2,128)(2,1)S(1)}, bf16[2,1024]{1,0:T(2,128)(2,1)S(1)}, u32[]{:S(2)}, u32[]{:S(2)}) collective-permute-start(bf16[2,1024]{1,0:T(2,128)(2,1)S(1)} %get-tuple-element.46), channel_id=1, source_target_pairs={{0,1},{1,2},{2,3},{3,4},{4,5},{5,6},{6,7},{7,8},{8,9},{9,10},{10,1... | collective-permute-start | bytes 12296 | tf_op jit(solution)/shard_map/ppermute | solution.py:11
  9.5 78.9 %collective-permute-start.3 = (bf16[2,1024,768]{2,1,0:T(8,128)(2,1)S(1)}, bf16[2,1024,768]{2,1,0:T(8,128)(2,1)S(1)}, u32[]{:S(2)}, u32[]{:S(2)}) collective-permute-start(bf16[2,1024,768]{2,1,0:T(8,128)(2,1)S(1)} %fusion.17), channel_id=1, source_target_pairs={{0,2},{1,3},{2,4},{3,5},{4,6},{5,7},{6,8},{7,9},{8,10},{9,11},{10,... | collective-permute-start | bytes 9437192 | tf_op jit(solution)/shard_map/ppermute | solution.py:11
  79.2 6.1 %copy-start.2 = (f32[2,1024,1024]{2,1,0:T(8,128)}, f32[2,1024,1024]{2,1,0:T(8,128)S(1)}, u32[]{:S(2)}) copy-start(f32[2,1024,1024]{2,1,0:T(8,128)S(1)} %get-tuple-element.50) | copy-start | bytes 25165828
  88.5 5.7 %copy-start.1 = (bf16[2,1024,768]{2,1,0:T(8,128)(2,1)}, bf16[2,1024,768]{2,1,0:T(8,128)(2,1)S(1)}, u32[]{:S(2)}) copy-start(bf16[2,1024,768]{2,1,0:T(8,128)(2,1)S(1)} %collective-permute-done.3) | copy-start | bytes 9437188
  115.4 27.6 %collective-permute-start.5 = (f32[2,1024]{1,0:T(2,128)S(1)}, f32[2,1024]{1,0:T(2,128)S(1)}, u32[]{:S(2)}, u32[]{:S(2)}) collective-permute-start(f32[2,1024]{1,0:T(2,128)S(1)} %add_multiply_fusion), channel_id=1, source_target_pairs={{0,14},{1,15},{2,0},{3,1},{4,2},{5,3},{6,4},{7,5},{8,6},{9,7},{10,... | collective-permute-start | bytes 24584 | tf_op jit(solution)/shard_map/ppermute | solution.py:11
  119.6 24.7 %collective-permute-start.4 = (f32[2,1024]{1,0:T(2,128)S(1)}, f32[2,1024]{1,0:T(2,128)S(1)}, u32[]{:S(2)}, u32[]{:S(2)}) collective-permute-start(f32[2,1024]{1,0:T(2,128)S(1)} %add_multiply_fusion.1), channel_id=1, source_target_pairs={{0,15},{1,0},{2,1},{3,2},{4,3},{5,4},{6,5},{7,6},{8,7},{9,8},{10,9... | collective-permute-start | bytes 24584 | tf_op jit(solution)/shard_map/ppermute | solution.py:11
where the time goes:
time: 145 us
  waiting for transfers between devices  60.8 us (42%)
  starting transfers between devices  33.4 us (23%)
  matrix products  28 us (19%)
  other arithmetic  22.6 us (16%)
    ppermute x6, waiting for transfers between devices, from_behind(): lax.ppermute(shard, axis, [(i, (i + by) % count) for i in range(count)])  60.8 us
    ppermute x6, starting transfers between devices, from_behind(): lax.ppermute(shard, axis, [(i, (i + by) % count) for i in range(count)])  33.4 us
    dot_general x5, matrix products, soft_terms(): jnp.einsum('te,bse->bts', left, right, preferred_element_type=jnp.float32)  28 us
    reduce_sum x3, other arithmetic, soft_terms(): jnp.sum(jnp.exp(row_scores - row_peak), axis=2)  13.5 us
    reduce_sum x2, other arithmetic, soft_terms(): jnp.sum(jnp.exp(col_scores - col_peak), axis=1)  3.01 us
  transfers between devices with their start and end apart: 6, of which 2 were waited for; matrix products, arithmetic and copies ran while one was open for 12% of the time, Pallas kernels for 0%

commit v1 on v0

v1 whole, which is shorter than its diff:
```python
import functools

import jax
import jax.numpy as jnp
from jax import lax
from jax.experimental import pallas as pl
from jax.experimental.pallas import tpu as pltpu
from jax.sharding import PartitionSpec as P

SCALE = 256.0 * 1.4426950408889634
LOWEST = -1e30
LANES = 128
ROW_TILE = 1024
COL_TILE = 512
SUM_TILE = 256
SUM_STEP = 64


def unit_rows(embeddings):
    values = embeddings.astype(jnp.float32)
    scale = lax.rsqrt(jnp.sum(values * values, axis=-1, keepdims=True) + 1e-06)
    return (values * scale).astype(jnp.bfloat16)


def unit_kernel(values_ref, unit_ref):
    unit_ref[...] = unit_rows(values_ref[...])


def make_unit(embeddings):
    answers, length, width = embeddings.shape
    rows = answers * length
    tile = min(512, rows)
    flat = pl.pallas_call(
        unit_kernel,
        grid=(rows // tile,),
        in_specs=[pl.BlockSpec((tile, width), lambda i: (i, 0))],
        out_specs=pl.BlockSpec((tile, width), lambda i: (i, 0)),
        out_shape=jax.ShapeDtypeStruct((rows, width), jnp.bfloat16),
    )(embeddings.reshape(rows, width))
    return flat.reshape(embeddings.shape)


def pair_kernel(meta, left_ref, right_ref, row_ref, col_ref, unit, scores, peak, total, *, raw):
    pair = pl.program_id(0)
    left_rows = left_ref.shape[1]
    right_rows = right_ref.shape[1]
    left_len = meta[2, pair]
    right_len = meta[3, pair]
    row_tile = min(ROW_TILE, left_rows)
    col_tile = min(COL_TILE, right_rows)
    sum_rows = min(SUM_TILE, left_rows)
    sum_cols = min(SUM_TILE, right_rows)

    if raw:

        @pl.when(pair == 0)
        def _():
            for start in range(0, left_rows, LANES):
                unit[start : start + LANES, :] = unit_rows(left_ref[0, start : start + LANES, :])

    row_ref[...] = jnp.zeros_like(row_ref)
    col_ref[...] = jnp.zeros_like(col_ref)

    def at(index, size):
        return pl.ds(pl.multiple_of(index * size, size), size)

    def steps(count, size):
        return lax.div(count + size - 1, size)

    @pl.when((left_len > 0) & (right_len > 0))
    def _():
        peak[...] = jnp.full_like(peak, LOWEST)
        total[...] = jnp.zeros_like(total)

        def score_cols(j, carry):
            cols = at(j, col_tile)
            right = right_ref[0, cols, :]
            col_at = lax.broadcasted_iota(jnp.int32, (1, col_tile), 1) + j * col_tile
            col_bias = jnp.where(col_at < right_len, 0.0, LOWEST)

            def score_rows(i, col_peak):
                rows = at(i, row_tile)
                left = unit[rows, :] if raw else left_ref[0, rows, :]
                tile = lax.dot_general(
                    left, right, (((1,), (1,)), ((), ())), preferred_element_type=jnp.float32
                )
                row_at = lax.broadcasted_iota(jnp.int32, (row_tile, 1), 0) + i * row_tile
                row_bias = jnp.where(row_at < left_len, 0.0, LOWEST)
                tile = (tile * SCALE + col_bias) + row_bias
                scores[rows, cols] = tile
                row_peak = peak[rows, :]
                for k in range(0, col_tile, LANES):
                    row_peak = jnp.maximum(row_peak, tile[:, k : k + LANES])
                peak[rows, :] = row_peak
                folded = jnp.max(tile.reshape(row_tile // 8, 8, col_tile), axis=0)
                return jnp.maximum(col_peak, folded)

            col_peak = lax.fori_loop(
                0, steps(left_len, row_tile), score_rows, jnp.full((8, col_tile), LOWEST, jnp.float32)
            )
            col_ref[0, :, cols] = jnp.max(col_peak, axis=0, keepdims=True)
            return carry

        lax.fori_loop(0, steps(right_len, col_tile), score_cols, 0)

        def sum_cols_of(j, carry):
            cols = at(j, sum_cols)
            col_peak = col_ref[0, :, cols]

            def sum_rows_of(i, col_sum):
                for step in range(0, sum_rows, SUM_STEP):
                    rows = pl.ds(pl.multiple_of(i * sum_rows, sum_rows) + step, SUM_STEP)
                    tile = scores[rows, cols]
                    row_peak = peak[rows, :]
                    row_sum = total[rows, :]
                    for k in range(0, sum_cols, LANES):
                        row_sum = row_sum + jnp.exp2(tile[:, k : k + LANES] - row_peak)
                    total[rows, :] = row_sum
                    terms = jnp.exp2(tile - col_peak)
                    col_sum = col_sum + jnp.sum(terms.reshape(SUM_STEP // 8, 8, sum_cols), axis=0)
                return col_sum

            col_sum = lax.fori_loop(
                0, steps(left_len, sum_rows), sum_rows_of, jnp.zeros((8, sum_cols), jnp.float32)
            )
            col_sum = jnp.sum(col_sum, axis=0, keepdims=True)
            col_ref[0, :, cols] = (col_peak + jnp.log2(col_sum)) * (1.0 / SCALE)
            return carry

        lax.fori_loop(0, steps(right_len, sum_cols), sum_cols_of, 0)

        def finish_rows(i, carry):
            rows = at(i, sum_rows)
            lane_peak = jnp.transpose(peak[rows, :])
            lane_sum = jnp.transpose(total[rows, :])
            row_peak = jnp.max(lane_peak, axis=0, keepdims=True)
            row_sum = jnp.sum(lane_sum * jnp.exp2(lane_peak - row_peak), axis=0, keepdims=True)
            row_ref[0, :, rows] = (row_peak + jnp.log2(row_sum)) * (1.0 / SCALE)
            return carry

        lax.fori_loop(0, steps(left_len, sum_rows), finish_rows, 0)


def match_pairs(meta, left, right, raw):
    pairs = meta.shape[1]
    left_rows, width = left.shape[1:]
    right_rows = right.shape[1]
    rows, cols = pl.pallas_call(
        functools.partial(pair_kernel, raw=raw),
        grid_spec=pltpu.PrefetchScalarGridSpec(
            num_scalar_prefetch=1,
            grid=(pairs,),
            in_specs=[
                pl.BlockSpec((1, left_rows, width), lambda p, m: (m[0, p], 0, 0)),
                pl.BlockSpec((1, right_rows, width), lambda p, m: (m[1, p], 0, 0)),
            ],
            out_specs=[
                pl.BlockSpec((1, 1, left_rows), lambda p, m: (p, 0, 0)),
                pl.BlockSpec((1, 1, right_rows), lambda p, m: (p, 0, 0)),
            ],
            scratch_shapes=[
                pltpu.VMEM((left_rows if raw else 16, width), jnp.bfloat16),
                pltpu.VMEM((left_rows, right_rows), jnp.float32),
                pltpu.VMEM((left_rows, LANES), jnp.float32),
                pltpu.VMEM((left_rows, LANES), jnp.float32),
            ],
        ),
        out_shape=[
            jax.ShapeDtypeStruct((pairs, 1, left_rows), jnp.float32),
            jax.ShapeDtypeStruct((pairs, 1, right_rows), jnp.float32),
        ],
        compiler_params=pltpu.CompilerParams(vmem_limit_bytes=32 << 20),
        cost_estimate=pl.CostEstimate(
            flops=2 * pairs * left_rows * right_rows * width,
            bytes_accessed=2 * (pairs + 1) * right_rows * width,
            transcendentals=2 * pairs * left_rows * right_rows,
        ),
    )(meta, left, right)
    return rows[:, 0], cols[:, 0]


def after(value, *earlier):
    return lax.optimization_barrier((value, *earlier))[0]


def shards(embeddings, lengths):
    answers, length, _ = embeddings.shape
    count = lax.axis_size("cand")
    here = lax.axis_index("cand")
    is_even = here % 2 == 0

    first_to = [(i, (i - 2 if i % 2 == 0 else i + 2) % count) for i in range(count)]
    second_to = [(i, (i - 1 if i % 2 == 0 else i + 1) % count) for i in range(count)]
    mate_to = [(i, i ^ 1) for i in range(count)]

    def move(value, pairs):
        return lax.ppermute(value, "cand", pairs)

    def back(value, pairs):
        return lax.ppermute(value, "cand", [(b, a) for a, b in pairs])

    first = move(embeddings[0:1], first_to)
    unit = make_unit(embeddings)
    mate_unit = move(unit, mate_to)

    table = lax.all_gather(lengths, "cand", axis=0)

    def lengths_of(offset):
        return lax.dynamic_index_in_dim(table, (here + offset) % count, 0, keepdims=False)

    near = jnp.concatenate([lengths, jnp.where(is_even, lengths_of(1), lengths_of(-1))])
    own_only = jnp.arange(2 * answers, dtype=jnp.int32) < answers
    first_len = jnp.where(is_even, lengths_of(2)[0], lengths_of(-2)[0])
    second_len = jnp.where(is_even, lengths_of(-1)[1], lengths_of(1)[1])
    first_near = jnp.where(is_even | own_only, near, 0)
    second_near = jnp.where(is_even & own_only, 0, near)

    def meta_of(left, right, left_len, right_len):
        return jnp.stack([left, right, jnp.broadcast_to(left_len, right.shape), right_len]).astype(jnp.int32)

    residents = jnp.concatenate([unit, mate_unit])
    inner_left = jnp.where(is_even, jnp.array([0, 0, 0]), jnp.array([0, 3, 3]))
    inner_right = jnp.where(is_even, jnp.array([1, 2, 3]), jnp.array([1, 0, 1]))
    inner_meta = meta_of(inner_left, inner_right, near[inner_left], near[inner_right])
    rows, cols = match_pairs(inner_meta, residents, residents, False)
    zero = jnp.zeros_like(rows[0])
    totals = jnp.where(
        is_even,
        jnp.stack([rows[0] + rows[1] + rows[2], cols[0], cols[1], cols[2]]),
        jnp.stack([rows[0] + cols[1], cols[0] + cols[2], zero, rows[1] + rows[2]]),
    )

    second = move(after(embeddings[1:2], rows), second_to)
    every = jnp.arange(2 * answers)
    nothing = jnp.zeros_like(every)
    rows, cols = match_pairs(meta_of(nothing, every, first_len, first_near), first, residents, True)
    totals = totals + cols
    first_back = back(jnp.sum(rows, axis=0), first_to)
    rows, cols = match_pairs(meta_of(nothing, every, second_len, second_near), second, residents, True)
    totals = totals + cols
    second_back = back(jnp.sum(rows, axis=0), second_to)
    mate_back = move(totals[answers:], mate_to)

    consensus = totals[:answers] + mate_back + jnp.stack([first_back, second_back])
    inside = lax.broadcasted_iota(jnp.int32, (answers, length), 1) < lengths[:, None]
    return jnp.where(inside, consensus / (answers - 1 + 4 * answers), 0.0)


def solution(mesh):
    return jax.shard_map(
        shards,
        mesh=mesh,
        in_specs=(P(("group", "cand"), None, None), P(("group", "cand"))),
        out_specs=P(("group", "cand"), None),
        check_vma=False,
    )
```

time: 145 us -> 141 us (0.972); the launches traced: 145 us -> 144 us
  blocking collectives: 0 us -> 72.5 us
  waiting for transfers between devices: 60.8 us -> 5.73 us
  Pallas kernels: 0 us -> 43.7 us
  matrix products: 28 us -> 0 us
  starting transfers between devices: 33.4 us -> 9.82 us
  other arithmetic: 22.6 us -> 4.47 us
  local copies, waits for them, and re-layouts: 0.01 us -> 5.59 us
  between operations: 0.17 us -> 2.14 us
    unnamed x0 -> x1, blocking collectives: none -> 72.5 us
    ppermute x6, waiting for transfers between devices: 60.8 us -> 5.73 us  [the longest x2 5.72 us: back(): return lax.ppermute(value, 'cand', [(b, a) for a, b in pairs])]
    pallas_call x0 -> x4, Pallas kernels: none -> 43.7 us  [the longest x3 39 us: match_pairs(): pl.pallas_call(functools.partial(pair_kernel, raw=raw), grid_spec=pltpu.P...]
    dot_general x5 -> x0, matrix products: 28 us -> none  [soft_terms(): jnp.einsum('te,bse->bts', left, right, preferred_element_type=jnp.float32)]
    ppermute x6, starting transfers between devices: 33.4 us -> 9.82 us  [the longest x4 6.26 us: move(): return lax.ppermute(value, 'cand', pairs)]
    reduce_sum x9 -> x2, other arithmetic: 19.2 us -> 0.04 us  [the longest x1 0.02 us: shards(): first_back = back(jnp.sum(rows, axis=0), first_to)]
    concatenate x0 -> x2, other arithmetic: none -> 3.46 us  [the longest x1 3.39 us: shards(): residents = jnp.concatenate([unit, mate_unit])]
    slice x0 -> x5, local copies, waits for them, and re-layouts: none -> 3.15 us  [the longest x1 1.92 us: shards(): first = move(embeddings[0:1], first_to)]
  transfers between devices with their start and end apart: 6 -> 6, of which waited for: 2 -> 2; matrix products, arithmetic and copies ran while one was open for 12% -> 6% of each run, Pallas kernels for 0% -> 21%
where the time goes in v1:
time: 141 us; the launch traced here: 144 us
  blocking collectives  72.5 us (51%)
  Pallas kernels  43.7 us (31%)
  starting transfers between devices  9.82 us (7%)
  waiting for transfers between devices  5.73 us (4%)
  local copies, waits for them, and re-layouts  5.59 us (4%)
  other arithmetic  4.47 us (3%)
  between operations  2.14 us (2%)
    unnamed x1, blocking collectives  72.5 us
    pallas_call x3, Pallas kernels, match_pairs(): pl.pallas_call(functools.partial(pair_kernel, raw=raw), grid_spec=pltpu.P...  39 us
    ppermute x4, starting transfers between devices, move(): return lax.ppermute(value, 'cand', pairs)  6.26 us
    ppermute x2, waiting for transfers between devices, back(): return lax.ppermute(value, 'cand', [(b, a) for a, b in pairs])  5.72 us
    pallas_call x1, Pallas kernels, make_unit(): pl.pallas_call(unit_kernel, grid=(rows // tile,), in_specs=[pl.BlockSpec(...  4.74 us
    ppermute x2, starting transfers between devices, back(): return lax.ppermute(value, 'cand', [(b, a) for a, b in pairs])  3.56 us
    concatenate x1, other arithmetic, shards(): residents = jnp.concatenate([unit, mate_unit])  3.39 us
  transfers between devices with their start and end apart: 6, of which 2 were waited for; matrix products, arithmetic and copies ran while one was open for 6% of the time, Pallas kernels for 21%

profile of v1, /device:TPU:0, one launch (start us, length us, event | category | flops | bytes accessed | tf_op | source)
XLA Modules:
  0.0 143.9 jit_solution(17389605862386656515)
XLA Ops:
  0.0 0.0 copy-start
  0.0 4.7 %shard_map.64 = bf16[2048,768]{1,0:T(8,128)(2,1)} custom-call(bf16[2048,768]{1,0:T(8,128)(2,1)} %bitcast.49), custom_call_target="tpu_custom_call" | custom-call | tf_op jit(solution)/shard_map/pallas_call | solution.py:33
  4.7 0.0 copy-start.5
  4.7 0.0 copy-start.1
  4.7 0.0 copy-start.2
  4.7 0.0 copy-start.3
  4.8 0.0 copy-start.4
  4.8 0.5 collective-permute-start
  5.3 0.0 copy-done
  5.3 1.9 %fusion.9 = (bf16[1,1024,768]{2,1,0:T(8,128)(2,1)}, bf16[1,1024,768]{2,1,0:T(8,128)(2,1)}) fusion(bf16[2,1024,768]{2,1,0:T(8,128)(2,1)S(1)} %copy-done), kind=kLoop, calls=%fused_computation.40 | loop fusion | bytes 6291456 | tf_op jit(solution)/shard_map/slice | solution.py:202
  7.2 5.6 %collective-permute-start.1 = (bf16[1,1024,768]{2,1,0:T(8,128)(2,1)}, bf16[1,1024,768]{2,1,0:T(8,128)(2,1)S(1)}, u32[]{:S(2)}, u32[]{:S(2)}) collective-permute-start(bf16[1,1024,768]{2,1,0:T(8,128)(2,1)} %get-tuple-element.20), channel_id=1, source_target_pairs={{0,14},{1,3},{2,0},{3,5},{4,2},{5,7},{6,4},{7,9},{8,6},{9,11},{10,... | collective-permute-start | bytes 4718600 | tf_op jit(solution)/shard_map/ppermute | solution.py:197
  12.8 0.1 collective-permute-start.2
  12.9 0.0 copy-done.5
  12.9 0.6 dynamic-slice
  14.1 0.0 copy-done.1
  14.1 0.2 dynamic-update-slice
  14.4 72.5 %all-reduce = s32[32]{0:T(128)S(1)} all-reduce(s32[32]{0:T(128)S(1)} %dynamic-update-slice), channel_id=2, replica_groups=mesh['group'=2,'cand'=16] {'cand'}, use_global_device_ids=true, to_apply=%add | all-reduce | flops 32 | bytes 256
  86.9 0.1 reshape.191
  87.0 0.6 slice.76
  87.5 0.6 slice.77
  89.5 0.1 pad.4.clone
  89.6 0.1 pad.8.clone
  89.7 0.1 pad_add_fusion.3
  89.7 0.0 copy-done.2
  89.7 0.0 copy-done.3
  89.7 0.0 copy-done.4
  89.8 0.6 gather_fusion
  90.4 0.6 gather_fusion.1
  91.0 0.1 pad.14.clone
  91.1 0.1 or_select_fusion
  91.2 0.1 pad_add_fusion.1
  91.3 0.0 collective-permute-done
  91.3 3.4 %pad_maximum_fusion.left_ref.right_ref = bf16[4,1024,768]{2,1,0:T(8,128)(2,1)S(1)} fusion(bf16[2,1024,768]{2,1,0:T(8,128)(2,1)} %collective-permute-done, bf16[2,1024,768]{2,1,0:T(8,128)(2,1)} %bitcast.51), kind=kLoop, calls=%fused_computation.2 | loop fusion | flops 3145728 | bytes 12582912 | tf_op jit(solution)/shard_map/concatenate | solution.py:221
  94.7 13.8 %shard_map.65 = (f32[3,1,1024]{2,1,0:T(1,128)S(1)}, f32[3,1,1024]{2,1,0:T(1,128)S(1)}) custom-call(s32[4,3]{1,0:T(4,128)S(1)} %pad_add_fusion.meta, bf16[4,1024,768]{2,1,0:T(8,128)(2,1)S(1)} %pad_maximum_fusion.left_ref.right_ref, bf16[4,1024,768]{2,1,0:T(8,128)(2,1)S(1)} %pad_maximum_fusion.left_ref.right_ref), custom_call_target="tpu_custom_call" | custom-call | flops 4831838208 | bytes 6291456 | tf_op jit(solution)/shard_map/pallas_call | solution.py:148
  108.5 0.0 collective-permute-done.1.left_ref
  108.5 16.9 %shard_map.66 = (f32[4,1,1024]{2,1,0:T(1,128)S(1)}, f32[4,1,1024]{2,1,0:T(1,128)S(1)}) custom-call(s32[4,4]{1,0:T(4,128)S(1)} %get-tuple-element.34.meta, bf16[1,1024,768]{2,1,0:T(8,128)(2,1)S(1)} %collective-permute-done.1.left_ref, bf16[4,1024,768]{2,1,0:T(8,128)(2,1)S(1)} %pad_maximum_fusion.left_ref.right_ref), custom_call_target="tpu_custom_call" | custom-call | flops 6442450944 | bytes 7864320 | tf_op jit(solution)/shard_map/pallas_call | solution.py:148
  125.5 0.0 collective-permute-done.2.left_ref
  125.5 8.2 %shard_map.67 = (f32[4,1,1024]{2,1,0:T(1,128)S(1)}, f32[4,1,1024]{2,1,0:T(1,128)S(1)}) custom-call(s32[4,4]{1,0:T(4,128)S(1)} %get-tuple-element.35.meta, bf16[1,1024,768]{2,1,0:T(8,128)(2,1)S(1)} %collective-permute-done.2.left_ref, bf16[4,1024,768]{2,1,0:T(8,128)(2,1)S(1)} %pad_maximum_fusion.left_ref.right_ref), custom_call_target="tpu_custom_call" | custom-call | flops 6442450944 | bytes 7864320 | tf_op jit(solution)/shard_map/pallas_call | solution.py:148
  133.8 0.1 fusion.1
  133.9 0.1 collective-permute-start.3
  134.0 3.5 %collective-permute-start.4 = (f32[1024]{0:T(1024)S(1)}, f32[1024]{0:T(1024)S(1)}, u32[]{:S(2)}, u32[]{:S(2)}) collective-permute-start(f32[1024]{0:T(1024)S(1)} %reduce_sum.18), channel_id=1, source_target_pairs={{14,0},{3,1},{0,2},{5,3},{2,4},{7,5},{4,6},{9,7},{6,8},{11,9},{8,1... | collective-permute-start | bytes 12296 | tf_op jit(solution)/shard_map/ppermute | solution.py:200
  137.5 0.1 collective-permute-start.5
  137.6 2.8 %collective-permute-done.4 = f32[1024]{0:T(1024)S(1)} collective-permute-done((f32[1024]{0:T(1024)S(1)}, f32[1024]{0:T(1024)S(1)}, u32[]{:S(2)}, u32[]{:S(2)}) %collective-permute-start.4) | collective-permute-done | bytes 4128 | tf_op jit(solution)/shard_map/ppermute | solution.py:200
  140.3 3.0 %collective-permute-done.5 = f32[1024]{0:T(1024)S(1)} collective-permute-done((f32[1024]{0:T(1024)S(1)}, f32[1024]{0:T(1024)S(1)}, u32[]{:S(2)}, u32[]{:S(2)}) %collective-permute-start.5) | collective-permute-done | bytes 4128 | tf_op jit(solution)/shard_map/ppermute | solution.py:200
  143.3 0.0 collective-permute-done.3
  143.3 0.7 compare_select_fusion
  (13 shorter events, 0.1 us)
Async XLA Ops:
  0.0 5.3 %copy-start = (bf16[2,1024,768]{2,1,0:T(8,128)(2,1)S(1)}, bf16[2,1024,768]{2,1,0:T(8,128)(2,1)}, u32[]{:S(2)}) copy-start(bf16[2,1024,768]{2,1,0:T(8,128)(2,1)} %param.6) | copy-start | bytes 9437188
  4.7 8.1 %copy-start.5 = (u32[32]{0:T(128)S(1)}, u32[32]{0:T(128)}, u32[]{:S(2)}) copy-start(u32[32]{0:T(128)} %constant.90) | copy-start | bytes 388
  4.7 9.4 %copy-start.1 = (s32[2]{0:T(128)S(1)}, s32[2]{0:T(128)}, u32[]{:S(2)}) copy-start(s32[2]{0:T(128)} %param.7) | copy-start | bytes 28
  4.7 85.0 %copy-start.2 = (s32[3]{0:T(128)S(1)}, s32[3]{0:T(128)}, u32[]{:S(2)}) copy-start(s32[3]{0:T(128)} %constant.83.clone) | copy-start | bytes 40
  4.7 85.0 %copy-start.3 = (s32[3]{0:T(128)S(1)}, s32[3]{0:T(128)}, u32[]{:S(2)}) copy-start(s32[3]{0:T(128)} %constant.84.clone) | copy-start | bytes 40
  4.8 85.0 %copy-start.4 = (s32[3]{0:T(128)S(1)}, s32[3]{0:T(128)}, u32[]{:S(2)}) copy-start(s32[3]{0:T(128)} %constant.85.clone) | copy-start | bytes 40
  4.8 86.5 %collective-permute-start = (bf16[2,1024,768]{2,1,0:T(8,128)(2,1)}, bf16[2,1024,768]{2,1,0:T(8,128)(2,1)}, u32[]{:S(2)}, u32[]{:S(2)}) collective-permute-start(bf16[2,1024,768]{2,1,0:T(8,128)(2,1)} %bitcast.50), channel_id=1, source_target_pairs={{0,1},{1,0},{2,3},{3,2},{4,5},{5,4},{6,7},{7,6},{8,9},{9,8},{10,11... | collective-permute-start | bytes 9437192 | tf_op jit(solution)/shard_map/ppermute | solution.py:197
  7.2 101.3 %collective-permute-start.1 = (bf16[1,1024,768]{2,1,0:T(8,128)(2,1)}, bf16[1,1024,768]{2,1,0:T(8,128)(2,1)S(1)}, u32[]{:S(2)}, u32[]{:S(2)}) collective-permute-start(bf16[1,1024,768]{2,1,0:T(8,128)(2,1)} %get-tuple-element.20), channel_id=1, source_target_pairs={{0,14},{1,3},{2,0},{3,5},{4,2},{5,7},{6,4},{7,9},{8,6},{9,11},{10,... | collective-permute-start | bytes 4718600 | tf_op jit(solution)/shard_map/ppermute | solution.py:197
  12.8 112.7 %collective-permute-start.2 = (bf16[1,1024,768]{2,1,0:T(8,128)(2,1)}, bf16[1,1024,768]{2,1,0:T(8,128)(2,1)S(1)}, u32[]{:S(2)}, u32[]{:S(2)}) collective-permute-start(bf16[1,1024,768]{2,1,0:T(8,128)(2,1)} %get-tuple-element.21), channel_id=1, source_target_pairs={{0,15},{1,2},{2,1},{3,4},{4,3},{5,6},{6,5},{7,8},{8,7},{9,10},{10,... | collective-permute-start | bytes 4718600 | tf_op jit(solution)/shard_map/ppermute | solution.py:197
  133.9 9.4 %collective-permute-start.3 = (f32[2,1024]{1,0:T(2,128)S(1)}, f32[2,1024]{1,0:T(2,128)S(1)}, u32[]{:S(2)}, u32[]{:S(2)}) collective-permute-start(f32[2,1024]{1,0:T(2,128)S(1)} %slice.86), channel_id=1, source_target_pairs={{0,1},{1,0},{2,3},{3,2},{4,5},{5,4},{6,7},{7,6},{8,9},{9,8},{10,11... | collective-permute-start | bytes 24584 | tf_op jit(solution)/shard_map/ppermute | solution.py:197
  134.0 6.4 %collective-permute-start.4 = (f32[1024]{0:T(1024)S(1)}, f32[1024]{0:T(1024)S(1)}, u32[]{:S(2)}, u32[]{:S(2)}) collective-permute-start(f32[1024]{0:T(1024)S(1)} %reduce_sum.18), channel_id=1, source_target_pairs={{14,0},{3,1},{0,2},{5,3},{2,4},{7,5},{4,6},{9,7},{6,8},{11,9},{8,1... | collective-permute-start | bytes 12296 | tf_op jit(solution)/shard_map/ppermute | solution.py:200
  137.5 5.8 %collective-permute-start.5 = (f32[1024]{0:T(1024)S(1)}, f32[1024]{0:T(1024)S(1)}, u32[]{:S(2)}, u32[]{:S(2)}) collective-permute-start(f32[1024]{0:T(1024)S(1)} %reduce_sum.19), channel_id=1, source_target_pairs={{15,0},{2,1},{1,2},{4,3},{3,4},{6,5},{5,6},{8,7},{7,8},{10,9},{9,1... | collective-permute-start | bytes 12296 | tf_op jit(solution)/shard_map/ppermute | solution.py:200

commit v2 on v1

--- a/solution.py
+++ b/solution.py
@@ -10,6 +10,8 @@
 SCALE = 256.0 * 1.4426950408889634
 LOWEST = -1e30
 LANES = 128
+TAG_ROWS = 16
+TAG_BASE = 64
 ROW_TILE = 1024
 COL_TILE = 512
 SUM_TILE = 256
@@ -22,30 +24,50 @@
     return (values * scale).astype(jnp.bfloat16)
 
 
-def unit_kernel(values_ref, unit_ref):
-    unit_ref[...] = unit_rows(values_ref[...])
-
-
-def make_unit(embeddings):
+def tag_of(length, shape):
+    top = lax.broadcasted_iota(jnp.int32, shape, len(shape) - 2) < TAG_ROWS // 2
+    return jnp.where(top, length // TAG_BASE, length % TAG_BASE).astype(jnp.bfloat16)
+
+
+def length_of(tag):
+    values = tag.astype(jnp.float32)
+    top = lax.broadcasted_iota(jnp.int32, values.shape, 0) < TAG_ROWS // 2
+    high = jnp.max(jnp.where(top, values, 0.0))
+    low = jnp.max(jnp.where(top, 0.0, values))
+    return (high * TAG_BASE + low).astype(jnp.int32)
+
+
+def packet_of(answer, length):
+    return jnp.concatenate([answer, tag_of(length, (TAG_ROWS, answer.shape[1]))])[None]
+
+
+def unit_kernel(lengths, values_ref, unit_ref):
+    rows = values_ref.shape[1]
+    for start in range(0, rows, LANES):
+        unit_ref[0, start : start + LANES, :] = unit_rows(values_ref[0, start : start + LANES, :])
+    unit_ref[0, rows:, :] = tag_of(lengths[pl.program_id(0)], (TAG_ROWS, values_ref.shape[2]))
+
+
+def make_unit(embeddings, lengths):
     answers, length, width = embeddings.shape
-    rows = answers * length
-    tile = min(512, rows)
-    flat = pl.pallas_call(
+    return pl.pallas_call(
         unit_kernel,
-        grid=(rows // tile,),
-        in_specs=[pl.BlockSpec((tile, width), lambda i: (i, 0))],
-        out_specs=pl.BlockSpec((tile, width), lambda i: (i, 0)),
-        out_shape=jax.ShapeDtypeStruct((rows, width), jnp.bfloat16),
-    )(embeddings.reshape(rows, width))
-    return flat.reshape(embeddings.shape)
+        grid_spec=pltpu.PrefetchScalarGridSpec(
+            num_scalar_prefetch=1,
+            grid=(answers,),
+            in_specs=[pl.BlockSpec((1, length, width), lambda i, m: (i, 0, 0))],
+            out_specs=pl.BlockSpec((1, length + TAG_ROWS, width), lambda i, m: (i, 0, 0)),
+        ),
+        out_shape=jax.ShapeDtypeStruct((answers, length + TAG_ROWS, width), jnp.bfloat16),
+    )(lengths, embeddings)
 
 
 def pair_kernel(meta, left_ref, right_ref, row_ref, col_ref, unit, scores, peak, total, *, raw):
     pair = pl.program_id(0)
-    left_rows = left_ref.shape[1]
-    right_rows = right_ref.shape[1]
-    left_len = meta[2, pair]
-    right_len = meta[3, pair]
+    left_rows = left_ref.shape[1] - TAG_ROWS
+    right_rows = right_ref.shape[1] - TAG_ROWS
+    left_len = length_of(left_ref[0, left_rows:, :])
+    right_len = length_of(right_ref[0, right_rows:, :])
     row_tile = min(ROW_TILE, left_rows)
     col_tile = min(COL_TILE, right_rows)
     sum_rows = min(SUM_TILE, left_rows)
@@ -67,7 +89,7 @@
     def steps(count, size):
         return lax.div(count + size - 1, size)
 
-    @pl.when((left_len > 0) & (right_len > 0))
+    @pl.when(meta[2, pair] > 0)
     def _():
         peak[...] = jnp.full_like(peak, LOWEST)
         total[...] = jnp.zeros_like(total)
@@ -143,16 +165,17 @@
 
 def match_pairs(meta, left, right, raw):
     pairs = meta.shape[1]
-    left_rows, width = left.shape[1:]
-    right_rows = right.shape[1]
+    width = left.shape[2]
+    left_rows = left.shape[1] - TAG_ROWS
+    right_rows = right.shape[1] - TAG_ROWS
     rows, cols = pl.pallas_call(
         functools.partial(pair_kernel, raw=raw),
         grid_spec=pltpu.PrefetchScalarGridSpec(
             num_scalar_prefetch=1,
             grid=(pairs,),
             in_specs=[
-                pl.BlockSpec((1, left_rows, width), lambda p, m: (m[0, p], 0, 0)),
-                pl.BlockSpec((1, right_rows, width), lambda p, m: (m[1, p], 0, 0)),
+                pl.BlockSpec((1,) + left.shape[1:], lambda p, m: (m[0, p], 0, 0)),
+                pl.BlockSpec((1,) + right.shape[1:], lambda p, m: (m[1, p], 0, 0)),
             ],
             out_specs=[
                 pl.BlockSpec((1, 1, left_rows), lambda p, m: (p, 0, 0)),
@@ -199,29 +222,20 @@
     def back(value, pairs):
         return lax.ppermute(value, "cand", [(b, a) for a, b in pairs])
 
-    first = move(embeddings[0:1], first_to)
-    unit = make_unit(embeddings)
+    first = move(packet_of(embeddings[0], lengths[0]), first_to)
+    unit = make_unit(embeddings, lengths)
     mate_unit = move(unit, mate_to)
-
-    table = lax.all_gather(lengths, "cand", axis=0)
-
-    def lengths_of(offset):
-        return lax.dynamic_index_in_dim(table, (here + offset) % count, 0, keepdims=False)
-
-    near = jnp.concatenate([lengths, jnp.where(is_even, lengths_of(1), lengths_of(-1))])
-    own_only = jnp.arange(2 * answers, dtype=jnp.int32) < answers
-    first_len = jnp.where(is_even, lengths_of(2)[0], lengths_of(-2)[0])
-    second_len = jnp.where(is_even, lengths_of(-1)[1], lengths_of(1)[1])
-    first_near = jnp.where(is_even | own_only, near, 0)
-    second_near = jnp.where(is_even & own_only, 0, near)
-
-    def meta_of(left, right, left_len, right_len):
-        return jnp.stack([left, right, jnp.broadcast_to(left_len, right.shape), right_len]).astype(jnp.int32)
-
     residents = jnp.concatenate([unit, mate_unit])
-    inner_left = jnp.where(is_even, jnp.array([0, 0, 0]), jnp.array([0, 3, 3]))
-    inner_right = jnp.where(is_even, jnp.array([1, 2, 3]), jnp.array([1, 0, 1]))
-    inner_meta = meta_of(inner_left, inner_right, near[inner_left], near[inner_right])
+
+    every = jnp.arange(2 * answers, dtype=jnp.int32)
+    nothing = jnp.zeros_like(every)
+    first_meta = jnp.stack([nothing, every, (is_even | (every < answers)).astype(jnp.int32)])
+    second_meta = jnp.stack([nothing, every, (~is_even | (every >= answers)).astype(jnp.int32)])
+    inner_meta = jnp.where(
+        is_even,
+        jnp.array([[0, 0, 0], [1, 2, 3], [1, 1, 1]], jnp.int32),
+        jnp.array([[0, 3, 3], [1, 0, 1], [1, 1, 1]], jnp.int32),
+    )
     rows, cols = match_pairs(inner_meta, residents, residents, False)
     zero = jnp.zeros_like(rows[0])
     totals = jnp.where(
@@ -230,13 +244,11 @@
         jnp.stack([rows[0] + cols[1], cols[0] + cols[2], zero, rows[1] + rows[2]]),
     )
 
-    second = move(after(embeddings[1:2], rows), second_to)
-    every = jnp.arange(2 * answers)
-    nothing = jnp.zeros_like(every)
-    rows, cols = match_pairs(meta_of(nothing, every, first_len, first_near), first, residents, True)
+    second = move(after(packet_of(embeddings[1], lengths[1]), rows), second_to)
+    rows, cols = match_pairs(first_meta, first, residents, True)
     totals = totals + cols
     first_back = back(jnp.sum(rows, axis=0), first_to)
-    rows, cols = match_pairs(meta_of(nothing, every, second_len, second_near), second, residents, True)
+    rows, cols = match_pairs(second_meta, second, residents, True)
     totals = totals + cols
     second_back = back(jnp.sum(rows, axis=0), second_to)
     mate_back = move(totals[answers:], mate_to)

time: 141 us -> 111 us (0.79); the launches traced: 144 us -> 112 us
  blocking collectives: 72.5 us -> 0 us
  waiting for transfers between devices: 5.73 us -> 41.6 us
  local copies, waits for them, and re-layouts: 5.59 us -> 2.19 us
  between operations: 2.14 us -> 5.31 us
  other arithmetic: 4.47 us -> 7.39 us
  Pallas kernels: 43.7 us -> 45.4 us
    unnamed x1 -> x0, blocking collectives: 72.5 us -> none
    ppermute x4, waiting for transfers between devices: 0.01 us -> 35.3 us  [move(): return lax.ppermute(value, 'cand', pairs)]
    broadcast_in_dim x0 -> x2, other arithmetic: none -> 3.05 us  [packet_of(): jnp.concatenate([answer, tag_of(length, (TAG_ROWS, answer.shape[1]))])[None]]
    slice x3 -> x1, local copies, waits for them, and re-layouts: 3.14 us -> 0.62 us  [shards(): first = move(packet_of(embeddings[0], lengths[0]), first_to)]
    pallas_call x3, Pallas kernels: 39 us -> 40.9 us  [match_pairs(): pl.pallas_call(functools.partial(pair_kernel, raw=raw), grid_spec=pltpu.P...]
    squeeze x0 -> x1, local copies, waits for them, and re-layouts: none -> 1.45 us  [shards(): first = move(packet_of(embeddings[0], lengths[0]), first_to)]
  transfers between devices with their start and end apart: 6 -> 6, of which waited for: 2 -> 3; matrix products, arithmetic and copies ran while one was open for 6% -> 8% of each run, Pallas kernels for 21% -> 21%
where the time goes in v2:
time: 111 us; the launch traced here: 112 us
  Pallas kernels  45.4 us (41%)
  waiting for transfers between devices  41.6 us (37%)
  starting transfers between devices  9.79 us (9%)
  other arithmetic  7.39 us (7%)
  between operations  5.31 us (5%)
  local copies, waits for them, and re-layouts  2.19 us (2%)
    pallas_call x3, Pallas kernels, match_pairs(): pl.pallas_call(functools.partial(pair_kernel, raw=raw), grid_spec=pltpu.P...  40.9 us
    ppermute x4, waiting for transfers between devices, move(): return lax.ppermute(value, 'cand', pairs)  35.3 us
    ppermute x4, starting transfers between devices, move(): return lax.ppermute(value, 'cand', pairs)  6.7 us
    ppermute x2, waiting for transfers between devices, back(): return lax.ppermute(value, 'cand', [(b, a) for a, b in pairs])  6.29 us
    pallas_call x1, Pallas kernels, make_unit(): pl.pallas_call(unit_kernel, grid_spec=pltpu.PrefetchScalarGridSpec(num_sc...  4.52 us
    concatenate x1, other arithmetic, shards(): residents = jnp.concatenate([unit, mate_unit])  3.43 us
    ppermute x2, starting transfers between devices, back(): return lax.ppermute(value, 'cand', [(b, a) for a, b in pairs])  3.09 us
    broadcast_in_dim x2, other arithmetic, packet_of(): jnp.concatenate([answer, tag_of(length, (TAG_ROWS, answer.shape[1]))])[None]  3.05 us
  transfers between devices with their start and end apart: 6, of which 3 were waited for; matrix products, arithmetic and copies ran while one was open for 8% of the time, Pallas kernels for 21%

profile of v2, /device:TPU:0, one launch (start us, length us, event | category | flops | bytes accessed | tf_op | source)
XLA Modules:
  0.0 111.6 jit_solution(1183396162509908207)
XLA Ops:
  0.0 0.0 copy-start.2
  0.0 0.0 copy-start
  0.0 4.5 %shard_map.46 = bf16[2,1040,768]{2,1,0:T(8,128)(2,1)} custom-call(s32[2]{0:T(128)} %lengths.1, bf16[2,1024,768]{2,1,0:T(8,128)(2,1)} %values_ref.1), custom_call_target="tpu_custom_call" | custom-call | tf_op jit(solution)/shard_map/pallas_call | solution.py:53
  4.5 0.5 collective-permute-start
  5.0 0.0 copy-done.2
  5.0 0.6 fusion.8
  8.2 0.0 copy-done
  8.2 1.4 %slice_bitcast_fusion.1 = (bf16[1024,768]{1,0:T(8,128)(2,1)}, bf16[1024,768]{1,0:T(8,128)(2,1)S(1)}) fusion(bf16[2,1024,768]{2,1,0:T(8,128)(2,1)S(1)} %copy-done), kind=kLoop, calls=%fused_computation.4 | loop fusion | bytes 6291456 | tf_op jit(solution)/shard_map/squeeze | solution.py:225
  9.6 0.0 copy-start.1
  9.6 0.0 copy-start.3
  9.6 0.0 copy-start.4
  9.6 1.5 %maximum_bitcast_fusion.1 = bf16[1,1040,768]{2,1,0:T(8,128)(2,1)} fusion(bf16[1024,768]{1,0:T(8,128)(2,1)S(1)} %get-tuple-element.18, bf16[1040]{0:T(1024)(128)(2,1)S(1)} %pad.3.clone), kind=kLoop, calls=%fused_computation.2 | loop fusion | flops 3194880 | bytes 3172384 | tf_op jit(solution)/shard_map/broadcast_in_dim | solution.py:41
  11.1 5.7 %collective-permute-start.2 = (bf16[1,1040,768]{2,1,0:T(8,128)(2,1)}, bf16[1,1040,768]{2,1,0:T(8,128)(2,1)S(1)}, u32[]{:S(2)}, u32[]{:S(2)}) collective-permute-start(bf16[1,1040,768]{2,1,0:T(8,128)(2,1)} %maximum_bitcast_fusion.1), channel_id=1, source_target_pairs={{0,15},{1,2},{2,1},{3,4},{4,3},{5,6},{6,5},{7,8},{8,7},{9,10},{10,... | collective-permute-start | bytes 4792328 | tf_op jit(solution)/shard_map/ppermute | solution.py:220
  19.4 0.0 copy-done.1
  19.4 1.6 %maximum_bitcast_fusion = bf16[1,1040,768]{2,1,0:T(8,128)(2,1)} fusion(bf16[1024,768]{1,0:T(8,128)(2,1)S(1)} %copy-done.1, bf16[1040]{0:T(1024)(128)(2,1)S(1)} %pad.8.clone), kind=kLoop, calls=%fused_computation.1 | loop fusion | flops 3194880 | bytes 3172384 | tf_op jit(solution)/shard_map/broadcast_in_dim | solution.py:41
  21.0 0.5 collective-permute-start.1
  21.5 0.1 pad.14.clone
  21.6 0.0 copy-done.3
  21.6 0.0 copy-done.4
  21.6 0.1 pad_add_fusion
  21.7 0.0 collective-permute-done
  21.7 3.4 %pad_maximum_fusion.left_ref.right_ref = bf16[4,1040,768]{2,1,0:T(8,128)(2,1)S(1)} fusion(bf16[2,1040,768]{2,1,0:T(8,128)(2,1)} %collective-permute-done, bf16[2,1040,768]{2,1,0:T(8,128)(2,1)} %shard_map.46), kind=kLoop, calls=%fused_computation | loop fusion | flops 3194880 | bytes 12779520 | tf_op jit(solution)/shard_map/concatenate | solution.py:228
  25.1 14.0 %shard_map.47 = (f32[3,1,1024]{2,1,0:T(1,128)S(1)}, f32[3,1,1024]{2,1,0:T(1,128)S(1)}) custom-call(s32[3,3]{1,0:T(4,128)S(1)} %broadcast_select_fusion.meta, bf16[4,1040,768]{2,1,0:T(8,128)(2,1)S(1)} %pad_maximum_fusion.left_ref.right_ref, bf16[4,1040,768]{2,1,0:T(8,128)(2,1)S(1)} %pad_maximum_fusion.left_ref.right_ref), custom_call_target="tpu_custom_call" | custom-call | flops 4831838208 | bytes 6291456 | tf_op jit(solution)/shard_map/pallas_call | solution.py:171
  39.1 0.0 collective-permute-done.2.left_ref
  39.1 9.4 %shard_map.49 = (f32[4,1,1024]{2,1,0:T(1,128)S(1)}, f32[4,1,1024]{2,1,0:T(1,128)S(1)}) custom-call(s32[3,4]{1,0:T(4,128)S(1)} %get-tuple-element.27.meta, bf16[1,1040,768]{2,1,0:T(8,128)(2,1)S(1)} %collective-permute-done.2.left_ref, bf16[4,1040,768]{2,1,0:T(8,128)(2,1)S(1)} %pad_maximum_fusion.left_ref.right_ref), custom_call_target="tpu_custom_call" | custom-call | flops 6442450944 | bytes 7864320 | tf_op jit(solution)/shard_map/pallas_call | solution.py:171
  48.6 35.3 %collective-permute-done.1.left_ref = bf16[1,1040,768]{2,1,0:T(8,128)(2,1)S(1)} collective-permute-done((bf16[1,1040,768]{2,1,0:T(8,128)(2,1)}, bf16[1,1040,768]{2,1,0:T(8,128)(2,1)S(1)}, u32[]{:S(2)}, u32[]{:S(2)}) %collective-permute-start.1) | collective-permute-done | bytes 1597472 | tf_op jit(solution)/shard_map/ppermute | solution.py:220
  83.8 17.5 %shard_map.48 = (f32[4,1,1024]{2,1,0:T(1,128)S(1)}, f32[4,1,1024]{2,1,0:T(1,128)S(1)}) custom-call(s32[3,4]{1,0:T(4,128)S(1)} %get-tuple-element.26.meta, bf16[1,1040,768]{2,1,0:T(8,128)(2,1)S(1)} %collective-permute-done.1.left_ref, bf16[4,1040,768]{2,1,0:T(8,128)(2,1)S(1)} %pad_maximum_fusion.left_ref.right_ref), custom_call_target="tpu_custom_call" | custom-call | flops 6442450944 | bytes 7864320 | tf_op jit(solution)/shard_map/pallas_call | solution.py:171
  101.3 0.1 fusion.1
  101.4 0.1 collective-permute-start.3
  101.5 3.0 %collective-permute-start.5 = (f32[1024]{0:T(1024)S(1)}, f32[1024]{0:T(1024)S(1)}, u32[]{:S(2)}, u32[]{:S(2)}) collective-permute-start(f32[1024]{0:T(1024)S(1)} %reduce_sum.19), channel_id=1, source_target_pairs={{15,0},{2,1},{1,2},{4,3},{3,4},{6,5},{5,6},{8,7},{7,8},{10,9},{9,1... | collective-permute-start | bytes 12296 | tf_op jit(solution)/shard_map/ppermute | solution.py:223
  104.6 0.1 collective-permute-start.4
  104.7 2.7 %collective-permute-done.5 = f32[1024]{0:T(1024)S(1)} collective-permute-done((f32[1024]{0:T(1024)S(1)}, f32[1024]{0:T(1024)S(1)}, u32[]{:S(2)}, u32[]{:S(2)}) %collective-permute-start.5) | collective-permute-done | bytes 4128 | tf_op jit(solution)/shard_map/ppermute | solution.py:223
  107.3 3.6 %collective-permute-done.4 = f32[1024]{0:T(1024)S(1)} collective-permute-done((f32[1024]{0:T(1024)S(1)}, f32[1024]{0:T(1024)S(1)}, u32[]{:S(2)}, u32[]{:S(2)}) %collective-permute-start.4) | collective-permute-done | bytes 4128 | tf_op jit(solution)/shard_map/ppermute | solution.py:223
  111.0 0.0 collective-permute-done.3
  111.0 0.7 compare_select_fusion
  (13 shorter events, 0.1 us)
Async XLA Ops:
  0.0 5.0 %copy-start.2 = (s32[2]{0:T(128)S(1)}, s32[2]{0:T(128)}, u32[]{:S(2)}) copy-start(s32[2]{0:T(128)} %lengths.1) | copy-start | bytes 28
  0.0 8.2 %copy-start = (bf16[2,1024,768]{2,1,0:T(8,128)(2,1)S(1)}, bf16[2,1024,768]{2,1,0:T(8,128)(2,1)}, u32[]{:S(2)}) copy-start(bf16[2,1024,768]{2,1,0:T(8,128)(2,1)} %values_ref.1) | copy-start | bytes 9437188
  4.5 17.2 %collective-permute-start = (bf16[2,1040,768]{2,1,0:T(8,128)(2,1)}, bf16[2,1040,768]{2,1,0:T(8,128)(2,1)}, u32[]{:S(2)}, u32[]{:S(2)}) collective-permute-start(bf16[2,1040,768]{2,1,0:T(8,128)(2,1)} %shard_map.46), channel_id=1, source_target_pairs={{0,1},{1,0},{2,3},{3,2},{4,5},{5,4},{6,7},{7,6},{8,9},{9,8},{10,11... | collective-permute-start | bytes 9584648 | tf_op jit(solution)/shard_map/ppermute | solution.py:220
  9.6 9.8 %copy-start.1 = (bf16[1024,768]{1,0:T(8,128)(2,1)S(1)}, bf16[1024,768]{1,0:T(8,128)(2,1)}, u32[]{:S(2)}) copy-start(bf16[1024,768]{1,0:T(8,128)(2,1)} %get-tuple-element.17) | copy-start | bytes 4718596
  9.6 12.0 %copy-start.3 = (s32[3,3]{1,0:T(4,128)S(1)}, s32[3,3]{1,0:T(4,128)}, u32[]{:S(2)}) copy-start(s32[3,3]{1,0:T(4,128)} %constant.65.clone) | copy-start | bytes 112
  9.6 12.0 %copy-start.4 = (s32[3,3]{1,0:T(4,128)S(1)}, s32[3,3]{1,0:T(4,128)}, u32[]{:S(2)}) copy-start(s32[3,3]{1,0:T(4,128)} %constant.66.clone) | copy-start | bytes 112
  11.1 28.0 %collective-permute-start.2 = (bf16[1,1040,768]{2,1,0:T(8,128)(2,1)}, bf16[1,1040,768]{2,1,0:T(8,128)(2,1)S(1)}, u32[]{:S(2)}, u32[]{:S(2)}) collective-permute-start(bf16[1,1040,768]{2,1,0:T(8,128)(2,1)} %maximum_bitcast_fusion.1), channel_id=1, source_target_pairs={{0,15},{1,2},{2,1},{3,4},{4,3},{5,6},{6,5},{7,8},{8,7},{9,10},{10,... | collective-permute-start | bytes 4792328 | tf_op jit(solution)/shard_map/ppermute | solution.py:220
  21.0 62.9 %collective-permute-start.1 = (bf16[1,1040,768]{2,1,0:T(8,128)(2,1)}, bf16[1,1040,768]{2,1,0:T(8,128)(2,1)S(1)}, u32[]{:S(2)}, u32[]{:S(2)}) collective-permute-start(bf16[1,1040,768]{2,1,0:T(8,128)(2,1)} %maximum_bitcast_fusion), channel_id=1, source_target_pairs={{0,14},{1,3},{2,0},{3,5},{4,2},{5,7},{6,4},{7,9},{8,6},{9,11},{10,... | collective-permute-start | bytes 4792328 | tf_op jit(solution)/shard_map/ppermute | solution.py:220
  101.4 9.5 %collective-permute-start.3 = (f32[2,1024]{1,0:T(2,128)S(1)}, f32[2,1024]{1,0:T(2,128)S(1)}, u32[]{:S(2)}, u32[]{:S(2)}) collective-permute-start(f32[2,1024]{1,0:T(2,128)S(1)} %slice.70), channel_id=1, source_target_pairs={{0,1},{1,0},{2,3},{3,2},{4,5},{5,4},{6,7},{7,6},{8,9},{9,8},{10,11... | collective-permute-start | bytes 24584 | tf_op jit(solution)/shard_map/ppermute | solution.py:220
  101.5 5.8 %collective-permute-start.5 = (f32[1024]{0:T(1024)S(1)}, f32[1024]{0:T(1024)S(1)}, u32[]{:S(2)}, u32[]{:S(2)}) collective-permute-start(f32[1024]{0:T(1024)S(1)} %reduce_sum.19), channel_id=1, source_target_pairs={{15,0},{2,1},{1,2},{4,3},{3,4},{6,5},{5,6},{8,7},{7,8},{10,9},{9,1... | collective-permute-start | bytes 12296 | tf_op jit(solution)/shard_map/ppermute | solution.py:223
  104.6 6.4 %collective-permute-start.4 = (f32[1024]{0:T(1024)S(1)}, f32[1024]{0:T(1024)S(1)}, u32[]{:S(2)}, u32[]{:S(2)}) collective-permute-start(f32[1024]{0:T(1024)S(1)} %reduce_sum.18), channel_id=1, source_target_pairs={{14,0},{3,1},{0,2},{5,3},{2,4},{7,5},{4,6},{9,7},{6,8},{11,9},{8,1... | collective-permute-start | bytes 12296 | tf_op jit(solution)/shard_map/ppermute | solution.py:223

commit v3 on v2

v3 whole, which is shorter than its diff:
```python
import functools

import jax
import jax.numpy as jnp
from jax import lax
from jax.experimental import pallas as pl
from jax.experimental.pallas import tpu as pltpu
from jax.sharding import PartitionSpec as P

SCALE = 256.0 * 1.4426950408889634
LOWEST = -1e30
LANES = 128
TAG_ROWS = 16
TAG_BASE = 64
ROW_TILE = 1024
COL_TILE = 512
SUM_TILE = 256
SUM_STEP = 64


def unit_rows(embeddings):
    values = embeddings.astype(jnp.float32)
    scale = lax.rsqrt(jnp.sum(values * values, axis=-1, keepdims=True) + 1e-06)
    return (values * scale).astype(jnp.bfloat16)


def length_of(tag):
    return tag[0, 0].astype(jnp.int32) * TAG_BASE + tag[TAG_ROWS - 1, 0].astype(jnp.int32)


def packet_kernel(lengths, values_ref, *refs, slot, rows):
    unit_ref = refs[-1]
    tile = unit_ref.shape[1]
    unit = unit_rows(values_ref[0])
    row = lax.broadcasted_iota(jnp.int32, unit.shape, 0) + pl.program_id(0) * tile
    high = lengths[slot] // TAG_BASE
    low = lengths[slot] % TAG_BASE
    tag = jnp.where(row < rows + TAG_ROWS // 2, high, low).astype(jnp.float32)
    unit_ref[0] = jnp.where(row < rows, unit.astype(jnp.float32), tag).astype(jnp.bfloat16)


def packet_of(embeddings, lengths, slot, *earlier):
    _, rows, width = embeddings.shape
    whole = rows + TAG_ROWS
    steps = max(n for n in range(1, 9) if whole % (n * TAG_ROWS) == 0)
    tile = whole // steps
    return pl.pallas_call(
        functools.partial(packet_kernel, slot=slot, rows=rows),
        grid_spec=pltpu.PrefetchScalarGridSpec(
            num_scalar_prefetch=1,
            grid=(steps,),
            in_specs=[pl.BlockSpec((1, tile, width), lambda i, m: (slot, i, 0))]
            + [pl.BlockSpec(memory_space=pl.ANY)] * len(earlier),
            out_specs=pl.BlockSpec((1, tile, width), lambda i, m: (0, i, 0)),
        ),
        out_shape=jax.ShapeDtypeStruct((1, whole, width), jnp.bfloat16),
    )(lengths, embeddings, *earlier)


def pass_kernel(*refs):
    del refs


def after(value, *earlier):
    spec = pl.BlockSpec(memory_space=pl.ANY)
    return pl.pallas_call(
        pass_kernel,
        in_specs=[spec] * (1 + len(earlier)),
        out_specs=spec,
        out_shape=jax.ShapeDtypeStruct(value.shape, value.dtype),
        input_output_aliases={0: 0},
    )(value, *earlier)


def pair_kernel(meta, left_ref, right_ref, peak_in, sum_in, row_ref, peak_ref, sum_ref, scores, peak, total):
    pair = pl.program_id(0)
    left_rows = scores.shape[0]
    right_rows = scores.shape[1]
    left_len = meta[2, pair]
    right_len = meta[3, pair]
    row_tile = min(ROW_TILE, left_rows)
    col_tile = min(COL_TILE, right_rows)
    sum_rows = min(SUM_TILE, left_rows)
    sum_cols = min(SUM_TILE, right_rows)

    row_ref[...] = jnp.zeros_like(row_ref)
    peak_ref[...] = peak_in[...]
    sum_ref[...] = sum_in[...]

    def at(index, size):
        return pl.ds(pl.multiple_of(index * size, size), size)

    def steps(count, size):
        return lax.div(count + size - 1, size)

    @pl.when((left_len > 0) & (right_len > 0))
    def _():
        peak[...] = jnp.full_like(peak, LOWEST)
        total[...] = jnp.zeros_like(total)

        def score_cols(j, carry):
            cols = at(j, col_tile)
            right = right_ref[0, cols, :]
            col_at = lax.broadcasted_iota(jnp.int32, (1, col_tile), 1) + j * col_tile
            col_bias = jnp.where(col_at < right_len, 0.0, LOWEST)

            def score_rows(i, col_peak):
                rows = at(i, row_tile)
                tile = lax.dot_general(
                    left_ref[0, rows, :], right, (((1,), (1,)), ((), ())), preferred_element_type=jnp.float32
                )
                row_at = lax.broadcasted_iota(jnp.int32, (row_tile, 1), 0) + i * row_tile
                row_bias = jnp.where(row_at < left_len, 0.0, LOWEST)
                tile = (tile * SCALE + col_bias) + row_bias
                scores[rows, cols] = tile
                row_peak = peak[rows, :]
                for k in range(0, col_tile, LANES):
                    row_peak = jnp.maximum(row_peak, tile[:, k : k + LANES])
                peak[rows, :] = row_peak
                folded = jnp.max(tile.reshape(row_tile // 8, 8, col_tile), axis=0)
                return jnp.maximum(col_peak, folded)

            col_peak = lax.fori_loop(
                0, steps(left_len, row_tile), score_rows, jnp.full((8, col_tile), LOWEST, jnp.float32)
            )
            peak_ref[0, :, cols] = jnp.maximum(peak_in[0, :, cols], jnp.max(col_peak, axis=0, keepdims=True))
            return carry

        lax.fori_loop(0, steps(right_len, col_tile), score_cols, 0)

        def sum_cols_of(j, carry):
            cols = at(j, sum_cols)
            col_peak = peak_ref[0, :, cols]

            def sum_rows_of(i, col_sum):
                for step in range(0, sum_rows, SUM_STEP):
                    rows = pl.ds(pl.multiple_of(i * sum_rows, sum_rows) + step, SUM_STEP)
                    tile = scores[rows, cols]
                    row_peak = peak[rows, :]
                    row_sum = total[rows, :]
                    for k in range(0, sum_cols, LANES):
                        row_sum = row_sum + jnp.exp2(tile[:, k : k + LANES] - row_peak)
                    total[rows, :] = row_sum
                    terms = jnp.exp2(tile - col_peak)
                    col_sum = col_sum + jnp.sum(terms.reshape(SUM_STEP // 8, 8, sum_cols), axis=0)
                return col_sum

            col_sum = lax.fori_loop(
                0, steps(left_len, sum_rows), sum_rows_of, jnp.zeros((8, sum_cols), jnp.float32)
            )
            earlier = sum_in[0, :, cols] * jnp.exp2(peak_in[0, :, cols] - col_peak)
            sum_ref[0, :, cols] = earlier + jnp.sum(col_sum, axis=0, keepdims=True)
            return carry

        lax.fori_loop(0, steps(right_len, sum_cols), sum_cols_of, 0)

        def finish_rows(i, carry):
            rows = at(i, sum_rows)
            lane_peak = jnp.transpose(peak[rows, :])
            lane_sum = jnp.transpose(total[rows, :])
            row_peak = jnp.max(lane_peak, axis=0, keepdims=True)
            row_sum = jnp.sum(lane_sum * jnp.exp2(lane_peak - row_peak), axis=0, keepdims=True)
            row_ref[0, :, rows] = (row_peak + jnp.log2(row_sum)) * (1.0 / SCALE)
            return carry

        lax.fori_loop(0, steps(left_len, sum_rows), finish_rows, 0)


def match_pairs(meta, left, left_rows, right, peaks=None, sums=None):
    pairs = meta.shape[1]
    width = left.shape[2]
    right_rows = right.shape[1] - TAG_ROWS
    if peaks is None:
        peaks = jnp.full((pairs, 1, right_rows), LOWEST, jnp.float32)
        sums = jnp.zeros((pairs, 1, right_rows), jnp.float32)
    row_spec = pl.BlockSpec((1, 1, left_rows), lambda p, m: (p, 0, 0))
    col_spec = pl.BlockSpec((1, 1, right_rows), lambda p, m: (p, 0, 0))
    col_shape = jax.ShapeDtypeStruct((pairs, 1, right_rows), jnp.float32)
    return pl.pallas_call(
        pair_kernel,
        grid_spec=pltpu.PrefetchScalarGridSpec(
            num_scalar_prefetch=1,
            grid=(pairs,),
            in_specs=[
                pl.BlockSpec((1,) + left.shape[1:], lambda p, m: (m[0, p], 0, 0)),
                pl.BlockSpec((1,) + right.shape[1:], lambda p, m: (m[1, p], 0, 0)),
                col_spec,
                col_spec,
            ],
            out_specs=[row_spec, col_spec, col_spec],
            scratch_shapes=[
                pltpu.VMEM((left_rows, right_rows), jnp.float32),
                pltpu.VMEM((left_rows, LANES), jnp.float32),
                pltpu.VMEM((left_rows, LANES), jnp.float32),
            ],
        ),
        out_shape=[jax.ShapeDtypeStruct((pairs, 1, left_rows), jnp.float32), col_shape, col_shape],
        compiler_params=pltpu.CompilerParams(vmem_limit_bytes=32 << 20),
        cost_estimate=pl.CostEstimate(
            flops=2 * pairs * left_rows * right_rows * width,
            bytes_accessed=2 * (pairs + 1) * right_rows * width,
            transcendentals=2 * pairs * left_rows * right_rows,
        ),
    )(meta, left, right, peaks, sums)


def matches_of(meta, peaks, sums):
    return jnp.where(meta[3][:, None] > 0, (peaks + jnp.log2(sums))[:, 0] * (1.0 / SCALE), 0.0)


def shards(embeddings, lengths):
    answers, length, _ = embeddings.shape
    count = lax.axis_size("cand")
    is_even = lax.axis_index("cand") % 2 == 0

    first_to = [(i, (i - 2 if i % 2 == 0 else i + 2) % count) for i in range(count)]
    second_to = [(i, (i - 1 if i % 2 == 0 else i + 1) % count) for i in range(count)]
    mate_to = [(i, i ^ 1) for i in range(count)]

    def move(value, pairs):
        return lax.ppermute(value, "cand", pairs)

    def back(value, pairs):
        return lax.ppermute(value, "cand", [(b, a) for a, b in pairs])

    own_first = packet_of(embeddings, lengths, 0)
    first = move(own_first, first_to)
    own_second = packet_of(embeddings, lengths, 1, own_first)
    unit = jnp.concatenate([own_first, own_second])
    mate_unit = move(unit, mate_to)
    residents = jnp.concatenate([unit, mate_unit])
    near = jnp.concatenate([lengths, jnp.stack([length_of(mate_unit[k, length:]) for k in range(answers)])])

    every = jnp.arange(2 * answers, dtype=jnp.int32)
    nothing = jnp.zeros_like(every)

    def arrival_meta(left_len, active):
        return jnp.stack([nothing, every, jnp.broadcast_to(left_len, every.shape), jnp.where(active, near, 0)])

    inner_left = jnp.where(is_even, jnp.array([0, 0, 0]), jnp.array([0, 3, 3]))
    inner_right = jnp.where(is_even, jnp.array([1, 2, 3]), jnp.array([1, 0, 1]))
    inner_meta = jnp.stack([inner_left, inner_right, near[inner_left], near[inner_right]]).astype(jnp.int32)
    rows, peaks, sums = match_pairs(inner_meta, residents, length, residents)
    rows = rows[:, 0]
    cols = matches_of(inner_meta, peaks, sums)
    zero = jnp.zeros_like(rows[0])
    totals = jnp.where(
        is_even,
        jnp.stack([rows[0] + rows[1] + rows[2], cols[0], cols[1], cols[2]]),
        jnp.stack([rows[0] + cols[1], cols[0] + cols[2], zero, rows[1] + rows[2]]),
    )

    half = length // 2
    lower = after(jnp.concatenate([own_second[:, :half], own_second[:, length:]], axis=1), first, rows)
    lower = move(lower, second_to)
    first_meta = arrival_meta(length_of(first[0, length:]), is_even | (every < answers))
    rows, peaks, sums = match_pairs(first_meta, first, length, residents)
    totals = totals + matches_of(first_meta, peaks, sums)
    upper = move(after(own_second[:, half:length], rows), second_to)
    first_back = back(jnp.sum(rows[:, 0], axis=0), first_to)

    second_len = length_of(lower[0, half:])
    second_near = ~is_even | (every >= answers)
    second_meta = arrival_meta(jnp.minimum(second_len, half), second_near)
    lower_rows, peaks, sums = match_pairs(second_meta, lower, half, residents)
    second_meta = arrival_meta(jnp.maximum(second_len - half, 0), second_near)
    upper_rows, peaks, sums = match_pairs(second_meta, upper, length - half, residents, peaks, sums)
    totals = totals + matches_of(second_meta, peaks, sums)
    second_rows = jnp.concatenate([jnp.sum(lower_rows[:, 0], axis=0), jnp.sum(upper_rows[:, 0], axis=0)])
    second_back = back(second_rows, second_to)
    mate_back = move(totals[answers:], mate_to)

    consensus = totals[:answers] + mate_back + jnp.stack([first_back, second_back])
    inside = lax.broadcasted_iota(jnp.int32, (answers, length), 1) < lengths[:, None]
    return jnp.where(inside, consensus / (answers - 1 + 4 * answers), 0.0)


def solution(mesh):
    return jax.shard_map(
        shards,
        mesh=mesh,
        in_specs=(P(("group", "cand"), None, None), P(("group", "cand"))),
        out_specs=P(("group", "cand"), None),
        check_vma=False,
    )
```

time: 111 us -> 131 us (1.18); the launches traced: 112 us -> 130 us
  starting transfers between devices: 9.79 us -> 32 us
  waiting for transfers between devices: 41.6 us -> 22.7 us
  local copies, waits for them, and re-layouts: 2.19 us -> 18 us
  Pallas kernels: 45.4 us -> 41.5 us
  other arithmetic: 7.39 us -> 10.2 us
    ppermute x4 -> x5, waiting for transfers between devices: 35.3 us -> 19.9 us  [move(): return lax.ppermute(value, 'cand', pairs)]
    ppermute x4 -> x5, starting transfers between devices: 6.7 us -> 19.7 us  [move(): return lax.ppermute(value, 'cand', pairs)]
    unnamed x10 -> x25, local copies, waits for them, and re-layouts: 0.02 us -> 12.2 us
    ppermute x2, starting transfers between devices: 3.09 us -> 12.3 us  [back(): return lax.ppermute(value, 'cand', [(b, a) for a, b in pairs])]
    concatenate x0 -> x3, other arithmetic: none -> 5 us  [the longest x1 4.01 us: shards(): unit = jnp.concatenate([own_first, own_second])]
    pallas_call x4 -> x8, Pallas kernels: 45.4 us -> 41.5 us  [the longest x4 31.2 us: match_pairs(): pl.pallas_call(pair_kernel, grid_spec=pltpu.PrefetchScalarGridSpec(num_sc...]
    ppermute x2, waiting for transfers between devices: 6.29 us -> 2.82 us  [back(): return lax.ppermute(value, 'cand', [(b, a) for a, b in pairs])]
    broadcast_in_dim x2 -> x0, other arithmetic: 3.05 us -> none  [packet_of(): jnp.concatenate([answer, tag_of(length, (TAG_ROWS, answer.shape[1]))])[None]]
  transfers between devices with their start and end apart: 6 -> 7, of which waited for: 3 -> 3; matrix products, arithmetic and copies ran while one was open for 8% -> 9% of each run, Pallas kernels for 21% -> 14%
where the time goes in v3:
time: 131 us; the launch traced here: 130 us
  Pallas kernels  41.5 us (32%)
  starting transfers between devices  32 us (24%)
  waiting for transfers between devices  22.7 us (17%)
  local copies, waits for them, and re-layouts  18 us (14%)
  other arithmetic  10.2 us (8%)
  between operations  5.35 us (4%)
    pallas_call x4, Pallas kernels, match_pairs(): pl.pallas_call(pair_kernel, grid_spec=pltpu.PrefetchScalarGridSpec(num_sc...  31.2 us
    ppermute x5, waiting for transfers between devices, move(): return lax.ppermute(value, 'cand', pairs)  19.9 us
    ppermute x5, starting transfers between devices, move(): return lax.ppermute(value, 'cand', pairs)  19.7 us
    ppermute x2, starting transfers between devices, back(): return lax.ppermute(value, 'cand', [(b, a) for a, b in pairs])  12.3 us
    unnamed x25, local copies, waits for them, and re-layouts  12.2 us
    pallas_call x2, Pallas kernels, packet_of(): pl.pallas_call(functools.partial(packet_kernel, slot=slot, rows=rows), gr...  10.3 us
    concatenate x1, other arithmetic, shards(): unit = jnp.concatenate([own_first, own_second])  4.01 us
    concatenate x1, other arithmetic, shards(): residents = jnp.concatenate([unit, mate_unit])  3.29 us
  transfers between devices with their start and end apart: 7, of which 3 were waited for; matrix products, arithmetic and copies ran while one was open for 9% of the time, Pallas kernels for 14%

profile of v3, /device:TPU:0, one launch (start us, length us, event | category | flops | bytes accessed | tf_op | source)
XLA Modules:
  0.0 129.9 jit_solution(15065300833402347665)
XLA Ops:
  0.0 5.2 %shard_map.64.refs_0_ = bf16[1,1040,768]{2,1,0:T(8,128)(2,1)} custom-call(s32[2]{0:T(128)} %lengths.3, bf16[2,1024,768]{2,1,0:T(8,128)(2,1)} %values_ref.3), custom_call_target="tpu_custom_call" | custom-call | tf_op jit(solution)/shard_map/pallas_call | solution.py:47
  5.2 5.1 %shard_map.65 = bf16[1,1040,768]{2,1,0:T(8,128)(2,1)} custom-call(s32[2]{0:T(128)} %lengths.3, bf16[2,1024,768]{2,1,0:T(8,128)(2,1)} %values_ref.3, bf16[1,1040,768]{2,1,0:T(8,128)(2,1)} %shard_map.64.refs_0_), custom_call_target="tpu_custom_call" | custom-call | tf_op jit(solution)/shard_map/pallas_call | solution.py:47
  10.3 0.0 copy-start.9
  10.3 0.0 copy-start.10
  10.3 0.0 copy-start.11
  10.3 0.0 copy-start.7
  10.3 4.0 %pad_maximum_fusion.1 = bf16[2,1040,768]{2,1,0:T(8,128)(2,1)} fusion(bf16[1,1040,768]{2,1,0:T(8,128)(2,1)} %shard_map.65, bf16[1,1040,768]{2,1,0:T(8,128)(2,1)} %shard_map.64.refs_0_), kind=kLoop, calls=%fused_computation.3 | loop fusion | flops 1597440 | bytes 6389760 | tf_op jit(solution)/shard_map/concatenate | solution.py:229
  14.3 0.5 collective-permute-start
  14.8 5.6 %collective-permute-start.1 = (bf16[1,1040,768]{2,1,0:T(8,128)(2,1)}, bf16[1,1040,768]{2,1,0:T(8,128)(2,1)S(1)}, u32[]{:S(2)}, u32[]{:S(2)}) collective-permute-start(bf16[1,1040,768]{2,1,0:T(8,128)(2,1)} %shard_map.64.refs_0_), channel_id=1, source_target_pairs={{0,14},{1,3},{2,0},{3,5},{4,2},{5,7},{6,4},{7,9},{8,6},{9,11},{10,... | collective-permute-start | bytes 4792328 | tf_op jit(solution)/shard_map/ppermute | solution.py:221
  20.4 0.1 pad.23.clone
  20.5 0.0 copy-done.9
  20.5 0.0 copy-done.10
  20.5 0.0 copy-done.11
  20.5 0.0 copy-done.7
  20.5 1.0 fusion.14
  21.5 0.0 slice-done
  21.5 1.0 pad_maximum_fusion.2.refs_0_
  22.5 0.0 collective-permute-done
  22.5 0.8 slice_bitcast_fusion.3
  23.3 0.6 fusion.17
  26.5 0.0 copy-done.8
  26.5 0.1 fusion.10
  26.6 0.6 gather_fusion
  27.2 0.6 gather_fusion.1
  27.9 3.3 %pad_maximum_fusion.left_ref.right_ref = bf16[4,1040,768]{2,1,0:T(8,128)(2,1)S(1)} fusion(bf16[2,1040,768]{2,1,0:T(8,128)(2,1)} %collective-permute-done, bf16[1,1040,768]{2,1,0:T(8,128)(2,1)S(1)} %copy-done.7, bf16[1,1040,768]{2,1,0:T(8,128)(2,1)} %shard_map.64.refs_0_), kind=kLoop, calls=%fused_computation.2 | loop fusion | flops 6389760 | bytes 12779520 | tf_op jit(solution)/shard_map/concatenate | solution.py:231
  31.2 0.0 copy-start
  31.2 9.6 %shard_map.66 = (f32[3,1,1024]{2,1,0:T(1,128)S(1)}, f32[3,1,1024]{2,1,0:T(1,128)S(1)}, f32[3,1,1024]{2,1,0:T(1,128)S(1)}) custom-call(s32[4,3]{1,0:T(4,128)S(1)} %pad_add_fusion.2.meta, bf16[4,1040,768]{2,1,0:T(8,128)(2,1)S(1)} %pad_maximum_fusion.left_ref.right_ref, bf16[4,1040,768]{2,1,0:T(8,128)(2,1)S(1)} %pad_maximum_fusion.left_ref.right_ref, ...), custom_call_target="tpu_custom_call" | custom-call | flops 4831838208 | bytes 6291456 | tf_op jit(solution)/shard_map/pallas_call | solution.py:179
  40.8 0.0 copy-done
  40.8 0.6 copy.45
  41.4 11.9 %collective-permute-done.1.left_ref.refs_1_ = bf16[1,1040,768]{2,1,0:T(8,128)(2,1)S(1)} collective-permute-done((bf16[1,1040,768]{2,1,0:T(8,128)(2,1)}, bf16[1,1040,768]{2,1,0:T(8,128)(2,1)S(1)}, u32[]{:S(2)}, u32[]{:S(2)}) %collective-permute-start.1) | collective-permute-done | bytes 1597472 | tf_op jit(solution)/shard_map/ppermute | solution.py:221
  53.3 1.2 copy-done.4
  54.5 4.0 %collective-permute-start.2 = (bf16[1,528,768]{2,1,0:T(8,128)(2,1)}, bf16[1,528,768]{2,1,0:T(8,128)(2,1)S(1)}, u32[]{:S(2)}, u32[]{:S(2)}) collective-permute-start(bf16[1,528,768]{2,1,0:T(8,128)(2,1)} %shard_map.68), channel_id=1, source_target_pairs={{0,15},{1,2},{2,1},{3,4},{4,3},{5,6},{6,5},{7,8},{8,7},{9,10},{10,... | collective-permute-start | bytes 2433032 | tf_op jit(solution)/shard_map/ppermute | solution.py:221
  58.5 0.7 slice_bitcast_fusion.1
  59.2 0.5 fusion.15
  61.0 0.1 pad.16.clone
  61.1 0.1 or_select_fusion.2
  61.2 8.0 %collective-permute-done.2.left_ref = bf16[1,528,768]{2,1,0:T(8,128)(2,1)S(1)} collective-permute-done((bf16[1,528,768]{2,1,0:T(8,128)(2,1)}, bf16[1,528,768]{2,1,0:T(8,128)(2,1)S(1)}, u32[]{:S(2)}, u32[]{:S(2)}) %collective-permute-start.2) | collective-permute-done | bytes 811040 | tf_op jit(solution)/shard_map/ppermute | solution.py:221
  69.2 0.5 fusion.16
  71.0 0.1 pad.10.clone
  71.1 0.1 pad.6.clone
  71.2 0.1 pad_add_fusion
  71.3 0.0 copy-start.1
  71.3 2.8 %copy-done.1 = bf16[4,1040,768]{2,1,0:T(8,128)(2,1)S(1)} copy-done((bf16[4,1040,768]{2,1,0:T(8,128)(2,1)S(1)}, bf16[4,1040,768]{2,1,0:T(8,128)(2,1)}, u32[]{:S(2)}) %copy-start.1) | copy-done | bytes 6389784
  74.1 1.4 %copy-done.5 = bf16[1,1040,768]{2,1,0:T(8,128)(2,1)S(1)} copy-done((bf16[1,1040,768]{2,1,0:T(8,128)(2,1)S(1)}, bf16[1,1040,768]{2,1,0:T(8,128)(2,1)}, u32[]{:S(2)}) %copy-start.5) | copy-done | bytes 1597464
  75.5 13.2 %shard_map.67 = (f32[4,1,1024]{2,1,0:T(1,128)S(1)}, f32[4,1,1024]{2,1,0:T(1,128)S(1)}, f32[4,1,1024]{2,1,0:T(1,128)S(1)}) custom-call(s32[4,4]{1,0:T(4,128)S(1)} %get-tuple-element.51.meta, bf16[1,1040,768]{2,1,0:T(8,128)(2,1)S(1)} %copy-done.5, bf16[4,1040,768]{2,1,0:T(8,128)(2,1)S(1)} %copy-done.1, f32[4,1,1024]{2,1,0:T(1,128)S(1)} %broadcast_15_peak_in.2.peak_in, ...), custom_call_target="tpu_custom_call" | custom-call | flops 6442450944 | bytes 7864320 | tf_op jit(solution)/shard_map/pallas_call | solution.py:179
  88.7 0.0 copy-start.6
  88.7 0.6 copy-done.6
  89.3 0.0 collective-permute-start.3
  89.3 0.1 bitcast_select_fusion.2
  89.4 0.7 reduce_sum.27
  90.1 0.0 copy-start.2
  90.1 2.8 %copy-done.2 = bf16[4,1040,768]{2,1,0:T(8,128)(2,1)S(1)} copy-done((bf16[4,1040,768]{2,1,0:T(8,128)(2,1)S(1)}, bf16[4,1040,768]{2,1,0:T(8,128)(2,1)}, u32[]{:S(2)}) %copy-start.2) | copy-done | bytes 6389784
  92.9 4.6 %shard_map.70 = (f32[4,1,512]{2,1,0:T(1,128)S(1)}, f32[4,1,1024]{2,1,0:T(1,128)S(1)}, f32[4,1,1024]{2,1,0:T(1,128)S(1)}) custom-call(s32[4,4]{1,0:T(4,128)S(1)} %get-tuple-element.49.meta, bf16[1,528,768]{2,1,0:T(8,128)(2,1)S(1)} %collective-permute-done.2.left_ref, bf16[4,1040,768]{2,1,0:T(8,128)(2,1)S(1)} %copy-done.2, ...), custom_call_target="tpu_custom_call" | custom-call | flops 3221225472 | bytes 7864320 | tf_op jit(solution)/shard_map/pallas_call | solution.py:179
  97.6 9.4 %collective-permute-start.5 = (f32[1024]{0:T(1024)S(1)}, f32[1024]{0:T(1024)S(1)}, u32[]{:S(2)}, u32[]{:S(2)}) collective-permute-start(f32[1024]{0:T(1024)S(1)} %reduce_sum.27), channel_id=1, source_target_pairs={{14,0},{3,1},{0,2},{5,3},{2,4},{7,5},{4,6},{9,7},{6,8},{11,9},{8,1... | collective-permute-start | bytes 12296 | tf_op jit(solution)/shard_map/ppermute | solution.py:224
  107.0 0.0 collective-permute-done.3.left_ref
  107.0 2.8 %copy-done.3 = bf16[4,1040,768]{2,1,0:T(8,128)(2,1)S(1)} copy-done((bf16[4,1040,768]{2,1,0:T(8,128)(2,1)S(1)}, bf16[4,1040,768]{2,1,0:T(8,128)(2,1)}, u32[]{:S(2)}) %copy-start.3) | copy-done | bytes 6389784
  109.9 3.8 %shard_map.71 = (f32[4,1,512]{2,1,0:T(1,128)S(1)}, f32[4,1,1024]{2,1,0:T(1,128)S(1)}, f32[4,1,1024]{2,1,0:T(1,128)S(1)}) custom-call(s32[4,4]{1,0:T(4,128)S(1)} %get-tuple-element.50.meta, bf16[1,512,768]{2,1,0:T(8,128)(2,1)S(1)} %collective-permute-done.3.left_ref, bf16[4,1040,768]{2,1,0:T(8,128)(2,1)S(1)} %copy-done.3, ...), custom_call_target="tpu_custom_call" | custom-call | flops 3221225472 | bytes 7864320 | tf_op jit(solution)/shard_map/pallas_call | solution.py:179
  113.8 0.1 fusion.1
  113.9 9.6 %collective-permute-start.4 = (f32[2,1024]{1,0:T(2,128)S(1)}, f32[2,1024]{1,0:T(2,128)S(1)}, u32[]{:S(2)}, u32[]{:S(2)}) collective-permute-start(f32[2,1024]{1,0:T(2,128)S(1)} %slice.125), channel_id=1, source_target_pairs={{0,1},{1,0},{2,3},{3,2},{4,5},{5,4},{6,7},{7,6},{8,9},{9,8},{10,11... | collective-permute-start | bytes 24584 | tf_op jit(solution)/shard_map/ppermute | solution.py:221
  123.5 2.9 %collective-permute-start.6 = (f32[1024]{0:T(1024)S(1)}, f32[1024]{0:T(1024)S(1)}, u32[]{:S(2)}, u32[]{:S(2)}) collective-permute-start(f32[1024]{0:T(1024)S(1)} %pad_maximum_fusion.3), channel_id=1, source_target_pairs={{15,0},{2,1},{1,2},{4,3},{3,4},{6,5},{5,6},{8,7},{7,8},{10,9},{9,1... | collective-permute-start | bytes 12296 | tf_op jit(solution)/shard_map/ppermute | solution.py:224
  126.4 0.0 collective-permute-done.5
  126.4 2.8 %collective-permute-done.6 = f32[1024]{0:T(1024)S(1)} collective-permute-done((f32[1024]{0:T(1024)S(1)}, f32[1024]{0:T(1024)S(1)}, u32[]{:S(2)}, u32[]{:S(2)}) %collective-permute-start.6) | collective-permute-done | bytes 4128 | tf_op jit(solution)/shard_map/ppermute | solution.py:224
  129.3 0.0 collective-permute-done.4
  129.3 0.7 compare_select_fusion
  (27 shorter events, 0.2 us)
Async XLA Ops:
  10.3 10.2 %copy-start.9 = (s32[3]{0:T(128)S(1)}, s32[3]{0:T(128)}, u32[]{:S(2)}) copy-start(s32[3]{0:T(128)} %constant.63.clone) | copy-start | bytes 40
  10.3 10.2 %copy-start.10 = (s32[3]{0:T(128)S(1)}, s32[3]{0:T(128)}, u32[]{:S(2)}) copy-start(s32[3]{0:T(128)} %constant.64.clone) | copy-start | bytes 40
  10.3 10.2 %copy-start.11 = (s32[3]{0:T(128)S(1)}, s32[3]{0:T(128)}, u32[]{:S(2)}) copy-start(s32[3]{0:T(128)} %constant.65.clone) | copy-start | bytes 40
  10.3 10.2 %copy-start.7 = (bf16[1,1040,768]{2,1,0:T(8,128)(2,1)S(1)}, bf16[1,1040,768]{2,1,0:T(8,128)(2,1)}, u32[]{:S(2)}) copy-start(bf16[1,1040,768]{2,1,0:T(8,128)(2,1)} %shard_map.65) | copy-start | bytes 4792324
  14.3 7.2 %slice-start = ((bf16[1,1040,768]{2,1,0:T(8,128)(2,1)}), bf16[1,16,768]{2,1,0:T(8,128)(2,1)S(1)}, s32[]{:S(2)}) async-start(bf16[1,1040,768]{2,1,0:T(8,128)(2,1)} %shard_map.65), calls=%async_computation | async-start | bytes 49152 | tf_op jit(solution)/shard_map/slice | solution.py:254
  14.3 12.2 %copy-start.8 = (s32[2]{0:T(128)S(1)}, s32[2]{0:T(128)}, u32[]{:S(2)}) copy-start(s32[2]{0:T(128)} %lengths.3) | copy-start | bytes 28
  14.3 8.2 %collective-permute-start = (bf16[2,1040,768]{2,1,0:T(8,128)(2,1)}, bf16[2,1040,768]{2,1,0:T(8,128)(2,1)}, u32[]{:S(2)}, u32[]{:S(2)}) collective-permute-start(bf16[2,1040,768]{2,1,0:T(8,128)(2,1)} %pad_maximum_fusion.1), channel_id=1, source_target_pairs={{0,1},{1,0},{2,3},{3,2},{4,5},{5,4},{6,7},{7,6},{8,9},{9,8},{10,11... | collective-permute-start | bytes 9584648 | tf_op jit(solution)/shard_map/ppermute | solution.py:221
  14.8 38.6 %collective-permute-start.1 = (bf16[1,1040,768]{2,1,0:T(8,128)(2,1)}, bf16[1,1040,768]{2,1,0:T(8,128)(2,1)S(1)}, u32[]{:S(2)}, u32[]{:S(2)}) collective-permute-start(bf16[1,1040,768]{2,1,0:T(8,128)(2,1)} %shard_map.64.refs_0_), channel_id=1, source_target_pairs={{0,14},{1,3},{2,0},{3,5},{4,2},{5,7},{6,4},{7,9},{8,6},{9,11},{10,... | collective-permute-start | bytes 4792328 | tf_op jit(solution)/shard_map/ppermute | solution.py:221
  31.2 9.7 %copy-start = (bf16[4,1040,768]{2,1,0:T(8,128)(2,1)}, bf16[4,1040,768]{2,1,0:T(8,128)(2,1)S(1)}, u32[]{:S(2)}) copy-start(bf16[4,1040,768]{2,1,0:T(8,128)(2,1)S(1)} %pad_maximum_fusion.left_ref.right_ref) | copy-start | bytes 19169284
  53.3 1.2 copy-start.4
  54.5 14.7 %collective-permute-start.2 = (bf16[1,528,768]{2,1,0:T(8,128)(2,1)}, bf16[1,528,768]{2,1,0:T(8,128)(2,1)S(1)}, u32[]{:S(2)}, u32[]{:S(2)}) collective-permute-start(bf16[1,528,768]{2,1,0:T(8,128)(2,1)} %shard_map.68), channel_id=1, source_target_pairs={{0,15},{1,2},{2,1},{3,4},{4,3},{5,6},{6,5},{7,8},{8,7},{9,10},{10,... | collective-permute-start | bytes 2433032 | tf_op jit(solution)/shard_map/ppermute | solution.py:221
  71.3 2.8 %copy-start.1 = (bf16[4,1040,768]{2,1,0:T(8,128)(2,1)S(1)}, bf16[4,1040,768]{2,1,0:T(8,128)(2,1)}, u32[]{:S(2)}) copy-start(bf16[4,1040,768]{2,1,0:T(8,128)(2,1)} %copy-done) | copy-start | bytes 19169284
  74.1 1.4 %copy-start.5 = (bf16[1,1040,768]{2,1,0:T(8,128)(2,1)S(1)}, bf16[1,1040,768]{2,1,0:T(8,128)(2,1)}, u32[]{:S(2)}) copy-start(bf16[1,1040,768]{2,1,0:T(8,128)(2,1)} %copy-done.4) | copy-start | bytes 4792324
  88.7 0.6 copy-start.6
  89.3 17.8 %collective-permute-start.3 = (bf16[1,512,768]{2,1,0:T(8,128)(2,1)}, bf16[1,512,768]{2,1,0:T(8,128)(2,1)S(1)}, u32[]{:S(2)}, u32[]{:S(2)}) collective-permute-start(bf16[1,512,768]{2,1,0:T(8,128)(2,1)} %shard_map.69), channel_id=1, source_target_pairs={{0,15},{1,2},{2,1},{3,4},{4,3},{5,6},{6,5},{7,8},{8,7},{9,10},{10,... | collective-permute-start | bytes 2359304 | tf_op jit(solution)/shard_map/ppermute | solution.py:221
  90.1 2.8 %copy-start.2 = (bf16[4,1040,768]{2,1,0:T(8,128)(2,1)S(1)}, bf16[4,1040,768]{2,1,0:T(8,128)(2,1)}, u32[]{:S(2)}) copy-start(bf16[4,1040,768]{2,1,0:T(8,128)(2,1)} %copy-done) | copy-start | bytes 19169284
  97.6 28.8 %collective-permute-start.5 = (f32[1024]{0:T(1024)S(1)}, f32[1024]{0:T(1024)S(1)}, u32[]{:S(2)}, u32[]{:S(2)}) collective-permute-start(f32[1024]{0:T(1024)S(1)} %reduce_sum.27), channel_id=1, source_target_pairs={{14,0},{3,1},{0,2},{5,3},{2,4},{7,5},{4,6},{9,7},{6,8},{11,9},{8,1... | collective-permute-start | bytes 12296 | tf_op jit(solution)/shard_map/ppermute | solution.py:224
  107.0 2.8 %copy-start.3 = (bf16[4,1040,768]{2,1,0:T(8,128)(2,1)S(1)}, bf16[4,1040,768]{2,1,0:T(8,128)(2,1)}, u32[]{:S(2)}) copy-start(bf16[4,1040,768]{2,1,0:T(8,128)(2,1)} %copy-done) | copy-start | bytes 19169284
  113.9 15.4 %collective-permute-start.4 = (f32[2,1024]{1,0:T(2,128)S(1)}, f32[2,1024]{1,0:T(2,128)S(1)}, u32[]{:S(2)}, u32[]{:S(2)}) collective-permute-start(f32[2,1024]{1,0:T(2,128)S(1)} %slice.125), channel_id=1, source_target_pairs={{0,1},{1,0},{2,3},{3,2},{4,5},{5,4},{6,7},{7,6},{8,9},{9,8},{10,11... | collective-permute-start | bytes 24584 | tf_op jit(solution)/shard_map/ppermute | solution.py:221
  123.5 5.7 %collective-permute-start.6 = (f32[1024]{0:T(1024)S(1)}, f32[1024]{0:T(1024)S(1)}, u32[]{:S(2)}, u32[]{:S(2)}) collective-permute-start(f32[1024]{0:T(1024)S(1)} %pad_maximum_fusion.3), channel_id=1, source_target_pairs={{15,0},{2,1},{1,2},{4,3},{3,4},{6,5},{5,6},{8,7},{7,8},{10,9},{9,1... | collective-permute-start | bytes 12296 | tf_op jit(solution)/shard_map/ppermute | solution.py:224

commit v4 on v0

v4 whole, which is shorter than its diff:
```python
import functools

import jax
import jax.numpy as jnp
from jax import lax
from jax.experimental import pallas as pl
from jax.experimental.pallas import tpu as pltpu
from jax.sharding import PartitionSpec as P

SCALE = 256.0 * 1.4426950408889634
LOWEST = -1e30
LANES = 128
TAG_ROWS = 16
TAG_BASE = 64
ROW_TILE = 512
COL_TILE = 512
SUM_STEP = 64
CHUNKS = 4
SMALL_COST = pl.CostEstimate(flops=1, bytes_accessed=1, transcendentals=0)


def unit_rows(embeddings):
    values = embeddings.astype(jnp.float32)
    scale = lax.rsqrt(jnp.sum(values * values, axis=-1, keepdims=True) + 1e-06)
    return (values * scale).astype(jnp.bfloat16)


def length_of(tag):
    values = tag.astype(jnp.float32)
    upper = lax.broadcasted_iota(jnp.int32, values.shape, 0) < TAG_ROWS // 2
    high = jnp.max(jnp.where(upper, values, 0.0)).astype(jnp.int32)
    low = jnp.max(jnp.where(upper, 0.0, values)).astype(jnp.int32)
    return high * TAG_BASE + low


def packet_kernel(lengths, values_ref, *refs, slot, rows):
    packet_ref, values_buf, packet_buf, in_sem, out_sem = refs[-5:]
    chunk = rows // CHUNKS
    tags = pl.ds(rows, TAG_ROWS)

    def copy_in(k):
        at = pl.ds(k * chunk, chunk)
        return pltpu.make_async_copy(values_ref.at[slot, at, :], values_buf.at[at, :], in_sem.at[k])

    def copy_out(k):
        at = pl.ds(k * chunk, chunk)
        return pltpu.make_async_copy(packet_buf.at[at, :], packet_ref.at[0, at, :], out_sem.at[k])

    for k in range(CHUNKS):
        copy_in(k).start()
    shape = (TAG_ROWS, values_buf.shape[1])
    upper = lax.broadcasted_iota(jnp.int32, shape, 0) < TAG_ROWS // 2
    tag = jnp.where(upper, lengths[slot] // TAG_BASE, lengths[slot] % TAG_BASE)
    packet_buf[tags, :] = tag.astype(jnp.float32).astype(jnp.bfloat16)
    tag_out = pltpu.make_async_copy(packet_buf.at[tags, :], packet_ref.at[0, tags, :], out_sem.at[CHUNKS])
    tag_out.start()
    for k in range(CHUNKS):
        copy_in(k).wait()
        at = pl.ds(k * chunk, chunk)
        packet_buf[at, :] = unit_rows(values_buf[at, :])
        copy_out(k).start()
    for k in range(CHUNKS):
        copy_out(k).wait()
    tag_out.wait()


def packet_of(embeddings, lengths, slot, *earlier):
    _, rows, width = embeddings.shape
    whole = rows + TAG_ROWS
    anywhere = pl.BlockSpec(memory_space=pl.ANY)
    return pl.pallas_call(
        functools.partial(packet_kernel, slot=slot, rows=rows),
        grid_spec=pltpu.PrefetchScalarGridSpec(
            num_scalar_prefetch=1,
            grid=(1,),
            in_specs=[anywhere] * (1 + len(earlier)),
            out_specs=anywhere,
            scratch_shapes=[
                pltpu.VMEM((rows, width), jnp.bfloat16),
                pltpu.VMEM((whole, width), jnp.bfloat16),
                pltpu.SemaphoreType.DMA((CHUNKS,)),
                pltpu.SemaphoreType.DMA((CHUNKS + 1,)),
            ],
        ),
        out_shape=jax.ShapeDtypeStruct((1, whole, width), jnp.bfloat16),
        compiler_params=pltpu.CompilerParams(vmem_limit_bytes=60 << 20),
        cost_estimate=SMALL_COST,
    )(lengths, embeddings, *earlier)


def pass_kernel(*refs):
    del refs


def after(value, *earlier):
    spec = pl.BlockSpec(memory_space=pl.ANY)
    return pl.pallas_call(
        pass_kernel,
        in_specs=[spec] * (1 + len(earlier)),
        out_specs=spec,
        out_shape=jax.ShapeDtypeStruct(value.shape, value.dtype),
        input_output_aliases={0: 0},
        cost_estimate=SMALL_COST,
    )(value, *earlier)


def match_kernel(meta, *refs, lefts, rights, offset):
    left_refs = refs[:lefts]
    tag_refs = refs[lefts : 2 * lefts]
    right_refs = refs[2 * lefts : 2 * lefts + rights]
    peak_in, sum_in, row_ref, peak_ref, sum_ref = refs[2 * lefts + rights : 2 * lefts + rights + 5]
    (left_buf, left_tags, right_buf, scores_even, scores_odd, rows_even, rows_odd, cols_even, cols_odd, base, total,
     items, waiting, left_sem, tag_sem, right_sem) = refs[2 * lefts + rights + 5 :]
    row_tile, col_tile = scores_even.shape
    left_rows = left_buf.shape[1]
    right_rows = peak_ref.shape[2]
    most = (meta.shape[0] - 1) // 2
    pairs = meta[0]

    def left_copy(k):
        return pltpu.make_async_copy(left_refs[k].at[0, pl.ds(0, left_rows), :], left_buf.at[k], left_sem.at[k])

    def tag_copy(k):
        tag_at = tag_refs[k].shape[1] - TAG_ROWS
        return pltpu.make_async_copy(tag_refs[k].at[0, pl.ds(tag_at, TAG_ROWS), :], left_tags.at[k], tag_sem.at[k])

    def right_tag_copy(k):
        return pltpu.make_async_copy(
            right_refs[k].at[0, pl.ds(right_rows, TAG_ROWS), :], left_tags.at[lefts + k], tag_sem.at[lefts + k]
        )

    def right_copy(k):
        return pltpu.make_async_copy(right_refs[k].at[0, pl.ds(0, right_rows), :], right_buf.at[k], right_sem.at[k])

    for k in range(lefts):
        tag_copy(k).start()
    for k in range(rights):
        right_tag_copy(k).start()
    def fetch(p):
        for k in range(rights):

            @pl.when((p < pairs) & (meta[1 + most + jnp.minimum(p, most - 1)] == k))
            def _():
                right_copy(k).start()

    left_copy(0).start()
    fetch(0)
    for k in range(1, lefts):
        left_copy(k).start()
    waiting[0] = 0

    row_ref[...] = jnp.zeros_like(row_ref)
    peak_ref[...] = peak_in[...]
    sum_ref[...] = sum_in[...]
    for k in range(lefts):
        tag_copy(k).wait()
    for k in range(rights):
        right_tag_copy(k).wait()
    left_lens = [jnp.clip(length_of(left_tags[k]) - offset, 0, left_rows) for k in range(lefts)]
    right_lens = [length_of(left_tags[lefts + k]) for k in range(rights)]

    def pick(values, index):
        found = values[0]
        for k in range(1, len(values)):
            found = jnp.where(index == k, values[k], found)
        return found

    def list_pair(p, n):
        left = meta[1 + p]
        right = meta[1 + most + p]
        left_len = pick(left_lens, left)
        right_len = pick(right_lens, right)
        down = lax.div(left_len + row_tile - 1, row_tile)
        across = lax.div(right_len + col_tile - 1, col_tile)

        def list_tile(t, n):
            i = lax.div(t, across)
            j = lax.rem(t, across)
            items[0, n] = left
            items[1, n] = right
            items[2, n] = i
            items[3, n] = j
            items[4, n] = left_len - i * row_tile
            items[5, n] = right_len - j * col_tile
            items[6, n] = (j == 0).astype(jnp.int32)
            items[7, n] = (j == across - 1).astype(jnp.int32)
            items[8, n] = p
            return n + 1

        return lax.fori_loop(0, down * across, list_tile, n)

    count = lax.fori_loop(0, pairs, list_pair, 0)
    for k in range(lefts):
        left_copy(k).wait()

    def at(index, size):
        return pl.ds(pl.multiple_of(index * size, size), size)

    def score(item, scores, rows_now, rows_before, cols_now):
        left = items[0, item]
        right = items[1, item]
        rows = at(items[2, item], row_tile)
        cols = at(items[3, item], col_tile)
        row_left = items[4, item]
        col_left = items[5, item]
        first = items[6, item] > 0
        col_bias = jnp.where(lax.broadcasted_iota(jnp.int32, (1, col_tile), 1) < col_left, 0.0, LOWEST)
        row_bias = jnp.where(lax.broadcasted_iota(jnp.int32, (row_tile, 1), 0) < row_left, 0.0, LOWEST)
        tile = lax.dot_general(
            left_buf[left, rows, :], right_buf[right, cols, :], (((1,), (1,)), ((), ())),
            preferred_element_type=jnp.float32,
        )
        tile = (tile * SCALE + col_bias) + row_bias
        scores[...] = tile
        row_peak = jnp.where(first, LOWEST, rows_before[...])
        for k in range(0, col_tile, LANES):
            row_peak = jnp.maximum(row_peak, tile[:, k : k + LANES])
        rows_now[...] = row_peak
        old = peak_ref[right, :, cols]
        new = jnp.maximum(old, jnp.max(tile, axis=0, keepdims=True))
        cols_now[0:1, :] = old
        cols_now[1:2, :] = new
        peak_ref[right, :, cols] = new

    def add(item, real, scores, rows_now, cols_now):
        right = items[1, item]
        cols = at(items[3, item], col_tile)
        first = items[6, item] > 0
        old = cols_now[0:1, :]
        new = cols_now[1:2, :]
        col_sum = jnp.zeros((8, col_tile), jnp.float32)
        for start in range(0, row_tile, SUM_STEP):
            rows = pl.ds(start, SUM_STEP)
            tile = scores[rows, :]
            row_peak = rows_now[rows, :]
            row_sum = total[rows, :] * jnp.exp2(base[rows, :] - row_peak)
            row_sum = jnp.where(first, 0.0, row_sum)
            for k in range(0, col_tile, LANES):
                row_sum = row_sum + jnp.exp2(tile[:, k : k + LANES] - row_peak)
            total[rows, :] = row_sum
            base[rows, :] = row_peak
            terms = jnp.exp2(tile - new)
            col_sum = col_sum + jnp.sum(terms.reshape(SUM_STEP // 8, 8, col_tile), axis=0)
        before = sum_ref[right, :, cols]
        after_sum = before * jnp.exp2(old - new) + jnp.sum(col_sum, axis=0, keepdims=True)
        sum_ref[right, :, cols] = jnp.where(real, after_sum, before)

    def finish(item, real):
        @pl.when(real & (items[7, item] > 0))
        def _():
            left = items[0, item]
            lane_peak = jnp.transpose(base[...])
            lane_sum = jnp.transpose(total[...])
            row_peak = jnp.max(lane_peak, axis=0, keepdims=True)
            row_sum = jnp.sum(lane_sum * jnp.exp2(lane_peak - row_peak), axis=0, keepdims=True)
            rows = at(items[2, item], row_tile)
            row_ref[left, :, rows] = row_ref[left, :, rows] + (row_peak + jnp.log2(row_sum)) * (1.0 / SCALE)

    def ready(item):
        pair = items[8, item]

        @pl.when(waiting[0] <= pair)
        def _():
            fetch(pair + 1)
            right = items[1, item]
            for k in range(rights):

                @pl.when(right == k)
                def _():
                    right_copy(k).wait()

            waiting[0] = pair + 1

    @pl.when(count == 0)
    def _():
        for k in range(rights):

            @pl.when(meta[1 + most] == k)
            def _():
                right_copy(k).wait()

    @pl.when(count > 0)
    def _():
        def two(t, carry):
            before = jnp.maximum(2 * t - 1, 0)
            even = jnp.minimum(2 * t, count - 1)
            odd = jnp.minimum(2 * t + 1, count - 1)
            ready(even)
            was_real = (t > 0) & (2 * t - 1 < count)
            add(jnp.minimum(before, count - 1), was_real, scores_odd, rows_odd, cols_odd)
            score(even, scores_even, rows_even, rows_odd, cols_even)
            finish(jnp.minimum(before, count - 1), was_real)
            ready(odd)
            is_real = 2 * t < count
            add(even, is_real, scores_even, rows_even, cols_even)
            score(odd, scores_odd, rows_odd, rows_even, cols_odd)
            finish(even, is_real)
            return carry

        lax.fori_loop(0, lax.div(count, 2) + 1, two, 0)


def match(meta, lefts, left_rows, rights, tags=None, offset=0, carried=None):
    tags = lefts if tags is None else tags
    count = len(rights)
    _, whole, width = rights[0].shape
    right_rows = whole - TAG_ROWS
    row_tile = min(ROW_TILE, left_rows)
    col_tile = min(COL_TILE, right_rows)
    most = (meta.shape[0] - 1) // 2
    tiles = most * (left_rows // row_tile) * (right_rows // col_tile)
    if carried is None:
        carried = (
            jnp.full((count, 1, right_rows), LOWEST, jnp.float32),
            jnp.zeros((count, 1, right_rows), jnp.float32),
        )
    anywhere = pl.BlockSpec(memory_space=pl.ANY)
    row_shape = (len(lefts), 1, left_rows)
    col_shape = (count, 1, right_rows)
    row_spec = pl.BlockSpec(row_shape, lambda p, m: (0, 0, 0))
    col_spec = pl.BlockSpec(col_shape, lambda p, m: (0, 0, 0))
    rows, peaks, sums = pl.pallas_call(
        functools.partial(match_kernel, lefts=len(lefts), rights=count, offset=offset),
        grid_spec=pltpu.PrefetchScalarGridSpec(
            num_scalar_prefetch=1,
            grid=(1,),
            in_specs=[anywhere] * (2 * len(lefts) + count) + [col_spec, col_spec],
            out_specs=[row_spec, col_spec, col_spec],
            scratch_shapes=[
                pltpu.VMEM((len(lefts), left_rows, width), jnp.bfloat16),
                pltpu.VMEM((len(lefts) + count, TAG_ROWS, width), jnp.bfloat16),
                pltpu.VMEM((count, right_rows, width), jnp.bfloat16),
                pltpu.VMEM((row_tile, col_tile), jnp.float32),
                pltpu.VMEM((row_tile, col_tile), jnp.float32),
                pltpu.VMEM((row_tile, LANES), jnp.float32),
                pltpu.VMEM((row_tile, LANES), jnp.float32),
                pltpu.VMEM((8, col_tile), jnp.float32),
                pltpu.VMEM((8, col_tile), jnp.float32),
                pltpu.VMEM((row_tile, LANES), jnp.float32),
                pltpu.VMEM((row_tile, LANES), jnp.float32),
                pltpu.SMEM((9, tiles), jnp.int32),
                pltpu.SMEM((1,), jnp.int32),
                pltpu.SemaphoreType.DMA((len(lefts),)),
                pltpu.SemaphoreType.DMA((len(lefts) + count,)),
                pltpu.SemaphoreType.DMA((count,)),
            ],
        ),
        out_shape=[
            jax.ShapeDtypeStruct(row_shape, jnp.float32),
            jax.ShapeDtypeStruct(col_shape, jnp.float32),
            jax.ShapeDtypeStruct(col_shape, jnp.float32),
        ],
        compiler_params=pltpu.CompilerParams(vmem_limit_bytes=32 << 20),
        cost_estimate=SMALL_COST,
    )(meta, *lefts, *tags, *rights, *carried)
    return rows[:, 0], (peaks, sums)


def matches_of(active, carried):
    peaks, sums = carried
    return jnp.where(active[:, None], (peaks + jnp.log2(sums))[:, 0] * (1.0 / SCALE), 0.0)


def shards(embeddings, lengths):
    answers, length, _ = embeddings.shape
    count = lax.axis_size("cand")
    is_even = lax.axis_index("cand") % 2 == 0

    first_to = [(i, (i - 2 if i % 2 == 0 else i + 2) % count) for i in range(count)]
    second_to = [(i, (i - 1 if i % 2 == 0 else i + 1) % count) for i in range(count)]
    mate_to = [(i, i ^ 1) for i in range(count)]

    def move(value, pairs):
        return lax.ppermute(value, "cand", pairs)

    def back(value, pairs):
        return lax.ppermute(value, "cand", [(b, a) for a, b in pairs])

    def by_role(even, odd):
        return jnp.where(is_even, jnp.array(even, jnp.int32), jnp.array(odd, jnp.int32))

    own_first = packet_of(embeddings, lengths, 0)
    first = move(own_first, first_to)
    own_second = packet_of(embeddings, lengths, 1, own_first)
    mate_first = move(own_first, mate_to)
    mate_second = move(own_second, mate_to)
    near = [own_first, own_second, mate_first, mate_second]
    every = jnp.arange(2 * answers)

    inner_meta = by_role([3, 0, 0, 0, 1, 2, 3], [3, 0, 2, 1, 1, 0, 3])
    inner_rows, inner_cols = match(inner_meta, [own_first, own_second, mate_second], length, near)

    half = length // 2
    lower = jnp.concatenate([own_second[:, :half], own_second[:, length:]], axis=1)
    lower = move(after(lower, inner_rows), second_to)
    upper = move(after(own_second[:, half:length], first), second_to)
    first_meta = by_role([4, 0, 0, 0, 0, 0, 1, 2, 3], [2, 0, 0, 0, 0, 0, 1, 1, 1])
    first_rows, first_cols = match(first_meta, [first], length, near)
    first_back = back(first_rows[0], first_to)
    second_meta = by_role([2, 0, 0, 0, 0, 2, 3, 3, 3], [4, 0, 0, 0, 0, 0, 1, 2, 3])
    lower_rows, second_cols = match(second_meta, [lower], half, near)
    upper_rows, second_cols = match(
        second_meta, [upper], length - half, near, tags=[lower], offset=half, carried=second_cols
    )
    second_back = back(jnp.concatenate([lower_rows[0], upper_rows[0]]), second_to)

    zero = jnp.zeros_like(inner_rows[0])
    totals = jnp.stack([inner_rows[0], inner_rows[1], zero, inner_rows[2]])
    totals = totals + matches_of(jnp.where(is_even, every > 0, every != 2), inner_cols)
    totals = totals + matches_of(is_even | (every < answers), first_cols)
    totals = totals + matches_of(~is_even | (every >= answers), second_cols)
    mate_back = move(totals[answers:], mate_to)

    consensus = totals[:answers] + mate_back + jnp.stack([first_back, second_back])
    inside = lax.broadcasted_iota(jnp.int32, (answers, length), 1) < lengths[:, None]
    return jnp.where(inside, consensus / (answers - 1 + 4 * answers), 0.0)


def solution(mesh):
    return jax.shard_map(
        shards,
        mesh=mesh,
        in_specs=(P(("group", "cand"), None, None), P(("group", "cand"))),
        out_specs=P(("group", "cand"), None),
        check_vma=False,
    )
```

time: 145 us -> 100 us (0.69); the launches traced: 145 us -> 98.3 us
  Pallas kernels: 0 us -> 41.9 us
  waiting for transfers between devices: 60.8 us -> 25.3 us
  matrix products: 28 us -> 0 us
  other arithmetic: 22.6 us -> 1.77 us
  starting transfers between devices: 33.4 us -> 24.5 us
  local copies, waits for them, and re-layouts: 0.01 us -> 4.55 us
    pallas_call x0 -> x8, Pallas kernels: none -> 41.9 us  [the longest x4 35.5 us: match(): pl.pallas_call(functools.partial(match_kernel, lefts=len(lefts), rights=c...]
    ppermute x6 -> x8, waiting for transfers between devices: 60.8 us -> 25.3 us  [the longest x6 19.6 us: move(): return lax.ppermute(value, 'cand', pairs)]
    dot_general x5 -> x0, matrix products: 28 us -> none  [soft_terms(): jnp.einsum('te,bse->bts', left, right, preferred_element_type=jnp.float32)]
    reduce_sum x9 -> x0, other arithmetic: 19.2 us -> none  [the longest x3 13.5 us: soft_terms(): jnp.sum(jnp.exp(row_scores - row_peak), axis=2)]
    ppermute x6 -> x8, starting transfers between devices: 33.4 us -> 24.5 us  [the longest x6 23.8 us: move(): return lax.ppermute(value, 'cand', pairs)]
    slice x0 -> x4, local copies, waits for them, and re-layouts: none -> 3.12 us  [the longest x1 2.37 us: shards(): own_second[:, :half]]
    convert_element_type x2 -> x0, other arithmetic: 2.54 us -> none  [the longest x1 2.46 us: unit_rows(): return (values * scale).astype(jnp.bfloat16)]
  transfers between devices with their start and end apart: 6 -> 8, of which waited for: 2 -> 2; matrix products, arithmetic and copies ran while one was open for 12% -> 5% of each run, Pallas kernels for 0% -> 36%
where the time goes in v4:
time: 100 us; the launch traced here: 98.3 us
  Pallas kernels  41.9 us (42%)
  waiting for transfers between devices  25.3 us (25%)
  starting transfers between devices  24.5 us (24%)
  local copies, waits for them, and re-layouts  4.55 us (5%)
  other arithmetic  1.77 us (2%)
    pallas_call x4, Pallas kernels, match(): pl.pallas_call(functools.partial(match_kernel, lefts=len(lefts), rights=c...  35.5 us
    ppermute x6, starting transfers between devices, move(): return lax.ppermute(value, 'cand', pairs)  23.8 us
    ppermute x6, waiting for transfers between devices, move(): return lax.ppermute(value, 'cand', pairs)  19.6 us
    pallas_call x2, Pallas kernels, packet_of(): pl.pallas_call(functools.partial(packet_kernel, slot=slot, rows=rows), gr...  6.42 us
    ppermute x2, waiting for transfers between devices, back(): return lax.ppermute(value, 'cand', [(b, a) for a, b in pairs])  5.71 us
    slice x1, local copies, waits for them, and re-layouts, shards(): own_second[:, :half]  2.37 us
  transfers between devices with their start and end apart: 8, of which 2 were waited for; matrix products, arithmetic and copies ran while one was open for 5% of the time, Pallas kernels for 36%

profile of v4, /device:TPU:0, one launch (start us, length us, event | category | flops | bytes accessed | tf_op | source)
XLA Modules:
  0.0 98.3 jit_solution(10024763377862254931)
XLA Ops:
  0.0 3.1 %shard_map.82.refs_0_.refs_3_.refs_6_.refs_2_ = bf16[1,1040,768]{2,1,0:T(8,128)(2,1)} custom-call(s32[2]{0:T(128)} %lengths.3, bf16[2,1024,768]{2,1,0:T(8,128)(2,1)} %values_ref.3), custom_call_target="tpu_custom_call" | custom-call | flops 1 | bytes 1 | tf_op jit(solution)/shard_map/pallas_call | solution.py:71
  3.2 0.0 copy-start
  3.2 3.3 %shard_map.83.refs_1_.refs_4_.refs_7_.refs_3_ = bf16[1,1040,768]{2,1,0:T(8,128)(2,1)} custom-call(s32[2]{0:T(128)} %lengths.3, bf16[2,1024,768]{2,1,0:T(8,128)(2,1)} %values_ref.3, bf16[1,1040,768]{2,1,0:T(8,128)(2,1)} %shard_map.82.refs_0_.refs_3_.refs_6_.refs_2_), custom_call_target="tpu_custom_call" | custom-call | flops 1 | bytes 1 | tf_op jit(solution)/shard_map/pallas_call | solution.py:71
  6.4 0.5 collective-permute-start
  7.0 0.0 copy-done
  7.0 0.1 collective-permute-start.1
  7.1 6.0 %collective-permute-start.2 = (bf16[1,1040,768]{2,1,0:T(8,128)(2,1)S(1)}, bf16[1,1040,768]{2,1,0:T(8,128)(2,1)}, u32[]{:S(2)}, u32[]{:S(2)}) collective-permute-start(bf16[1,1040,768]{2,1,0:T(8,128)(2,1)S(1)} %copy-done), channel_id=1, source_target_pairs={{0,14},{1,3},{2,0},{3,5},{4,2},{5,7},{6,4},{7,9},{8,6},{9,11},{10,... | collective-permute-start | bytes 4792328 | tf_op jit(solution)/shard_map/ppermute | solution.py:374
  13.0 0.7 slice.46
  13.8 2.4 %fusion.8 = (bf16[1,512,768]{2,1,0:T(8,128)(2,1)S(1)}, bf16[1,512,768]{2,1,0:T(8,128)(2,1)}) fusion(bf16[1,1040,768]{2,1,0:T(8,128)(2,1)} %shard_map.83.refs_1_.refs_4_.refs_7_.refs_3_), kind=kLoop, calls=%fused_computation.31 | loop fusion | bytes 3145728 | tf_op jit(solution)/shard_map/slice | solution.py:394
  16.1 0.0 copy-start.6
  16.1 0.0 copy-start.7
  16.1 0.0 copy-start.1
  16.1 1.0 pad_maximum_fusion.refs_0_
  17.1 0.0 copy-done.6
  17.1 0.0 copy-done.7
  17.1 0.0 collective-permute-done.refs_2_.refs_5_.refs_9_
  17.1 0.0 collective-permute-done.1.refs_8_.refs_4_
  17.2 0.7 copy-done.1
  17.9 8.8 %shard_map.84 = (f32[3,1,1024]{2,1,0:T(1,128)S(1)}, f32[4,1,1024]{2,1,0:T(1,128)S(1)}, f32[4,1,1024]{2,1,0:T(1,128)S(1)}) custom-call(s32[7]{0:T(128)S(1)} %broadcast_select_fusion.2.meta, bf16[1,1040,768]{2,1,0:T(8,128)(2,1)S(1)} %copy-done, bf16[1,1040,768]{2,1,0:T(8,128)(2,1)S(1)} %copy-done.1, ...), custom_call_target="tpu_custom_call" | custom-call | flops 1 | bytes 1 | tf_op jit(solution)/shard_map/pallas_call | solution.py:322
  26.7 0.6 copy.41
  27.3 0.0 copy-start.3
  27.3 0.0 copy-start.4
  27.3 0.0 copy-start.5
  27.3 7.6 %collective-permute-start.4 = (bf16[1,528,768]{2,1,0:T(8,128)(2,1)}, bf16[1,528,768]{2,1,0:T(8,128)(2,1)}, u32[]{:S(2)}, u32[]{:S(2)}) collective-permute-start(bf16[1,528,768]{2,1,0:T(8,128)(2,1)} %shard_map.87), channel_id=1, source_target_pairs={{0,15},{1,2},{2,1},{3,4},{4,3},{5,6},{6,5},{7,8},{8,7},{9,10},{10,... | collective-permute-start | bytes 2433032 | tf_op jit(solution)/shard_map/ppermute | solution.py:374
  35.0 19.6 %collective-permute-done.2.refs_0_.refs_1_ = bf16[1,1040,768]{2,1,0:T(8,128)(2,1)} collective-permute-done((bf16[1,1040,768]{2,1,0:T(8,128)(2,1)S(1)}, bf16[1,1040,768]{2,1,0:T(8,128)(2,1)}, u32[]{:S(2)}, u32[]{:S(2)}) %collective-permute-start.2) | collective-permute-done | bytes 1597472 | tf_op jit(solution)/shard_map/ppermute | solution.py:374
  54.6 3.6 %collective-permute-start.3 = (bf16[1,512,768]{2,1,0:T(8,128)(2,1)}, bf16[1,512,768]{2,1,0:T(8,128)(2,1)}, u32[]{:S(2)}, u32[]{:S(2)}) collective-permute-start(bf16[1,512,768]{2,1,0:T(8,128)(2,1)} %shard_map.86), channel_id=1, source_target_pairs={{0,15},{1,2},{2,1},{3,4},{4,3},{5,6},{6,5},{7,8},{8,7},{9,10},{10,... | collective-permute-start | bytes 2359304 | tf_op jit(solution)/shard_map/ppermute | solution.py:374
  58.2 0.1 pad.8.clone
  58.3 0.0 copy-done.3
  58.3 0.0 copy-done.4
  58.3 0.0 copy-done.5
  58.3 10.6 %shard_map.85 = (f32[1,1,1024]{2,1,0:T(1,128)S(1)}, f32[4,1,1024]{2,1,0:T(1,128)S(1)}, f32[4,1,1024]{2,1,0:T(1,128)S(1)}) custom-call(s32[9]{0:T(128)S(1)} %get-tuple-element.34.meta, bf16[1,1040,768]{2,1,0:T(8,128)(2,1)} %collective-permute-done.2.refs_0_.refs_1_, bf16[1,1040,768]{2,1,0:T(8,128)(2,1)} %collective-permute-done.2.refs_0_.refs_1_, ...), custom_call_target="tpu_custom_call" | custom-call | flops 1 | bytes 1 | tf_op jit(solution)/shard_map/pallas_call | solution.py:322
  68.9 0.7 collective-permute-start.6
  69.6 0.0 collective-permute-done.4.refs_0_.refs_1_
  69.6 8.0 %shard_map.88 = (f32[1,1,512]{2,1,0:T(1,128)S(1)}, f32[4,1,1024]{2,1,0:T(1,128)S(1)}, f32[4,1,1024]{2,1,0:T(1,128)S(1)}) custom-call(s32[9]{0:T(128)S(1)} %get-tuple-element.35.meta, bf16[1,528,768]{2,1,0:T(8,128)(2,1)} %collective-permute-done.4.refs_0_.refs_1_, bf16[1,528,768]{2,1,0:T(8,128)(2,1)} %collective-permute-done.4.refs_0_.refs_1_, ...), custom_call_target="tpu_custom_call" | custom-call | flops 1 | bytes 1 | tf_op jit(solution)/shard_map/pallas_call | solution.py:322
  77.6 0.0 collective-permute-done.3.refs_0_
  77.6 0.0 copy-start.2
  77.6 8.0 %shard_map.89 = (f32[1,1,512]{2,1,0:T(1,128)S(1)}, f32[4,1,1024]{2,1,0:T(1,128)S(1)}, f32[4,1,1024]{2,1,0:T(1,128)S(1)}) custom-call(s32[9]{0:T(128)S(1)} %get-tuple-element.35.meta, bf16[1,512,768]{2,1,0:T(8,128)(2,1)} %collective-permute-done.3.refs_0_, bf16[1,528,768]{2,1,0:T(8,128)(2,1)} %collective-permute-done.4.refs_0_.refs_1_, ...), custom_call_target="tpu_custom_call" | custom-call | flops 1 | bytes 1 | tf_op jit(solution)/shard_map/pallas_call | solution.py:322
  85.8 0.1 fusion.1
  85.9 6.0 %collective-permute-start.5 = (f32[2,1024]{1,0:T(2,128)S(1)}, f32[2,1024]{1,0:T(2,128)S(1)}, u32[]{:S(2)}, u32[]{:S(2)}) collective-permute-start(f32[2,1024]{1,0:T(2,128)S(1)} %slice.48), channel_id=1, source_target_pairs={{0,1},{1,0},{2,3},{3,2},{4,5},{5,4},{6,7},{7,6},{8,9},{9,8},{10,11... | collective-permute-start | bytes 24584 | tf_op jit(solution)/shard_map/ppermute | solution.py:374
  91.9 0.0 collective-permute-start.7
  91.9 0.0 collective-permute-done.6
  91.9 5.7 %collective-permute-done.7 = f32[1024]{0:T(1024)S(1)} collective-permute-done((f32[1024]{0:T(1024)S(1)}, f32[1024]{0:T(1024)S(1)}, u32[]{:S(2)}, u32[]{:S(2)}) %collective-permute-start.7) | collective-permute-done | bytes 4128 | tf_op jit(solution)/shard_map/ppermute | solution.py:377
  97.6 0.0 collective-permute-done.5
  97.6 0.0 copy-done.2
  97.6 0.7 compare_select_fusion
  (12 shorter events, 0.1 us)
Async XLA Ops:
  3.2 3.8 %copy-start = (bf16[1,1040,768]{2,1,0:T(8,128)(2,1)S(1)}, bf16[1,1040,768]{2,1,0:T(8,128)(2,1)}, u32[]{:S(2)}) copy-start(bf16[1,1040,768]{2,1,0:T(8,128)(2,1)} %shard_map.82.refs_0_.refs_3_.refs_6_.refs_2_) | copy-start | bytes 4792324
  6.4 10.7 %collective-permute-start = (bf16[1,1040,768]{2,1,0:T(8,128)(2,1)}, bf16[1,1040,768]{2,1,0:T(8,128)(2,1)}, u32[]{:S(2)}, u32[]{:S(2)}) collective-permute-start(bf16[1,1040,768]{2,1,0:T(8,128)(2,1)} %shard_map.83.refs_1_.refs_4_.refs_7_.refs_3_), channel_id=1, source_target_pairs={{0,1},{1,0},{2,3},{3,2},{4,5},{5,4},{6,7},{7,6},{8,9},{9,8},{10,11... | collective-permute-start | bytes 4792328 | tf_op jit(solution)/shard_map/ppermute | solution.py:374
  7.0 10.2 %collective-permute-start.1 = (bf16[1,1040,768]{2,1,0:T(8,128)(2,1)S(1)}, bf16[1,1040,768]{2,1,0:T(8,128)(2,1)}, u32[]{:S(2)}, u32[]{:S(2)}) collective-permute-start(bf16[1,1040,768]{2,1,0:T(8,128)(2,1)S(1)} %copy-done), channel_id=1, source_target_pairs={{0,1},{1,0},{2,3},{3,2},{4,5},{5,4},{6,7},{7,6},{8,9},{9,8},{10,11... | collective-permute-start | bytes 4792328 | tf_op jit(solution)/shard_map/ppermute | solution.py:374
  7.1 47.5 %collective-permute-start.2 = (bf16[1,1040,768]{2,1,0:T(8,128)(2,1)S(1)}, bf16[1,1040,768]{2,1,0:T(8,128)(2,1)}, u32[]{:S(2)}, u32[]{:S(2)}) collective-permute-start(bf16[1,1040,768]{2,1,0:T(8,128)(2,1)S(1)} %copy-done), channel_id=1, source_target_pairs={{0,14},{1,3},{2,0},{3,5},{4,2},{5,7},{6,4},{7,9},{8,6},{9,11},{10,... | collective-permute-start | bytes 4792328 | tf_op jit(solution)/shard_map/ppermute | solution.py:374
  16.1 1.0 copy-start.6
  16.1 1.0 copy-start.7
  16.1 1.7 %copy-start.1 = (bf16[1,1040,768]{2,1,0:T(8,128)(2,1)S(1)}, bf16[1,1040,768]{2,1,0:T(8,128)(2,1)}, u32[]{:S(2)}) copy-start(bf16[1,1040,768]{2,1,0:T(8,128)(2,1)} %shard_map.83.refs_1_.refs_4_.refs_7_.refs_3_) | copy-start | bytes 4792324
  27.3 30.9 %copy-start.3 = (s32[9]{0:T(128)S(1)}, s32[9]{0:T(128)}, u32[]{:S(2)}) copy-start(s32[9]{0:T(128)} %constant.47.clone) | copy-start | bytes 112
  27.3 30.9 %copy-start.4 = (s32[9]{0:T(128)S(1)}, s32[9]{0:T(128)}, u32[]{:S(2)}) copy-start(s32[9]{0:T(128)} %constant.46.clone) | copy-start | bytes 112
  27.3 30.9 %copy-start.5 = (s32[9]{0:T(128)S(1)}, s32[9]{0:T(128)}, u32[]{:S(2)}) copy-start(s32[9]{0:T(128)} %constant.45.clone) | copy-start | bytes 112
  27.3 42.2 %collective-permute-start.4 = (bf16[1,528,768]{2,1,0:T(8,128)(2,1)}, bf16[1,528,768]{2,1,0:T(8,128)(2,1)}, u32[]{:S(2)}, u32[]{:S(2)}) collective-permute-start(bf16[1,528,768]{2,1,0:T(8,128)(2,1)} %shard_map.87), channel_id=1, source_target_pairs={{0,15},{1,2},{2,1},{3,4},{4,3},{5,6},{6,5},{7,8},{8,7},{9,10},{10,... | collective-permute-start | bytes 2433032 | tf_op jit(solution)/shard_map/ppermute | solution.py:374
  54.6 23.1 %collective-permute-start.3 = (bf16[1,512,768]{2,1,0:T(8,128)(2,1)}, bf16[1,512,768]{2,1,0:T(8,128)(2,1)}, u32[]{:S(2)}, u32[]{:S(2)}) collective-permute-start(bf16[1,512,768]{2,1,0:T(8,128)(2,1)} %shard_map.86), channel_id=1, source_target_pairs={{0,15},{1,2},{2,1},{3,4},{4,3},{5,6},{6,5},{7,8},{8,7},{9,10},{10,... | collective-permute-start | bytes 2359304 | tf_op jit(solution)/shard_map/ppermute | solution.py:374
  68.9 23.0 %collective-permute-start.6 = (f32[1024]{0:T(1024)S(1)}, f32[1024]{0:T(1024)S(1)}, u32[]{:S(2)}, u32[]{:S(2)}) collective-permute-start(f32[1024]{0:T(1024)S(1)} %bitcast.29), channel_id=1, source_target_pairs={{14,0},{3,1},{0,2},{5,3},{2,4},{7,5},{4,6},{9,7},{6,8},{11,9},{8,1... | collective-permute-start | bytes 12296 | tf_op jit(solution)/shard_map/ppermute | solution.py:377
  77.6 20.0 %copy-start.2 = (s32[2]{0:T(128)S(1)}, s32[2]{0:T(128)}, u32[]{:S(2)}) copy-start(s32[2]{0:T(128)} %lengths.3) | copy-start | bytes 28
  85.9 11.8 %collective-permute-start.5 = (f32[2,1024]{1,0:T(2,128)S(1)}, f32[2,1024]{1,0:T(2,128)S(1)}, u32[]{:S(2)}, u32[]{:S(2)}) collective-permute-start(f32[2,1024]{1,0:T(2,128)S(1)} %slice.48), channel_id=1, source_target_pairs={{0,1},{1,0},{2,3},{3,2},{4,5},{5,4},{6,7},{7,6},{8,9},{9,8},{10,11... | collective-permute-start | bytes 24584 | tf_op jit(solution)/shard_map/ppermute | solution.py:374
  91.9 5.7 %collective-permute-start.7 = (f32[1024]{0:T(1024)S(1)}, f32[1024]{0:T(1024)S(1)}, u32[]{:S(2)}, u32[]{:S(2)}) collective-permute-start(f32[1024]{0:T(1024)S(1)} %pad_maximum_fusion.1), channel_id=1, source_target_pairs={{15,0},{2,1},{1,2},{4,3},{3,4},{6,5},{5,6},{8,7},{7,8},{10,9},{9,1... | collective-permute-start | bytes 12296 | tf_op jit(solution)/shard_map/ppermute | solution.py:377

commit v5 on v4

v5 whole, which is shorter than its diff:
```python
import functools

import jax
import jax.numpy as jnp
from jax import lax
from jax.experimental import pallas as pl
from jax.experimental.pallas import tpu as pltpu
from jax.sharding import PartitionSpec as P

SCALE = 256.0 * 1.4426950408889634
LOWEST = -1e30
LANES = 128
TAG_ROWS = 16
TAG_BASE = 64
ROW_TILE = 512
COL_TILE = 256
SUM_STEP = 64
CHUNKS = 4
SMALL_COST = pl.CostEstimate(flops=1, bytes_accessed=1, transcendentals=0)


def unit_rows(embeddings):
    values = embeddings.astype(jnp.float32)
    scale = lax.rsqrt(jnp.sum(values * values, axis=-1, keepdims=True) + 1e-06)
    return (values * scale).astype(jnp.bfloat16)


def length_of(tag):
    values = tag.astype(jnp.float32)
    upper = lax.broadcasted_iota(jnp.int32, values.shape, 0) < TAG_ROWS // 2
    high = jnp.max(jnp.where(upper, values, 0.0)).astype(jnp.int32)
    low = jnp.max(jnp.where(upper, 0.0, values)).astype(jnp.int32)
    return high * TAG_BASE + low


def packet_kernel(lengths, values_ref, *refs, slot, rows, outs):
    packet_refs = refs[-outs - 4 : -4]
    values_buf, packet_buf, in_sem, out_sem = refs[-4:]
    chunk = rows // CHUNKS
    tags = pl.ds(rows, TAG_ROWS)
    parts = [packet_ref.shape[1] - TAG_ROWS for packet_ref in packet_refs]
    starts = [sum(parts[:k]) % rows for k in range(outs)]

    def copy_in(k):
        at = pl.ds(k * chunk, chunk)
        return pltpu.make_async_copy(values_ref.at[slot, at, :], values_buf.at[at, :], in_sem.at[k])

    def tag_out(k):
        to = packet_refs[k].at[0, pl.ds(parts[k], TAG_ROWS), :]
        return pltpu.make_async_copy(packet_buf.at[tags, :], to, out_sem.at[k, CHUNKS])

    def copies_out(c):
        copies = []
        for k in range(outs):
            offset = c * chunk - starts[k]
            if 0 <= offset < parts[k]:
                to = packet_refs[k].at[0, pl.ds(offset, chunk), :]
                copies.append(pltpu.make_async_copy(packet_buf.at[pl.ds(c * chunk, chunk), :], to, out_sem.at[k, c]))
        return copies

    for c in range(CHUNKS):
        copy_in(c).start()
    shape = (TAG_ROWS, values_buf.shape[1])
    upper = lax.broadcasted_iota(jnp.int32, shape, 0) < TAG_ROWS // 2
    tag = jnp.where(upper, lengths[slot] // TAG_BASE, lengths[slot] % TAG_BASE)
    packet_buf[tags, :] = tag.astype(jnp.float32).astype(jnp.bfloat16)
    for k in range(outs):
        tag_out(k).start()
    for c in range(CHUNKS):
        copy_in(c).wait()
        at = pl.ds(c * chunk, chunk)
        packet_buf[at, :] = unit_rows(values_buf[at, :])
        for copy in copies_out(c):
            copy.start()
    for c in range(CHUNKS):
        for copy in copies_out(c):
            copy.wait()
    for k in range(outs):
        tag_out(k).wait()


def packets_of(embeddings, lengths, slot, parts, *earlier):
    _, rows, width = embeddings.shape
    anywhere = pl.BlockSpec(memory_space=pl.ANY)
    return pl.pallas_call(
        functools.partial(packet_kernel, slot=slot, rows=rows, outs=len(parts)),
        grid_spec=pltpu.PrefetchScalarGridSpec(
            num_scalar_prefetch=1,
            grid=(1,),
            in_specs=[anywhere] * (1 + len(earlier)),
            out_specs=[anywhere] * len(parts),
            scratch_shapes=[
                pltpu.VMEM((rows, width), jnp.bfloat16),
                pltpu.VMEM((rows + TAG_ROWS, width), jnp.bfloat16),
                pltpu.SemaphoreType.DMA((CHUNKS,)),
                pltpu.SemaphoreType.DMA((len(parts), CHUNKS + 1)),
            ],
        ),
        out_shape=[jax.ShapeDtypeStruct((1, part + TAG_ROWS, width), jnp.bfloat16) for part in parts],
        compiler_params=pltpu.CompilerParams(vmem_limit_bytes=60 << 20),
        cost_estimate=SMALL_COST,
    )(lengths, embeddings, *earlier)


def pass_kernel(*refs):
    del refs


def after(value, *earlier):
    spec = pl.BlockSpec(memory_space=pl.ANY)
    return pl.pallas_call(
        pass_kernel,
        in_specs=[spec] * (1 + len(earlier)),
        out_specs=spec,
        out_shape=jax.ShapeDtypeStruct(value.shape, value.dtype),
        input_output_aliases={0: 0},
        cost_estimate=SMALL_COST,
    )(value, *earlier)


def match_kernel(meta, *refs, lefts, rights, offset):
    refs = list(refs)
    left_refs = [[refs.pop(0) for _ in range(parts)] for parts in lefts]
    right_refs = [[refs.pop(0) for _ in range(parts)] for parts in rights]
    (peak_in, sum_in, row_ref, peak_ref, sum_ref, left_buf, tags, right_buf, scores, peak, total, items, waiting,
     left_sem, tag_sem, right_sem) = refs
    lefts = len(lefts)
    rights = len(rights)
    row_tile = scores.shape[0]
    left_rows = left_buf.shape[1]
    right_rows = peak_ref.shape[2]
    col_tile = min(COL_TILE, right_rows)
    most = (meta.shape[0] - 1) // 2
    pairs = meta[0]

    def copies(parts, buf, sems):
        made = []
        start = 0
        for n, part in enumerate(parts):
            rows = part.shape[1] - TAG_ROWS
            to = buf.at[pl.ds(start, rows), :]
            made.append(pltpu.make_async_copy(part.at[0, pl.ds(0, rows), :], to, sems.at[n]))
            start += rows
        return made

    def left_copies(k):
        return copies(left_refs[k], left_buf.at[k], left_sem.at[k])

    def right_copies(k):
        return copies(right_refs[k], right_buf.at[k], right_sem.at[k])

    def tag_copy(k):
        part = (left_refs + right_refs)[k][0]
        tag_at = pl.ds(part.shape[1] - TAG_ROWS, TAG_ROWS)
        return pltpu.make_async_copy(part.at[0, tag_at, :], tags.at[k], tag_sem.at[k])

    def start(made):
        for copy in made:
            copy.start()

    def wait(made):
        for copy in made:
            copy.wait()

    for k in range(lefts + rights):
        tag_copy(k).start()

    def fetch(p):
        for k in range(rights):

            @pl.when((p < pairs) & (meta[1 + most + jnp.minimum(p, most - 1)] == k))
            def _():
                start(right_copies(k))

    start(left_copies(0))
    fetch(0)
    for k in range(1, lefts):
        start(left_copies(k))
    waiting[0] = 0

    row_ref[...] = jnp.zeros_like(row_ref)
    peak_ref[...] = peak_in[...]
    sum_ref[...] = sum_in[...]
    for k in range(lefts + rights):
        tag_copy(k).wait()
    left_lens = [jnp.clip(length_of(tags[k]) - offset, 0, left_rows) for k in range(lefts)]
    right_lens = [length_of(tags[lefts + k]) for k in range(rights)]

    def pick(values, index):
        found = values[0]
        for k in range(1, len(values)):
            found = jnp.where(index == k, values[k], found)
        return found

    def list_pair(p, n):
        left = meta[1 + p]
        right = meta[1 + most + p]
        left_len = pick(left_lens, left)
        right_len = pick(right_lens, right)

        def list_block(i, n):
            items[0, n] = left
            items[1, n] = right
            items[2, n] = i
            items[3, n] = left_len - i * row_tile
            items[4, n] = right_len
            items[5, n] = p
            return n + 1

        return lax.fori_loop(0, lax.div(left_len + row_tile - 1, row_tile), list_block, n)

    count = lax.fori_loop(0, pairs, list_pair, 0)
    for k in range(lefts):
        wait(left_copies(k))

    def at(index, size):
        return pl.ds(pl.multiple_of(index * size, size), size)

    def block(item, width):
        left = items[0, item]
        right = items[1, item]
        rows = at(items[2, item], row_tile)
        col_at = lax.broadcasted_iota(jnp.int32, (1, width), 1)
        col_bias = jnp.where(col_at < items[4, item], 0.0, LOWEST)
        row_at = lax.broadcasted_iota(jnp.int32, (row_tile, 1), 0)
        row_bias = jnp.where(row_at < items[3, item], 0.0, LOWEST)
        tile = lax.dot_general(
            left_buf[left, rows, :], right_buf[right, 0:width, :], (((1,), (1,)), ((), ())),
            preferred_element_type=jnp.float32,
        )
        tile = (tile * SCALE + col_bias) + row_bias
        scores[:, 0:width] = tile
        row_peak = tile[:, 0:LANES]
        for k in range(LANES, width, LANES):
            row_peak = jnp.maximum(row_peak, tile[:, k : k + LANES])
        peak[...] = row_peak
        old = peak_ref[right, :, 0:width]
        new = jnp.maximum(old, jnp.max(tile, axis=0, keepdims=True))
        peak_ref[right, :, 0:width] = new
        col_sum = jnp.zeros((8, width), jnp.float32)
        for start in range(0, row_tile, SUM_STEP):
            part = scores[start : start + SUM_STEP, 0:width]
            part_peak = peak[start : start + SUM_STEP, :]
            row_sum = jnp.exp2(part[:, 0:LANES] - part_peak)
            for k in range(LANES, width, LANES):
                row_sum = row_sum + jnp.exp2(part[:, k : k + LANES] - part_peak)
            total[start : start + SUM_STEP, :] = row_sum
            terms = jnp.exp2(part - new)
            col_sum = col_sum + jnp.sum(terms.reshape(SUM_STEP // 8, 8, width), axis=0)
        before = sum_ref[right, :, 0:width]
        sum_ref[right, :, 0:width] = before * jnp.exp2(old - new) + jnp.sum(col_sum, axis=0, keepdims=True)
        lane_peak = jnp.transpose(peak[...])
        lane_sum = jnp.transpose(total[...])
        top = jnp.max(lane_peak, axis=0, keepdims=True)
        all_sum = jnp.sum(lane_sum * jnp.exp2(lane_peak - top), axis=0, keepdims=True)
        row_ref[left, :, rows] = row_ref[left, :, rows] + (top + jnp.log2(all_sum)) * (1.0 / SCALE)

    def ready(item):
        pair = items[5, item]

        @pl.when(waiting[0] <= pair)
        def _():
            fetch(pair + 1)
            right = items[1, item]
            for k in range(rights):

                @pl.when(right == k)
                def _():
                    wait(right_copies(k))

            waiting[0] = pair + 1

    @pl.when(count == 0)
    def _():
        for k in range(rights):

            @pl.when(meta[1 + most] == k)
            def _():
                wait(right_copies(k))

    def one(item, carry):
        ready(item)
        tiles = lax.div(items[4, item] + col_tile - 1, col_tile)
        for n in range(1, right_rows // col_tile + 1):

            @pl.when(tiles == n)
            def _():
                block(item, n * col_tile)

        return carry

    lax.fori_loop(0, count, one, 0)


def match(meta, lefts, rights, offset=0, carried=None):
    count = len(rights)
    width = rights[0][0].shape[2]
    left_rows = sum(part.shape[1] - TAG_ROWS for part in lefts[0])
    right_rows = sum(part.shape[1] - TAG_ROWS for part in rights[0])
    row_tile = min(ROW_TILE, left_rows)
    most = (meta.shape[0] - 1) // 2
    blocks = most * (left_rows // row_tile)
    left_parts = [len(parts) for parts in lefts]
    right_parts = [len(parts) for parts in rights]
    packets = [part for parts in lefts + rights for part in parts]
    if carried is None:
        carried = (
            jnp.full((count, 1, right_rows), LOWEST, jnp.float32),
            jnp.zeros((count, 1, right_rows), jnp.float32),
        )
    anywhere = pl.BlockSpec(memory_space=pl.ANY)
    row_shape = (len(lefts), 1, left_rows)
    col_shape = (count, 1, right_rows)
    row_spec = pl.BlockSpec(row_shape, lambda p, m: (0, 0, 0))
    col_spec = pl.BlockSpec(col_shape, lambda p, m: (0, 0, 0))
    rows, peaks, sums = pl.pallas_call(
        functools.partial(match_kernel, lefts=left_parts, rights=right_parts, offset=offset),
        grid_spec=pltpu.PrefetchScalarGridSpec(
            num_scalar_prefetch=1,
            grid=(1,),
            in_specs=[anywhere] * len(packets) + [col_spec, col_spec],
            out_specs=[row_spec, col_spec, col_spec],
            scratch_shapes=[
                pltpu.VMEM((len(lefts), left_rows, width), jnp.bfloat16),
                pltpu.VMEM((len(lefts) + count, TAG_ROWS, width), jnp.bfloat16),
                pltpu.VMEM((count, right_rows, width), jnp.bfloat16),
                pltpu.VMEM((row_tile, right_rows), jnp.float32),
                pltpu.VMEM((row_tile, LANES), jnp.float32),
                pltpu.VMEM((row_tile, LANES), jnp.float32),
                pltpu.SMEM((6, blocks), jnp.int32),
                pltpu.SMEM((1,), jnp.int32),
                pltpu.SemaphoreType.DMA((len(lefts), max(left_parts))),
                pltpu.SemaphoreType.DMA((len(lefts) + count,)),
                pltpu.SemaphoreType.DMA((count, max(right_parts))),
            ],
        ),
        out_shape=[
            jax.ShapeDtypeStruct(row_shape, jnp.float32),
            jax.ShapeDtypeStruct(col_shape, jnp.float32),
            jax.ShapeDtypeStruct(col_shape, jnp.float32),
        ],
        compiler_params=pltpu.CompilerParams(vmem_limit_bytes=32 << 20),
        cost_estimate=SMALL_COST,
    )(meta, *packets, *carried)
    return rows[:, 0], (peaks, sums)


def matches_of(active, carried):
    peaks, sums = carried
    return jnp.where(active[:, None], (peaks + jnp.log2(sums))[:, 0] * (1.0 / SCALE), 0.0)


def shards(embeddings, lengths):
    answers, length, _ = embeddings.shape
    count = lax.axis_size("cand")
    is_even = lax.axis_index("cand") % 2 == 0

    first_to = [(i, (i - 2 if i % 2 == 0 else i + 2) % count) for i in range(count)]
    second_to = [(i, (i - 1 if i % 2 == 0 else i + 1) % count) for i in range(count)]
    mate_to = [(i, i ^ 1) for i in range(count)]

    def move(value, pairs):
        return lax.ppermute(value, "cand", pairs)

    def back(value, pairs):
        return lax.ppermute(value, "cand", [(b, a) for a, b in pairs])

    def by_role(even, odd):
        return jnp.where(is_even, jnp.array(even, jnp.int32), jnp.array(odd, jnp.int32))

    half = length // 2
    halves = [half, length - half]
    whole_first, *own_first = packets_of(embeddings, lengths, 0, [length] + halves)
    first = move(whole_first, first_to)
    own_second = packets_of(embeddings, lengths, 1, halves, whole_first)
    mate_first = [move(part, mate_to) for part in own_first]
    mate_second = [move(part, mate_to) for part in own_second]
    near = [own_first, own_second, mate_first, mate_second]
    every = jnp.arange(2 * answers)

    inner_meta = by_role([3, 0, 0, 0, 1, 2, 3], [3, 0, 2, 1, 1, 0, 3])
    inner_rows, inner_cols = match(inner_meta, [own_first, own_second, mate_second], near)

    lower = move(after(own_second[0], inner_rows), second_to)
    upper = move(after(own_second[1], first), second_to)
    first_meta = by_role([4, 0, 0, 0, 0, 0, 1, 2, 3], [2, 0, 0, 0, 0, 0, 1, 1, 1])
    first_rows, first_cols = match(first_meta, [[first]], near)
    first_back = back(first_rows[0], first_to)
    second_meta = by_role([2, 0, 0, 0, 0, 2, 3, 3, 3], [4, 0, 0, 0, 0, 0, 1, 2, 3])
    lower_rows, second_cols = match(second_meta, [[lower]], near)
    upper_rows, second_cols = match(second_meta, [[upper]], near, half, second_cols)
    second_back = back(jnp.concatenate([lower_rows[0], upper_rows[0]]), second_to)

    zero = jnp.zeros_like(inner_rows[0])
    totals = jnp.stack([inner_rows[0], inner_rows[1], zero, inner_rows[2]])
    totals = totals + matches_of(jnp.where(is_even, every > 0, every != 2), inner_cols)
    totals = totals + matches_of(is_even | (every < answers), first_cols)
    totals = totals + matches_of(~is_even | (every >= answers), second_cols)
    mate_back = move(totals[answers:], mate_to)

    consensus = totals[:answers] + mate_back + jnp.stack([first_back, second_back])
    inside = lax.broadcasted_iota(jnp.int32, (answers, length), 1) < lengths[:, None]
    return jnp.where(inside, consensus / (answers - 1 + 4 * answers), 0.0)


def solution(mesh):
    return jax.shard_map(
        shards,
        mesh=mesh,
        in_specs=(P(("group", "cand"), None, None), P(("group", "cand"))),
        out_specs=P(("group", "cand"), None),
        check_vma=False,
    )
```

time: 100 us -> 92.3 us (0.923); the launches traced: 98.3 us -> 92.5 us
  starting transfers between devices: 24.5 us -> 16.1 us
  Pallas kernels: 41.9 us -> 45.4 us
    ppermute x6 -> x8, starting transfers between devices: 23.8 us -> 15 us  [move(): return lax.ppermute(value, 'cand', pairs)]
    pallas_call x6, Pallas kernels: 41.9 us -> 45.4 us  [the longest x4 38.5 us: match(): pl.pallas_call(functools.partial(match_kernel, lefts=left_parts, rights=r...]
    slice x2 -> x0, local copies, waits for them, and re-layouts: 3.11 us -> none  [the longest x1 2.37 us: shards(): own_second[:, :half]]
    unnamed x17 -> x23, local copies, waits for them, and re-layouts: 1.34 us -> 3.86 us
    ppermute x6 -> x8, waiting for transfers between devices: 19.6 us -> 21.2 us  [move(): return lax.ppermute(value, 'cand', pairs)]
    ppermute x2, waiting for transfers between devices: 5.71 us -> 4.7 us  [back(): return lax.ppermute(value, 'cand', [(b, a) for a, b in pairs])]
  transfers between devices with their start and end apart: 8 -> 10, of which waited for: 2 -> 2; matrix products, arithmetic and copies ran while one was open for 5% -> 4% of each run, Pallas kernels for 36% -> 45%
where the time goes in v5:
time: 92.3 us; the launch traced here: 92.5 us
  Pallas kernels  45.4 us (49%)
  waiting for transfers between devices  25.9 us (28%)
  starting transfers between devices  16.1 us (17%)
  local copies, waits for them, and re-layouts  3.97 us (4%)
    pallas_call x4, Pallas kernels, match(): pl.pallas_call(functools.partial(match_kernel, lefts=left_parts, rights=r...  38.5 us
    ppermute x8, waiting for transfers between devices, move(): return lax.ppermute(value, 'cand', pairs)  21.2 us
    ppermute x8, starting transfers between devices, move(): return lax.ppermute(value, 'cand', pairs)  15 us
    pallas_call x2, Pallas kernels, packets_of(): pl.pallas_call(functools.partial(packet_kernel, slot=slot, rows=rows, out...  6.9 us
    ppermute x2, waiting for transfers between devices, back(): return lax.ppermute(value, 'cand', [(b, a) for a, b in pairs])  4.7 us
    unnamed x23, local copies, waits for them, and re-layouts  3.86 us
  transfers between devices with their start and end apart: 10, of which 2 were waited for; matrix products, arithmetic and copies ran while one was open for 4% of the time, Pallas kernels for 45%

profile of v5, /device:TPU:0, one launch (start us, length us, event | category | flops | bytes accessed | tf_op | source)
XLA Modules:
  0.0 92.5 jit_solution(12370783278377479970)
XLA Ops:
  0.0 3.7 %shard_map.82 = (bf16[1,1040,768]{2,1,0:T(8,128)(2,1)}, bf16[1,528,768]{2,1,0:T(8,128)(2,1)}, bf16[1,528,768]{2,1,0:T(8,128)(2,1)}) custom-call(s32[2]{0:T(128)} %lengths.3, bf16[2,1024,768]{2,1,0:T(8,128)(2,1)} %values_ref.3), custom_call_target="tpu_custom_call" | custom-call | flops 1 | bytes 1 | tf_op jit(solution)/shard_map/pallas_call | solution.py:85
  3.7 6.1 %collective-permute-start.4 = (bf16[1,1040,768]{2,1,0:T(8,128)(2,1)}, bf16[1,1040,768]{2,1,0:T(8,128)(2,1)}, u32[]{:S(2)}, u32[]{:S(2)}) collective-permute-start(bf16[1,1040,768]{2,1,0:T(8,128)(2,1)} %get-tuple-element.24.refs_0_), channel_id=1, source_target_pairs={{0,14},{1,3},{2,0},{3,5},{4,2},{5,7},{6,4},{7,9},{8,6},{9,11},{10,... | collective-permute-start | bytes 4792328 | tf_op jit(solution)/shard_map/ppermute | solution.py:363
  9.8 0.0 collective-permute-start.2
  9.8 0.5 collective-permute-start.3
  10.3 3.2 %shard_map.83 = (bf16[1,528,768]{2,1,0:T(8,128)(2,1)}, bf16[1,528,768]{2,1,0:T(8,128)(2,1)}) custom-call(s32[2]{0:T(128)} %lengths.3, bf16[2,1024,768]{2,1,0:T(8,128)(2,1)} %values_ref.3, bf16[1,1040,768]{2,1,0:T(8,128)(2,1)} %get-tuple-element.24.refs_0_), custom_call_target="tpu_custom_call" | custom-call | flops 1 | bytes 1 | tf_op jit(solution)/shard_map/pallas_call | solution.py:85
  13.5 0.0 copy-start.1
  13.5 0.1 collective-permute-start
  13.6 0.5 collective-permute-start.1
  14.1 0.0 copy-start.8
  14.1 0.0 copy-start.9
  14.1 0.0 copy-start
  14.1 0.0 copy-start.2
  14.1 0.0 copy-start.3
  14.1 2.3 %copy.43.refs_0_ = bf16[1,528,768]{2,1,0:T(8,128)(2,1)} copy(bf16[1,528,768]{2,1,0:T(8,128)(2,1)} %get-tuple-element.25.refs_2_.refs_8_.refs_3_) | data formatting | bytes 1622016
  16.3 0.0 copy-done.1
  16.3 1.0 %copy.42.refs_0_ = bf16[1,528,768]{2,1,0:T(8,128)(2,1)} copy(bf16[1,528,768]{2,1,0:T(8,128)(2,1)S(1)} %copy-done.1) | data formatting | bytes 1622016
  17.3 0.0 copy-done.8
  17.3 0.0 copy-done.9
  17.3 0.0 collective-permute-done.2.refs_10_.refs_5_
  17.3 0.0 collective-permute-done.3.refs_11_.refs_6_
  17.3 0.0 collective-permute-done.refs_4_.refs_12_.refs_7_
  17.4 0.0 collective-permute-done.1.refs_5_.refs_13_.refs_8_
  17.4 0.0 copy-done
  17.4 0.0 copy-done.2
  17.4 0.0 copy-done.3
  17.4 11.7 %shard_map.84 = (f32[3,1,1024]{2,1,0:T(1,128)S(1)}, f32[4,1,1024]{2,1,0:T(1,128)S(1)}, f32[4,1,1024]{2,1,0:T(1,128)S(1)}) custom-call(s32[7]{0:T(128)S(1)} %broadcast_select_fusion.2.meta, bf16[1,528,768]{2,1,0:T(8,128)(2,1)S(1)} %copy-done.2, bf16[1,528,768]{2,1,0:T(8,128)(2,1)S(1)} %copy-done.3, bf16[1,528,768]{2,1,0:T(8,128)(2,1)S(1)} %copy-done, ...), custom_call_target="tpu_custom_call" | custom-call | flops 1 | bytes 1 | tf_op jit(solution)/shard_map/pallas_call | solution.py:316
  29.2 0.6 copy.41
  29.8 0.0 copy-start.5
  29.8 0.0 copy-start.6
  29.8 0.0 copy-start.7
  29.8 0.5 collective-permute-start.6
  30.3 21.2 %collective-permute-done.4.refs_0_.refs_1_ = bf16[1,1040,768]{2,1,0:T(8,128)(2,1)} collective-permute-done((bf16[1,1040,768]{2,1,0:T(8,128)(2,1)}, bf16[1,1040,768]{2,1,0:T(8,128)(2,1)}, u32[]{:S(2)}, u32[]{:S(2)}) %collective-permute-start.4) | collective-permute-done | bytes 1597472 | tf_op jit(solution)/shard_map/ppermute | solution.py:363
  51.5 3.3 %collective-permute-start.5 = (bf16[1,528,768]{2,1,0:T(8,128)(2,1)}, bf16[1,528,768]{2,1,0:T(8,128)(2,1)}, u32[]{:S(2)}, u32[]{:S(2)}) collective-permute-start(bf16[1,528,768]{2,1,0:T(8,128)(2,1)} %shard_map.86), channel_id=1, source_target_pairs={{0,15},{1,2},{2,1},{3,4},{4,3},{5,6},{6,5},{7,8},{8,7},{9,10},{10,... | collective-permute-start | bytes 2433032 | tf_op jit(solution)/shard_map/ppermute | solution.py:363
  54.9 0.1 pad.6.clone
  54.9 0.0 copy-done.5
  55.0 0.0 copy-done.6
  55.0 0.0 copy-done.7
  55.0 15.0 %shard_map.85 = (f32[1,1,1024]{2,1,0:T(1,128)S(1)}, f32[4,1,1024]{2,1,0:T(1,128)S(1)}, f32[4,1,1024]{2,1,0:T(1,128)S(1)}) custom-call(s32[9]{0:T(128)S(1)} %get-tuple-element.42.meta, bf16[1,1040,768]{2,1,0:T(8,128)(2,1)} %collective-permute-done.4.refs_0_.refs_1_, bf16[1,528,768]{2,1,0:T(8,128)(2,1)S(1)} %copy-done.2, bf16[1,528,768]{2,1,0:T(8,128)(2,1)S(1)} %copy-done.3, ...), custom_call_target="tpu_custom_call" | custom-call | flops 1 | bytes 1 | tf_op jit(solution)/shard_map/pallas_call | solution.py:316
  70.0 0.1 collective-permute-start.8
  70.1 0.0 collective-permute-done.6.refs_0_
  70.1 5.9 %shard_map.88 = (f32[1,1,512]{2,1,0:T(1,128)S(1)}, f32[4,1,1024]{2,1,0:T(1,128)S(1)}, f32[4,1,1024]{2,1,0:T(1,128)S(1)}) custom-call(s32[9]{0:T(128)S(1)} %get-tuple-element.43.meta, bf16[1,528,768]{2,1,0:T(8,128)(2,1)} %collective-permute-done.6.refs_0_, bf16[1,528,768]{2,1,0:T(8,128)(2,1)S(1)} %copy-done.2, bf16[1,528,768]{2,1,0:T(8,128)(2,1)S(1)} %copy-done.3, ...), custom_call_target="tpu_custom_call" | custom-call | flops 1 | bytes 1 | tf_op jit(solution)/shard_map/pallas_call | solution.py:316
  76.0 0.0 collective-permute-done.5.refs_0_
  76.0 0.0 copy-start.4
  76.0 5.9 %shard_map.89 = (f32[1,1,512]{2,1,0:T(1,128)S(1)}, f32[4,1,1024]{2,1,0:T(1,128)S(1)}, f32[4,1,1024]{2,1,0:T(1,128)S(1)}) custom-call(s32[9]{0:T(128)S(1)} %get-tuple-element.43.meta, bf16[1,528,768]{2,1,0:T(8,128)(2,1)} %collective-permute-done.5.refs_0_, bf16[1,528,768]{2,1,0:T(8,128)(2,1)S(1)} %copy-done.2, bf16[1,528,768]{2,1,0:T(8,128)(2,1)S(1)} %copy-done.3, ...), custom_call_target="tpu_custom_call" | custom-call | flops 1 | bytes 1 | tf_op jit(solution)/shard_map/pallas_call | solution.py:316
  82.0 0.1 fusion.1
  82.1 4.1 %collective-permute-start.7 = (f32[2,1024]{1,0:T(2,128)S(1)}, f32[2,1024]{1,0:T(2,128)S(1)}, u32[]{:S(2)}, u32[]{:S(2)}) collective-permute-start(f32[2,1024]{1,0:T(2,128)S(1)} %slice.33), channel_id=1, source_target_pairs={{0,1},{1,0},{2,3},{3,2},{4,5},{5,4},{6,7},{7,6},{8,9},{9,8},{10,11... | collective-permute-start | bytes 24584 | tf_op jit(solution)/shard_map/ppermute | solution.py:363
  86.1 1.0 %collective-permute-start.9 = (f32[1024]{0:T(1024)S(1)}, f32[1024]{0:T(1024)S(1)}, u32[]{:S(2)}, u32[]{:S(2)}) collective-permute-start(f32[1024]{0:T(1024)S(1)} %pad_maximum_fusion), channel_id=1, source_target_pairs={{15,0},{2,1},{1,2},{4,3},{3,4},{6,5},{5,6},{8,7},{7,8},{10,9},{9,1... | collective-permute-start | bytes 12296 | tf_op jit(solution)/shard_map/ppermute | solution.py:366
  87.2 0.0 collective-permute-done.8
  87.2 4.7 %collective-permute-done.9 = f32[1024]{0:T(1024)S(1)} collective-permute-done((f32[1024]{0:T(1024)S(1)}, f32[1024]{0:T(1024)S(1)}, u32[]{:S(2)}, u32[]{:S(2)}) %collective-permute-start.9) | collective-permute-done | bytes 4128 | tf_op jit(solution)/shard_map/ppermute | solution.py:366
  91.9 0.0 collective-permute-done.7
  91.9 0.0 copy-done.4
  91.9 0.7 compare_select_fusion
  (12 shorter events, 0.1 us)
Async XLA Ops:
  3.7 47.8 %collective-permute-start.4 = (bf16[1,1040,768]{2,1,0:T(8,128)(2,1)}, bf16[1,1040,768]{2,1,0:T(8,128)(2,1)}, u32[]{:S(2)}, u32[]{:S(2)}) collective-permute-start(bf16[1,1040,768]{2,1,0:T(8,128)(2,1)} %get-tuple-element.24.refs_0_), channel_id=1, source_target_pairs={{0,14},{1,3},{2,0},{3,5},{4,2},{5,7},{6,4},{7,9},{8,6},{9,11},{10,... | collective-permute-start | bytes 4792328 | tf_op jit(solution)/shard_map/ppermute | solution.py:363
  9.8 7.6 %collective-permute-start.2 = (bf16[1,528,768]{2,1,0:T(8,128)(2,1)}, bf16[1,528,768]{2,1,0:T(8,128)(2,1)}, u32[]{:S(2)}, u32[]{:S(2)}) collective-permute-start(bf16[1,528,768]{2,1,0:T(8,128)(2,1)} %get-tuple-element.22.refs_0_.refs_6_.refs_1_), channel_id=1, source_target_pairs={{0,1},{1,0},{2,3},{3,2},{4,5},{5,4},{6,7},{7,6},{8,9},{9,8},{10,11... | collective-permute-start | bytes 2433032 | tf_op jit(solution)/shard_map/ppermute | solution.py:363
  9.8 7.6 %collective-permute-start.3 = (bf16[1,528,768]{2,1,0:T(8,128)(2,1)}, bf16[1,528,768]{2,1,0:T(8,128)(2,1)}, u32[]{:S(2)}, u32[]{:S(2)}) collective-permute-start(bf16[1,528,768]{2,1,0:T(8,128)(2,1)} %get-tuple-element.23.refs_1_.refs_7_.refs_2_), channel_id=1, source_target_pairs={{0,1},{1,0},{2,3},{3,2},{4,5},{5,4},{6,7},{7,6},{8,9},{9,8},{10,11... | collective-permute-start | bytes 2433032 | tf_op jit(solution)/shard_map/ppermute | solution.py:363
  13.5 2.9 %copy-start.1 = (bf16[1,528,768]{2,1,0:T(8,128)(2,1)S(1)}, bf16[1,528,768]{2,1,0:T(8,128)(2,1)}, u32[]{:S(2)}) copy-start(bf16[1,528,768]{2,1,0:T(8,128)(2,1)} %get-tuple-element.26.refs_3_.refs_9_.refs_4_) | copy-start | bytes 2433028
  13.5 3.9 %collective-permute-start = (bf16[1,528,768]{2,1,0:T(8,128)(2,1)}, bf16[1,528,768]{2,1,0:T(8,128)(2,1)}, u32[]{:S(2)}, u32[]{:S(2)}) collective-permute-start(bf16[1,528,768]{2,1,0:T(8,128)(2,1)} %get-tuple-element.25.refs_2_.refs_8_.refs_3_), channel_id=1, source_target_pairs={{0,1},{1,0},{2,3},{3,2},{4,5},{5,4},{6,7},{7,6},{8,9},{9,8},{10,11... | collective-permute-start | bytes 2433032 | tf_op jit(solution)/shard_map/ppermute | solution.py:363
  13.6 3.8 %collective-permute-start.1 = (bf16[1,528,768]{2,1,0:T(8,128)(2,1)}, bf16[1,528,768]{2,1,0:T(8,128)(2,1)}, u32[]{:S(2)}, u32[]{:S(2)}) collective-permute-start(bf16[1,528,768]{2,1,0:T(8,128)(2,1)} %get-tuple-element.26.refs_3_.refs_9_.refs_4_), channel_id=1, source_target_pairs={{0,1},{1,0},{2,3},{3,2},{4,5},{5,4},{6,7},{7,6},{8,9},{9,8},{10,11... | collective-permute-start | bytes 2433032 | tf_op jit(solution)/shard_map/ppermute | solution.py:363
  14.1 3.2 %copy-start.8 = (s32[7]{0:T(128)S(1)}, s32[7]{0:T(128)}, u32[]{:S(2)}) copy-start(s32[7]{0:T(128)} %constant.44.clone) | copy-start | bytes 88
  14.1 3.2 %copy-start.9 = (s32[7]{0:T(128)S(1)}, s32[7]{0:T(128)}, u32[]{:S(2)}) copy-start(s32[7]{0:T(128)} %constant.43.clone) | copy-start | bytes 88
  14.1 3.3 %copy-start = (bf16[1,528,768]{2,1,0:T(8,128)(2,1)S(1)}, bf16[1,528,768]{2,1,0:T(8,128)(2,1)}, u32[]{:S(2)}) copy-start(bf16[1,528,768]{2,1,0:T(8,128)(2,1)} %get-tuple-element.25.refs_2_.refs_8_.refs_3_) | copy-start | bytes 2433028
  14.1 3.3 %copy-start.2 = (bf16[1,528,768]{2,1,0:T(8,128)(2,1)S(1)}, bf16[1,528,768]{2,1,0:T(8,128)(2,1)}, u32[]{:S(2)}) copy-start(bf16[1,528,768]{2,1,0:T(8,128)(2,1)} %get-tuple-element.22.refs_0_.refs_6_.refs_1_) | copy-start | bytes 2433028
  14.1 3.4 %copy-start.3 = (bf16[1,528,768]{2,1,0:T(8,128)(2,1)S(1)}, bf16[1,528,768]{2,1,0:T(8,128)(2,1)}, u32[]{:S(2)}) copy-start(bf16[1,528,768]{2,1,0:T(8,128)(2,1)} %get-tuple-element.23.refs_1_.refs_7_.refs_2_) | copy-start | bytes 2433028
  29.8 25.2 %copy-start.5 = (s32[9]{0:T(128)S(1)}, s32[9]{0:T(128)}, u32[]{:S(2)}) copy-start(s32[9]{0:T(128)} %constant.47.clone) | copy-start | bytes 112
  29.8 25.2 %copy-start.6 = (s32[9]{0:T(128)S(1)}, s32[9]{0:T(128)}, u32[]{:S(2)}) copy-start(s32[9]{0:T(128)} %constant.46.clone) | copy-start | bytes 112
  29.8 25.2 %copy-start.7 = (s32[9]{0:T(128)S(1)}, s32[9]{0:T(128)}, u32[]{:S(2)}) copy-start(s32[9]{0:T(128)} %constant.45.clone) | copy-start | bytes 112
  29.8 40.3 %collective-permute-start.6 = (bf16[1,528,768]{2,1,0:T(8,128)(2,1)}, bf16[1,528,768]{2,1,0:T(8,128)(2,1)}, u32[]{:S(2)}, u32[]{:S(2)}) collective-permute-start(bf16[1,528,768]{2,1,0:T(8,128)(2,1)} %shard_map.87), channel_id=1, source_target_pairs={{0,15},{1,2},{2,1},{3,4},{4,3},{5,6},{6,5},{7,8},{8,7},{9,10},{10,... | collective-permute-start | bytes 2433032 | tf_op jit(solution)/shard_map/ppermute | solution.py:363
  51.5 24.5 %collective-permute-start.5 = (bf16[1,528,768]{2,1,0:T(8,128)(2,1)}, bf16[1,528,768]{2,1,0:T(8,128)(2,1)}, u32[]{:S(2)}, u32[]{:S(2)}) collective-permute-start(bf16[1,528,768]{2,1,0:T(8,128)(2,1)} %shard_map.86), channel_id=1, source_target_pairs={{0,15},{1,2},{2,1},{3,4},{4,3},{5,6},{6,5},{7,8},{8,7},{9,10},{10,... | collective-permute-start | bytes 2433032 | tf_op jit(solution)/shard_map/ppermute | solution.py:363
  70.0 17.2 %collective-permute-start.8 = (f32[1024]{0:T(1024)S(1)}, f32[1024]{0:T(1024)S(1)}, u32[]{:S(2)}, u32[]{:S(2)}) collective-permute-start(f32[1024]{0:T(1024)S(1)} %bitcast.29), channel_id=1, source_target_pairs={{14,0},{3,1},{0,2},{5,3},{2,4},{7,5},{4,6},{9,7},{6,8},{11,9},{8,1... | collective-permute-start | bytes 12296 | tf_op jit(solution)/shard_map/ppermute | solution.py:366
  76.0 15.9 %copy-start.4 = (s32[2]{0:T(128)S(1)}, s32[2]{0:T(128)}, u32[]{:S(2)}) copy-start(s32[2]{0:T(128)} %lengths.3) | copy-start | bytes 28
  82.1 9.8 %collective-permute-start.7 = (f32[2,1024]{1,0:T(2,128)S(1)}, f32[2,1024]{1,0:T(2,128)S(1)}, u32[]{:S(2)}, u32[]{:S(2)}) collective-permute-start(f32[2,1024]{1,0:T(2,128)S(1)} %slice.33), channel_id=1, source_target_pairs={{0,1},{1,0},{2,3},{3,2},{4,5},{5,4},{6,7},{7,6},{8,9},{9,8},{10,11... | collective-permute-start | bytes 24584 | tf_op jit(solution)/shard_map/ppermute | solution.py:363
  86.1 5.7 %collective-permute-start.9 = (f32[1024]{0:T(1024)S(1)}, f32[1024]{0:T(1024)S(1)}, u32[]{:S(2)}, u32[]{:S(2)}) collective-permute-start(f32[1024]{0:T(1024)S(1)} %pad_maximum_fusion), channel_id=1, source_target_pairs={{15,0},{2,1},{1,2},{4,3},{3,4},{6,5},{5,6},{8,7},{7,8},{10,9},{9,1... | collective-permute-start | bytes 12296 | tf_op jit(solution)/shard_map/ppermute | solution.py:366

commit v6 on v5

--- a/solution.py
+++ b/solution.py
@@ -382,7 +382,7 @@
     inner_rows, inner_cols = match(inner_meta, [own_first, own_second, mate_second], near)
 
     lower = move(after(own_second[0], inner_rows), second_to)
-    upper = move(after(own_second[1], first), second_to)
+    upper = move(after(own_second[1], first, lower), second_to)
     first_meta = by_role([4, 0, 0, 0, 0, 0, 1, 2, 3], [2, 0, 0, 0, 0, 0, 1, 1, 1])
     first_rows, first_cols = match(first_meta, [[first]], near)
     first_back = back(first_rows[0], first_to)

time: 92.3 us -> 108 us (1.17)
  starting transfers between devices: 16.1 us -> 44.7 us
  Pallas kernels: 45.4 us -> 35.8 us
  waiting for transfers between devices: 25.9 us -> 23.6 us
    ppermute x2, starting transfers between devices: 1.09 us -> 28.5 us  [back(): return lax.ppermute(value, 'cand', [(b, a) for a, b in pairs])]
    pallas_call x4, Pallas kernels: 38.5 us -> 28.7 us  [match(): pl.pallas_call(functools.partial(match_kernel, lefts=left_parts, rights=r...]
    ppermute x2, waiting for transfers between devices: 4.7 us -> 1.33 us  [back(): return lax.ppermute(value, 'cand', [(b, a) for a, b in pairs])]
    ppermute x8, starting transfers between devices: 15 us -> 16.2 us  [move(): return lax.ppermute(value, 'cand', pairs)]
  transfers between devices with their start and end apart: 10 -> 10, of which waited for: 2 -> 2; matrix products, arithmetic and copies ran while one was open for 4% -> 4% of each run, Pallas kernels for 45% -> 26%
where the time goes in v6:
time: 108 us; the launch traced here: 109 us
  starting transfers between devices  44.7 us (41%)
  Pallas kernels  35.8 us (33%)
  waiting for transfers between devices  23.6 us (22%)
  local copies, waits for them, and re-layouts  3.86 us (4%)
    pallas_call x4, Pallas kernels, match(): pl.pallas_call(functools.partial(match_kernel, lefts=left_parts, rights=r...  28.7 us
    ppermute x2, starting transfers between devices, back(): return lax.ppermute(value, 'cand', [(b, a) for a, b in pairs])  28.5 us
    ppermute x8, waiting for transfers between devices, move(): return lax.ppermute(value, 'cand', pairs)  22.3 us
    ppermute x8, starting transfers between devices, move(): return lax.ppermute(value, 'cand', pairs)  16.2 us
    pallas_call x2, Pallas kernels, packets_of(): pl.pallas_call(functools.partial(packet_kernel, slot=slot, rows=rows, out...  7.04 us
    unnamed x23, local copies, waits for them, and re-layouts  3.75 us
  transfers between devices with their start and end apart: 10, of which 2 were waited for; matrix products, arithmetic and copies ran while one was open for 4% of the time, Pallas kernels for 26%

profile of v6, /device:TPU:0, one launch (start us, length us, event | category | flops | bytes accessed | tf_op | source)
XLA Modules:
  0.0 109.0 jit_solution(8211358883644756412)
XLA Ops:
  0.0 3.6 %shard_map.82 = (bf16[1,1040,768]{2,1,0:T(8,128)(2,1)}, bf16[1,528,768]{2,1,0:T(8,128)(2,1)}, bf16[1,528,768]{2,1,0:T(8,128)(2,1)}) custom-call(s32[2]{0:T(128)} %lengths.3, bf16[2,1024,768]{2,1,0:T(8,128)(2,1)} %values_ref.3), custom_call_target="tpu_custom_call" | custom-call | flops 1 | bytes 1 | tf_op jit(solution)/shard_map/pallas_call | solution.py:85
  3.7 0.0 copy-start.2
  3.7 0.0 copy-start.3
  3.7 3.4 %shard_map.83 = (bf16[1,528,768]{2,1,0:T(8,128)(2,1)}, bf16[1,528,768]{2,1,0:T(8,128)(2,1)}) custom-call(s32[2]{0:T(128)} %lengths.3, bf16[2,1024,768]{2,1,0:T(8,128)(2,1)} %values_ref.3, bf16[1,1040,768]{2,1,0:T(8,128)(2,1)} %get-tuple-element.24.refs_0_), custom_call_target="tpu_custom_call" | custom-call | flops 1 | bytes 1 | tf_op jit(solution)/shard_map/pallas_call | solution.py:85
  7.1 0.0 copy-start.8
  7.1 0.0 copy-start.9
  7.1 0.0 copy-start
  7.1 0.0 copy-start.1
  7.1 0.5 collective-permute-start
  7.6 0.1 collective-permute-start.1
  7.7 0.0 copy-done.2
  7.7 0.4 collective-permute-start.2
  8.2 0.0 copy-done.3
  8.2 0.1 collective-permute-start.3
  8.2 6.0 %collective-permute-start.4 = (bf16[1,1040,768]{2,1,0:T(8,128)(2,1)}, bf16[1,1040,768]{2,1,0:T(8,128)(2,1)}, u32[]{:S(2)}, u32[]{:S(2)}) collective-permute-start(bf16[1,1040,768]{2,1,0:T(8,128)(2,1)} %get-tuple-element.24.refs_0_), channel_id=1, source_target_pairs={{0,14},{1,3},{2,0},{3,5},{4,2},{5,7},{6,4},{7,9},{8,6},{9,11},{10,... | collective-permute-start | bytes 4792328 | tf_op jit(solution)/shard_map/ppermute | solution.py:363
  14.2 2.2 %copy.42.refs_0_ = bf16[1,528,768]{2,1,0:T(8,128)(2,1)} copy(bf16[1,528,768]{2,1,0:T(8,128)(2,1)} %get-tuple-element.25.refs_2_.refs_8_.refs_3_) | data formatting | bytes 1622016
  16.4 0.0 copy-done.8
  16.4 0.0 copy-done.9
  16.4 0.0 collective-permute-done.refs_4_.refs_12_.refs_7_
  16.4 0.0 collective-permute-done.1.refs_5_.refs_13_.refs_8_
  16.4 0.0 collective-permute-done.2.refs_10_.refs_5_
  16.4 0.0 collective-permute-done.3.refs_11_.refs_6_
  16.5 0.0 copy-done
  16.5 0.0 copy-done.1
  16.5 10.3 %shard_map.84 = (f32[3,1,1024]{2,1,0:T(1,128)S(1)}, f32[4,1,1024]{2,1,0:T(1,128)S(1)}, f32[4,1,1024]{2,1,0:T(1,128)S(1)}) custom-call(s32[7]{0:T(128)S(1)} %broadcast_select_fusion.2.meta, bf16[1,528,768]{2,1,0:T(8,128)(2,1)S(1)} %copy-done.2, bf16[1,528,768]{2,1,0:T(8,128)(2,1)S(1)} %copy-done.3, bf16[1,528,768]{2,1,0:T(8,128)(2,1)S(1)} %copy-done, ...), custom_call_target="tpu_custom_call" | custom-call | flops 1 | bytes 1 | tf_op jit(solution)/shard_map/pallas_call | solution.py:316
  26.8 0.6 copy.41
  27.4 5.4 %collective-permute-start.5 = (bf16[1,528,768]{2,1,0:T(8,128)(2,1)}, bf16[1,528,768]{2,1,0:T(8,128)(2,1)}, u32[]{:S(2)}, u32[]{:S(2)}) collective-permute-start(bf16[1,528,768]{2,1,0:T(8,128)(2,1)} %shard_map.86), channel_id=1, source_target_pairs={{0,15},{1,2},{2,1},{3,4},{4,3},{5,6},{6,5},{7,8},{8,7},{9,10},{10,... | collective-permute-start | bytes 2433032 | tf_op jit(solution)/shard_map/ppermute | solution.py:363
  32.8 0.9 copy.43.refs_0_
  33.7 0.0 copy-start.5
  33.7 0.0 copy-start.6
  33.7 0.0 copy-start.7
  33.7 22.2 %collective-permute-done.4.refs_0_.refs_1_ = bf16[1,1040,768]{2,1,0:T(8,128)(2,1)} collective-permute-done((bf16[1,1040,768]{2,1,0:T(8,128)(2,1)}, bf16[1,1040,768]{2,1,0:T(8,128)(2,1)}, u32[]{:S(2)}, u32[]{:S(2)}) %collective-permute-start.4) | collective-permute-done | bytes 1597472 | tf_op jit(solution)/shard_map/ppermute | solution.py:363
  56.0 0.0 collective-permute-done.5.refs_2_.refs_0_
  56.0 3.6 %collective-permute-start.6 = (bf16[1,528,768]{2,1,0:T(8,128)(2,1)}, bf16[1,528,768]{2,1,0:T(8,128)(2,1)}, u32[]{:S(2)}, u32[]{:S(2)}) collective-permute-start(bf16[1,528,768]{2,1,0:T(8,128)(2,1)} %shard_map.87), channel_id=1, source_target_pairs={{0,15},{1,2},{2,1},{3,4},{4,3},{5,6},{6,5},{7,8},{8,7},{9,10},{10,... | collective-permute-start | bytes 2433032 | tf_op jit(solution)/shard_map/ppermute | solution.py:363
  59.6 0.1 pad.6.clone
  59.6 0.0 copy-done.5
  59.7 0.0 copy-done.6
  59.7 0.0 copy-done.7
  59.7 8.2 %shard_map.85 = (f32[1,1,1024]{2,1,0:T(1,128)S(1)}, f32[4,1,1024]{2,1,0:T(1,128)S(1)}, f32[4,1,1024]{2,1,0:T(1,128)S(1)}) custom-call(s32[9]{0:T(128)S(1)} %get-tuple-element.42.meta, bf16[1,1040,768]{2,1,0:T(8,128)(2,1)} %collective-permute-done.4.refs_0_.refs_1_, bf16[1,528,768]{2,1,0:T(8,128)(2,1)S(1)} %copy-done.2, bf16[1,528,768]{2,1,0:T(8,128)(2,1)S(1)} %copy-done.3, ...), custom_call_target="tpu_custom_call" | custom-call | flops 1 | bytes 1 | tf_op jit(solution)/shard_map/pallas_call | solution.py:316
  67.9 21.3 %collective-permute-start.8 = (f32[1024]{0:T(1024)S(1)}, f32[1024]{0:T(1024)S(1)}, u32[]{:S(2)}, u32[]{:S(2)}) collective-permute-start(f32[1024]{0:T(1024)S(1)} %bitcast.29), channel_id=1, source_target_pairs={{14,0},{3,1},{0,2},{5,3},{2,4},{7,5},{4,6},{9,7},{6,8},{11,9},{8,1... | collective-permute-start | bytes 12296 | tf_op jit(solution)/shard_map/ppermute | solution.py:366
  89.2 5.1 %shard_map.88 = (f32[1,1,512]{2,1,0:T(1,128)S(1)}, f32[4,1,1024]{2,1,0:T(1,128)S(1)}, f32[4,1,1024]{2,1,0:T(1,128)S(1)}) custom-call(s32[9]{0:T(128)S(1)} %get-tuple-element.43.meta, bf16[1,528,768]{2,1,0:T(8,128)(2,1)} %collective-permute-done.5.refs_2_.refs_0_, bf16[1,528,768]{2,1,0:T(8,128)(2,1)S(1)} %copy-done.2, bf16[1,528,768]{2,1,0:T(8,128)(2,1)S(1)} %copy-done.3, ...), custom_call_target="tpu_custom_call" | custom-call | flops 1 | bytes 1 | tf_op jit(solution)/shard_map/pallas_call | solution.py:316
  94.4 0.0 collective-permute-done.6.refs_0_
  94.4 0.0 copy-start.4
  94.4 5.1 %shard_map.89 = (f32[1,1,512]{2,1,0:T(1,128)S(1)}, f32[4,1,1024]{2,1,0:T(1,128)S(1)}, f32[4,1,1024]{2,1,0:T(1,128)S(1)}) custom-call(s32[9]{0:T(128)S(1)} %get-tuple-element.43.meta, bf16[1,528,768]{2,1,0:T(8,128)(2,1)} %collective-permute-done.6.refs_0_, bf16[1,528,768]{2,1,0:T(8,128)(2,1)S(1)} %copy-done.2, bf16[1,528,768]{2,1,0:T(8,128)(2,1)S(1)} %copy-done.3, ...), custom_call_target="tpu_custom_call" | custom-call | flops 1 | bytes 1 | tf_op jit(solution)/shard_map/pallas_call | solution.py:316
  99.6 0.1 fusion.1
  99.7 0.1 collective-permute-start.7
  99.8 7.2 %collective-permute-start.9 = (f32[1024]{0:T(1024)S(1)}, f32[1024]{0:T(1024)S(1)}, u32[]{:S(2)}, u32[]{:S(2)}) collective-permute-start(f32[1024]{0:T(1024)S(1)} %pad_maximum_fusion), channel_id=1, source_target_pairs={{15,0},{2,1},{1,2},{4,3},{3,4},{6,5},{5,6},{8,7},{7,8},{10,9},{9,1... | collective-permute-start | bytes 12296 | tf_op jit(solution)/shard_map/ppermute | solution.py:366
  107.0 0.0 collective-permute-done.8
  107.0 1.3 %collective-permute-done.9 = f32[1024]{0:T(1024)S(1)} collective-permute-done((f32[1024]{0:T(1024)S(1)}, f32[1024]{0:T(1024)S(1)}, u32[]{:S(2)}, u32[]{:S(2)}) %collective-permute-start.9) | collective-permute-done | bytes 4128 | tf_op jit(solution)/shard_map/ppermute | solution.py:366
  108.3 0.0 collective-permute-done.7
  108.3 0.0 copy-done.4
  108.3 0.7 compare_select_fusion
  (12 shorter events, 0.1 us)
Async XLA Ops:
  3.7 4.1 %copy-start.2 = (bf16[1,528,768]{2,1,0:T(8,128)(2,1)S(1)}, bf16[1,528,768]{2,1,0:T(8,128)(2,1)}, u32[]{:S(2)}) copy-start(bf16[1,528,768]{2,1,0:T(8,128)(2,1)} %get-tuple-element.22.refs_0_.refs_6_.refs_1_) | copy-start | bytes 2433028
  3.7 4.5 %copy-start.3 = (bf16[1,528,768]{2,1,0:T(8,128)(2,1)S(1)}, bf16[1,528,768]{2,1,0:T(8,128)(2,1)}, u32[]{:S(2)}) copy-start(bf16[1,528,768]{2,1,0:T(8,128)(2,1)} %get-tuple-element.23.refs_1_.refs_7_.refs_2_) | copy-start | bytes 2433028
  7.1 9.3 %copy-start.8 = (s32[7]{0:T(128)S(1)}, s32[7]{0:T(128)}, u32[]{:S(2)}) copy-start(s32[7]{0:T(128)} %constant.43.clone) | copy-start | bytes 88
  7.1 9.3 %copy-start.9 = (s32[7]{0:T(128)S(1)}, s32[7]{0:T(128)}, u32[]{:S(2)}) copy-start(s32[7]{0:T(128)} %constant.44.clone) | copy-start | bytes 88
  7.1 9.4 %copy-start = (bf16[1,528,768]{2,1,0:T(8,128)(2,1)S(1)}, bf16[1,528,768]{2,1,0:T(8,128)(2,1)}, u32[]{:S(2)}) copy-start(bf16[1,528,768]{2,1,0:T(8,128)(2,1)} %get-tuple-element.25.refs_2_.refs_8_.refs_3_) | copy-start | bytes 2433028
  7.1 9.4 %copy-start.1 = (bf16[1,528,768]{2,1,0:T(8,128)(2,1)S(1)}, bf16[1,528,768]{2,1,0:T(8,128)(2,1)}, u32[]{:S(2)}) copy-start(bf16[1,528,768]{2,1,0:T(8,128)(2,1)} %get-tuple-element.26.refs_3_.refs_9_.refs_4_) | copy-start | bytes 2433028
  7.1 9.3 %collective-permute-start = (bf16[1,528,768]{2,1,0:T(8,128)(2,1)}, bf16[1,528,768]{2,1,0:T(8,128)(2,1)}, u32[]{:S(2)}, u32[]{:S(2)}) collective-permute-start(bf16[1,528,768]{2,1,0:T(8,128)(2,1)} %get-tuple-element.25.refs_2_.refs_8_.refs_3_), channel_id=1, source_target_pairs={{0,1},{1,0},{2,3},{3,2},{4,5},{5,4},{6,7},{7,6},{8,9},{9,8},{10,11... | collective-permute-start | bytes 2433032 | tf_op jit(solution)/shard_map/ppermute | solution.py:363
  7.6 8.8 %collective-permute-start.1 = (bf16[1,528,768]{2,1,0:T(8,128)(2,1)}, bf16[1,528,768]{2,1,0:T(8,128)(2,1)}, u32[]{:S(2)}, u32[]{:S(2)}) collective-permute-start(bf16[1,528,768]{2,1,0:T(8,128)(2,1)} %get-tuple-element.26.refs_3_.refs_9_.refs_4_), channel_id=1, source_target_pairs={{0,1},{1,0},{2,3},{3,2},{4,5},{5,4},{6,7},{7,6},{8,9},{9,8},{10,11... | collective-permute-start | bytes 2433032 | tf_op jit(solution)/shard_map/ppermute | solution.py:363
  7.7 8.7 %collective-permute-start.2 = (bf16[1,528,768]{2,1,0:T(8,128)(2,1)S(1)}, bf16[1,528,768]{2,1,0:T(8,128)(2,1)}, u32[]{:S(2)}, u32[]{:S(2)}) collective-permute-start(bf16[1,528,768]{2,1,0:T(8,128)(2,1)S(1)} %copy-done.2), channel_id=1, source_target_pairs={{0,1},{1,0},{2,3},{3,2},{4,5},{5,4},{6,7},{7,6},{8,9},{9,8},{10,11... | collective-permute-start | bytes 2433032 | tf_op jit(solution)/shard_map/ppermute | solution.py:363
  8.2 8.3 %collective-permute-start.3 = (bf16[1,528,768]{2,1,0:T(8,128)(2,1)S(1)}, bf16[1,528,768]{2,1,0:T(8,128)(2,1)}, u32[]{:S(2)}, u32[]{:S(2)}) collective-permute-start(bf16[1,528,768]{2,1,0:T(8,128)(2,1)S(1)} %copy-done.3), channel_id=1, source_target_pairs={{0,1},{1,0},{2,3},{3,2},{4,5},{5,4},{6,7},{7,6},{8,9},{9,8},{10,11... | collective-permute-start | bytes 2433032 | tf_op jit(solution)/shard_map/ppermute | solution.py:363
  8.2 47.7 %collective-permute-start.4 = (bf16[1,1040,768]{2,1,0:T(8,128)(2,1)}, bf16[1,1040,768]{2,1,0:T(8,128)(2,1)}, u32[]{:S(2)}, u32[]{:S(2)}) collective-permute-start(bf16[1,1040,768]{2,1,0:T(8,128)(2,1)} %get-tuple-element.24.refs_0_), channel_id=1, source_target_pairs={{0,14},{1,3},{2,0},{3,5},{4,2},{5,7},{6,4},{7,9},{8,6},{9,11},{10,... | collective-permute-start | bytes 4792328 | tf_op jit(solution)/shard_map/ppermute | solution.py:363
  27.4 28.6 %collective-permute-start.5 = (bf16[1,528,768]{2,1,0:T(8,128)(2,1)}, bf16[1,528,768]{2,1,0:T(8,128)(2,1)}, u32[]{:S(2)}, u32[]{:S(2)}) collective-permute-start(bf16[1,528,768]{2,1,0:T(8,128)(2,1)} %shard_map.86), channel_id=1, source_target_pairs={{0,15},{1,2},{2,1},{3,4},{4,3},{5,6},{6,5},{7,8},{8,7},{9,10},{10,... | collective-permute-start | bytes 2433032 | tf_op jit(solution)/shard_map/ppermute | solution.py:363
  33.7 25.9 %copy-start.5 = (s32[9]{0:T(128)S(1)}, s32[9]{0:T(128)}, u32[]{:S(2)}) copy-start(s32[9]{0:T(128)} %constant.45.clone) | copy-start | bytes 112
  33.7 25.9 %copy-start.6 = (s32[9]{0:T(128)S(1)}, s32[9]{0:T(128)}, u32[]{:S(2)}) copy-start(s32[9]{0:T(128)} %constant.46.clone) | copy-start | bytes 112
  33.7 25.9 %copy-start.7 = (s32[9]{0:T(128)S(1)}, s32[9]{0:T(128)}, u32[]{:S(2)}) copy-start(s32[9]{0:T(128)} %constant.47.clone) | copy-start | bytes 112
  56.0 38.4 %collective-permute-start.6 = (bf16[1,528,768]{2,1,0:T(8,128)(2,1)}, bf16[1,528,768]{2,1,0:T(8,128)(2,1)}, u32[]{:S(2)}, u32[]{:S(2)}) collective-permute-start(bf16[1,528,768]{2,1,0:T(8,128)(2,1)} %shard_map.87), channel_id=1, source_target_pairs={{0,15},{1,2},{2,1},{3,4},{4,3},{5,6},{6,5},{7,8},{8,7},{9,10},{10,... | collective-permute-start | bytes 2433032 | tf_op jit(solution)/shard_map/ppermute | solution.py:363
  67.9 39.1 %collective-permute-start.8 = (f32[1024]{0:T(1024)S(1)}, f32[1024]{0:T(1024)S(1)}, u32[]{:S(2)}, u32[]{:S(2)}) collective-permute-start(f32[1024]{0:T(1024)S(1)} %bitcast.29), channel_id=1, source_target_pairs={{14,0},{3,1},{0,2},{5,3},{2,4},{7,5},{4,6},{9,7},{6,8},{11,9},{8,1... | collective-permute-start | bytes 12296 | tf_op jit(solution)/shard_map/ppermute | solution.py:366
  94.4 13.9 %copy-start.4 = (s32[2]{0:T(128)S(1)}, s32[2]{0:T(128)}, u32[]{:S(2)}) copy-start(s32[2]{0:T(128)} %lengths.3) | copy-start | bytes 28
  99.7 8.6 %collective-permute-start.7 = (f32[2,1024]{1,0:T(2,128)S(1)}, f32[2,1024]{1,0:T(2,128)S(1)}, u32[]{:S(2)}, u32[]{:S(2)}) collective-permute-start(f32[2,1024]{1,0:T(2,128)S(1)} %slice.33), channel_id=1, source_target_pairs={{0,1},{1,0},{2,3},{3,2},{4,5},{5,4},{6,7},{7,6},{8,9},{9,8},{10,11... | collective-permute-start | bytes 24584 | tf_op jit(solution)/shard_map/ppermute | solution.py:363
  99.8 8.5 %collective-permute-start.9 = (f32[1024]{0:T(1024)S(1)}, f32[1024]{0:T(1024)S(1)}, u32[]{:S(2)}, u32[]{:S(2)}) collective-permute-start(f32[1024]{0:T(1024)S(1)} %pad_maximum_fusion), channel_id=1, source_target_pairs={{15,0},{2,1},{1,2},{4,3},{3,4},{6,5},{5,6},{8,7},{7,8},{10,9},{9,1... | collective-permute-start | bytes 12296 | tf_op jit(solution)/shard_map/ppermute | solution.py:366
